TPU v7x, 32 devices: a whole 2x2x4 slice. The times are simulated.
32 devices in a mesh: group: 2 (over y), col: 8 (over z, x), batch: 2 (over core).
Axes of the slice: x: 2, y: 2, z: 4, core: 2. Of those that a mesh axis runs over, the one named last changes fastest.
Arguments:
- base_input: bfloat16 [1024, 131072], P(('group', 'batch'), 'col'), parts along dimension 0, may hold values from -6 to 6
- cotangent: bfloat16 [1024, 131072], P(('group', 'batch'), 'col'), parts along dimension 0, may hold values from -1.5 to 1.5
- u_factor: bfloat16 [131072, 1024], P(('col', 'batch')), may hold values from -0.1875 to 0.1875
- v_factor: bfloat16 [131072, 1024], P(('col', 'batch')), may hold values from -0.015625 to 0.015625
- bias: bfloat16 [131072], P('col'), may hold values from -4 to 4
Outputs:
- grad_input: bfloat16 [1024, 131072], P(('group', 'batch'), 'col'), parts along dimension 0
- grad_u: bfloat16 [262144, 1024], P(('group', 'col', 'batch')), parts along dimension 0
- grad_v: bfloat16 [262144, 1024], P(('group', 'col', 'batch')), parts along dimension 0
- grad_bias: float32 [262144], P(('group', 'col', 'batch')), parts along dimension 0
There are 2 independent parts, one for each index of `group`. A program takes and returns all parts, laid end to end along the dimension named above; an argument that names none is the same for every part. Nothing has to cross between parts.
All inputs are finite; a program needn't handle non-finite values.
Results may differ from a plain program's by a relative error of at most 0.0058.
Values may be sent and summed in bfloat16 or wider, within the bound.
No kernel may reach another device: no remote copies, remote signals or barrier semaphores. Data moves between devices by JAX's collectives and lax.ppermute only.
A program may use at most 640 MiB of HBM per device.

v0:
```python
import jax
import jax.numpy as jnp
from jax import lax
from jax.sharding import PartitionSpec as P


def cross_back(inputs, cot_in, u_rows, v_rows, bias_f, reduce_first, reduce_second):
    projected = reduce_first(jnp.dot(inputs, v_rows, preferred_element_type=jnp.float32))
    proj_bf = projected.astype(jnp.bfloat16)
    expanded = jnp.dot(proj_bf, u_rows.T, preferred_element_type=jnp.float32)
    cot_f = cot_in.astype(jnp.float32)
    grad_hidden = (cot_f * inputs.astype(jnp.float32)).astype(jnp.bfloat16)
    grad_proj = reduce_second(jnp.dot(grad_hidden, u_rows, preferred_element_type=jnp.float32))
    gproj_bf = grad_proj.astype(jnp.bfloat16)
    back = jnp.dot(gproj_bf, v_rows.T, preferred_element_type=jnp.float32)
    grad_input = (cot_f * (expanded + bias_f[None, :]) + cot_f + back).astype(jnp.bfloat16)
    u_term = jnp.dot(grad_hidden.T, proj_bf, preferred_element_type=jnp.float32)
    v_term = jnp.dot(inputs.T, gproj_bf, preferred_element_type=jnp.float32)
    bias_term = jnp.sum(grad_hidden.astype(jnp.float32), axis=0)
    return (grad_input, u_term, v_term, bias_term)


def local(base_input, cotangent, u_factor, v_factor, bias):
    inputs_all, cot_all = (
        lax.all_to_all(base_input, "batch", split_axis=1, concat_axis=0, tiled=True),
        lax.all_to_all(cotangent, "batch", split_axis=1, concat_axis=0, tiled=True),
    )
    half = u_factor.shape[0]
    bias_half = lax.dynamic_slice_in_dim(bias, lax.axis_index("batch") * half, half, 0)

    def first_sum(part_sum):
        return lax.psum(part_sum, ("col", "batch"))

    def second_sum(part_sum):
        return lax.psum(part_sum, ("col", "batch"))

    grad_half, u_term, v_term, bias_term = cross_back(
        inputs_all,
        cot_all,
        u_factor,
        v_factor,
        bias_half.astype(jnp.float32),
        first_sum,
        second_sum,
    )
    grad_input = lax.all_to_all(grad_half, "batch", split_axis=0, concat_axis=1, tiled=True)
    return (grad_input, u_term.astype(jnp.bfloat16), v_term.astype(jnp.bfloat16), bias_term)


def solution(mesh):
    return jax.shard_map(
        local,
        mesh=mesh,
        in_specs=(
            P(("group", "batch"), "col"),
            P(("group", "batch"), "col"),
            P(("col", "batch"), None),
            P(("col", "batch"), None),
            P("col"),
        ),
        out_specs=(
            P(("group", "batch"), "col"),
            P(("group", "col", "batch"), None),
            P(("group", "col", "batch"), None),
            P(("group", "col", "batch")),
        ),
        check_vma=False,
    )
```

profile of v0, /device:TPU:0, one launch (start us, length us, event | category | flops | bytes accessed | tf_op | source)
XLA Modules:
  0.0 281.8 jit_solution(17127563410886056216)
XLA Ops:
  0.6 7.8 %copy.18 = bf16[32,2,8,8192]{3,2,0,1:T(8,128)(2,1)} copy(bf16[32,2,8,8192]{3,2,1,0:T(8,128)(2,1)} %bitcast.47) | data formatting | bytes 16777216 | tf_op jit(solution)/shard_map/all_to_all | solution.py:25
  8.4 6.9 %all-to-all-start.1 = ((bf16[256,2,8192]{2,0,1:T(8,128)(2,1)}), bf16[256,2,8192]{2,0,1:T(8,128)(2,1)}, u32[]{:S(2)}, u32[]{:S(2)}) async-start(bf16[256,2,8192]{2,0,1:T(8,128)(2,1)} %bitcast.45), calls=%async_computation.1 | async-start | bytes 16777216 | tf_op jit(solution)/shard_map/all_to_all | solution.py:25
  15.4 7.8 %copy.19 = bf16[32,2,8,8192]{3,2,0,1:T(8,128)(2,1)} copy(bf16[32,2,8,8192]{3,2,1,0:T(8,128)(2,1)} %bitcast.48) | data formatting | bytes 16777216 | tf_op jit(solution)/shard_map/all_to_all | solution.py:26
  23.1 0.0 all-to-all-done.1
  23.1 6.9 %all-to-all-start = ((bf16[256,2,8192]{2,0,1:T(8,128)(2,1)}), bf16[256,2,8192]{2,0,1:T(8,128)(2,1)}, u32[]{:S(2)}, u32[]{:S(2)}) async-start(bf16[256,2,8192]{2,0,1:T(8,128)(2,1)} %bitcast.46), calls=%async_computation | async-start | bytes 16777216 | tf_op jit(solution)/shard_map/all_to_all | solution.py:26
  30.1 14.3 %fusion.10 = f32[512,1024]{1,0:T(8,128)S(1)} fusion(bf16[512,8192]{1,0:T(8,128)(2,1)} %bitcast.3, bf16[8192,1024]{1,0:T(8,128)(2,1)} %param.8), kind=kOutput, calls=%fused_computation.19 | convolution fusion | flops 8589934592 | bytes 27262976 | tf_op jit(solution)/shard_map/dot_general | solution.py:8
  44.4 0.0 all-to-all-done
  44.4 6.9 %fusion.4 = bf16[512,8192]{1,0:T(8,128)(2,1)S(1)} fusion(bf16[256,2,8192]{2,0,1:T(8,128)(2,1)} %all-to-all-done, bf16[256,2,8192]{2,0,1:T(8,128)(2,1)} %all-to-all-done.1), kind=kLoop, calls=%fused_computation.7 | loop fusion | flops 16777216 | bytes 25165824 | tf_op jit(solution)/shard_map/convert_element_type | solution.py:12
  51.3 0.0 copy-start
  51.3 3.2 %copy-done = bf16[512,8192]{1,0:T(8,128)(2,1)} copy-done((bf16[512,8192]{1,0:T(8,128)(2,1)}, bf16[512,8192]{1,0:T(8,128)(2,1)S(1)}, u32[]{:S(2)}) %copy-start) | copy-done | bytes 8388632
  54.6 13.4 %fusion.11 = f32[512,1024]{1,0:T(8,128)} fusion(bf16[512,8192]{1,0:T(8,128)(2,1)S(1)} %fusion.4, bf16[8192,1024]{1,0:T(8,128)(2,1)} %param.7), kind=kOutput, calls=%fused_computation.20 | convolution fusion | flops 8589934592 | bytes 27262976 | tf_op jit(solution)/shard_map/dot_general | solution.py:13
  68.0 98.1 %all-reduce.2 = (bf16[512,1024]{1,0:T(8,128)(2,1)}, bf16[512,1024]{1,0:T(8,128)(2,1)S(1)}) all-reduce(f32[512,1024]{1,0:T(8,128)S(1)} %fusion.10, f32[512,1024]{1,0:T(8,128)} %fusion.11), channel_id=1, replica_groups=mesh['group'=2,'col'=8,'batch'=2] {'col','batch'}, use_global_device_ids=true, to_apply=%region_0.0 | all-reduce | flops 1048576 | bytes 6291456 | tf_op jit(solution)/shard_map/psum | solution.py:32
  166.1 0.0 copy-start.1
  166.1 16.1 %fusion.12 = f32[512,8192]{1,0:T(8,128)} fusion(bf16[512,1024]{1,0:T(8,128)(2,1)} %get-tuple-element.8, bf16[8192,1024]{1,0:T(8,128)(2,1)} %param.7), kind=kOutput, calls=%fused_computation.21 | convolution fusion | flops 8589934592 | bytes 34603008 | tf_op jit(solution)/shard_map/dot_general | solution.py:10
  182.2 0.0 copy-done.1
  182.2 21.0 %fusion.1 = bf16[512,8192]{1,0:T(8,128)(2,1)} fusion(bf16[256,2,8192]{2,0,1:T(8,128)(2,1)} %all-to-all-done, f32[512,8192]{1,0:T(8,128)} %fusion.12, bf16[8192,1024]{1,0:T(8,128)(2,1)} %param.8, f32[8192]{0:T(1024)S(1)} %dynamic-slice_convert_fusion, bf16[512,1024]{1,0:T(8,128)(2,1)S(1)} %get-tuple-element.9), kind=kOutput, calls=%fused_computation.2 | convolution fusion | flops 8615100416 | bytes 51412992 | tf_op jit(solution)/shard_map/dot_general | solution.py:15
  203.2 0.0 copy-start.2
  203.2 7.4 %all-to-all-start.2 = ((bf16[2,256,8192]{2,1,0:T(8,128)(2,1)}), bf16[2,256,8192]{2,1,0:T(8,128)(2,1)}, u32[]{:S(2)}, u32[]{:S(2)}) async-start(bf16[2,256,8192]{2,1,0:T(8,128)(2,1)} %bitcast.49), calls=%async_computation.2 | async-start | bytes 16777216 | tf_op jit(solution)/shard_map/all_to_all | solution.py:46
  210.6 0.0 copy-done.2
  210.6 16.0 %convolution_convert_fusion = bf16[8192,1024]{1,0:T(8,128)(2,1)} fusion(bf16[512,8192]{1,0:T(8,128)(2,1)} %copy-done, bf16[512,1024]{1,0:T(8,128)(2,1)S(1)} %copy-done.2), kind=kOutput, calls=%fused_computation.10 | convolution fusion | flops 8598323200 | bytes 26214400 | tf_op jit(solution)/shard_map/dot_general | solution.py:17
  226.6 15.7 %convert_bitcast_fusion.1 = bf16[8192,1024]{0,1:T(8,128)(2,1)} fusion(bf16[512,8192]{1,0:T(8,128)(2,1)} %bitcast.3, bf16[512,1024]{1,0:T(8,128)(2,1)S(1)} %get-tuple-element.9), kind=kOutput, calls=%fused_computation.9 | convolution fusion | flops 8598323200 | bytes 26214400 | tf_op jit(solution)/shard_map/dot_general | solution.py:18
  242.3 22.4 %copy.12 = bf16[8192,1024]{1,0:T(8,128)(2,1)} copy(bf16[8192,1024]{0,1:T(8,128)(2,1)} %convert_bitcast_fusion.1) | data formatting | bytes 33554432
  264.7 0.0 all-to-all-done.2
  264.7 7.8 %copy.15 = bf16[2,32,8,8192]{3,2,0,1:T(8,128)(2,1)} copy(bf16[2,32,8,8192]{3,2,1,0:T(8,128)(2,1)} %bitcast.13) | data formatting | bytes 16777216 | tf_op jit(solution)/shard_map/all_to_all | solution.py:46
  272.5 9.3 %convert_reduce_fusion = f32[8192]{0:T(1024)} fusion(bf16[256,2,8192]{2,0,1:T(8,128)(2,1)} %all-to-all-done, bf16[256,2,8192]{2,0,1:T(8,128)(2,1)} %all-to-all-done.1), kind=kLoop, calls=%fused_computation.8 | loop fusion | flops 25157632 | bytes 16809984 | tf_op jit(solution)/shard_map/reduce_sum | solution.py:19
  (1 shorter events, 0.0 us)
Async XLA Ops:
  8.4 14.7 %all-to-all-start.1 = ((bf16[256,2,8192]{2,0,1:T(8,128)(2,1)}), bf16[256,2,8192]{2,0,1:T(8,128)(2,1)}, u32[]{:S(2)}, u32[]{:S(2)}) async-start(bf16[256,2,8192]{2,0,1:T(8,128)(2,1)} %bitcast.45), calls=%async_computation.1 | async-start | bytes 16777216 | tf_op jit(solution)/shard_map/all_to_all | solution.py:25
  23.1 21.2 %all-to-all-start = ((bf16[256,2,8192]{2,0,1:T(8,128)(2,1)}), bf16[256,2,8192]{2,0,1:T(8,128)(2,1)}, u32[]{:S(2)}, u32[]{:S(2)}) async-start(bf16[256,2,8192]{2,0,1:T(8,128)(2,1)} %bitcast.46), calls=%async_computation | async-start | bytes 16777216 | tf_op jit(solution)/shard_map/all_to_all | solution.py:26
  51.3 3.2 %copy-start = (bf16[512,8192]{1,0:T(8,128)(2,1)}, bf16[512,8192]{1,0:T(8,128)(2,1)S(1)}, u32[]{:S(2)}) copy-start(bf16[512,8192]{1,0:T(8,128)(2,1)S(1)} %fusion.4) | copy-start | bytes 25165828
  166.1 16.1 %copy-start.1 = (bf16[16384]{0:T(1024)(128)(2,1)S(1)}, bf16[16384]{0:T(1024)(128)(2,1)}, u32[]{:S(2)}) copy-start(bf16[16384]{0:T(1024)(128)(2,1)} %param.9) | copy-start | bytes 98308
  203.2 7.4 %copy-start.2 = (bf16[512,1024]{1,0:T(8,128)(2,1)S(1)}, bf16[512,1024]{1,0:T(8,128)(2,1)}, u32[]{:S(2)}) copy-start(bf16[512,1024]{1,0:T(8,128)(2,1)} %get-tuple-element.8) | copy-start | bytes 3145732
  203.2 61.5 %all-to-all-start.2 = ((bf16[2,256,8192]{2,1,0:T(8,128)(2,1)}), bf16[2,256,8192]{2,1,0:T(8,128)(2,1)}, u32[]{:S(2)}, u32[]{:S(2)}) async-start(bf16[2,256,8192]{2,1,0:T(8,128)(2,1)} %bitcast.49), calls=%async_computation.2 | async-start | bytes 16777216 | tf_op jit(solution)/shard_map/all_to_all | solution.py:46
where the time goes:
time: 284 us; the launch traced here: 282 us
  blocking collectives  98.1 us (35%)
  matrix products  96.5 us (34%)
  local copies, waits for them, and re-layouts  48.9 us (17%)
  starting transfers between devices  21.3 us (8%)
  other arithmetic  16.2 us (6%)
    psum x1, blocking collectives, first_sum(): return lax.psum(part_sum, ('col', 'batch'))  98.1 us
    unnamed x7, local copies, waits for them, and re-layouts  25.6 us
    dot_general x1, matrix products, cross_back(): back = jnp.dot(gproj_bf, v_rows.T, preferred_element_type=jnp.float32)  21 us
    dot_general x1, matrix products, cross_back(): expanded = jnp.dot(proj_bf, u_rows.T, preferred_element_type=jnp.float32)  16.1 us
    dot_general x1, matrix products, cross_back(): u_term = jnp.dot(grad_hidden.T, proj_bf, preferred_element_type=jnp.float32)  16 us
    dot_general x1, matrix products, cross_back(): v_term = jnp.dot(inputs.T, gproj_bf, preferred_element_type=jnp.float32)  15.7 us
    dot_general x1, matrix products, cross_back(): jnp.dot(inputs, v_rows, preferred_element_type=jnp.float32)  14.3 us
    dot_general x1, matrix products, cross_back(): jnp.dot(grad_hidden, u_rows, preferred_element_type=jnp.float32)  13.4 us
  transfers between devices with their start and end apart: 3, of which 0 were waited for; matrix products, arithmetic and copies ran while one was open for 27% of the time, Pallas kernels for 0%

commit v1 on v0

v1 whole, which is shorter than its diff:
```python
import functools

import jax
import jax.numpy as jnp
from jax import lax
from jax.experimental import pallas as pl
from jax.experimental.pallas import tpu as pltpu
from jax.sharding import PartitionSpec as P

BF, F32 = jnp.bfloat16, jnp.float32
ANY = pl.BlockSpec(memory_space=pl.ANY)
MIB = 1 << 20


def params(mib=56):
    return pltpu.CompilerParams(vmem_limit_bytes=mib * MIB)


def cost(flops, nbytes):
    return pl.CostEstimate(flops=int(flops), bytes_accessed=int(nbytes), transcendentals=0)


def call(body, name, at, grid, ins, in_specs, outs, out_specs, scratch=(), flops=0, aliases=None, mib=56):
    nbytes = sum(a.size * a.dtype.itemsize for a in list(ins) + list(outs))
    return pl.pallas_call(
        body,
        out_shape=tuple(outs),
        grid_spec=pltpu.PrefetchScalarGridSpec(
            num_scalar_prefetch=1, grid=grid, in_specs=in_specs, out_specs=tuple(out_specs), scratch_shapes=list(scratch)
        ),
        input_output_aliases=aliases or {},
        compiler_params=params(mib),
        cost_estimate=cost(flops, nbytes),
        name=name,
    )(at, *ins)


def shape(dims, dtype):
    return jax.ShapeDtypeStruct(dims, dtype)


def cut_half(at, x, half):
    rows = x.shape[0]
    pieces = 4
    step = rows // pieces

    def body(at_ref, x_ref, o_ref, sems):
        start = pl.multiple_of((1 - at_ref[0]) * half, half)
        copies = [
            pltpu.make_async_copy(
                x_ref.at[pl.ds(i * step, step), pl.ds(start, half)], o_ref.at[pl.ds(i * step, step), :], sems.at[i]
            )
            for i in range(pieces)
        ]
        for c in copies:
            c.start()
        for c in copies:
            c.wait()

    return call(
        body, "cut_half", at, (1,), [x], [ANY], [shape((rows, half), x.dtype)], [ANY], [pltpu.SemaphoreType.DMA((pieces,))]
    )[0]


def put_half(at, part, out):
    rows, half = part.shape
    pieces = 4
    step = rows // pieces

    def body(at_ref, p_ref, i_ref, o_ref, sems):
        start = pl.multiple_of((1 - at_ref[0]) * half, half)
        copies = [
            pltpu.make_async_copy(
                p_ref.at[pl.ds(i * step, step), :], o_ref.at[pl.ds(i * step, step), pl.ds(start, half)], sems.at[i]
            )
            for i in range(pieces)
        ]
        for c in copies:
            c.start()
        for c in copies:
            c.wait()

    return call(
        body,
        "put_half",
        at,
        (1,),
        [part, out],
        [ANY, ANY],
        [shape(out.shape, out.dtype)],
        [ANY],
        [pltpu.SemaphoreType.DMA((pieces,))],
        aliases={2: 0},
    )[0]


def project(at, x, v, offset):
    rows, half, rank = x.shape[0], v.shape[0], v.shape[1]
    tk = min(1024, half)
    steps = half // tk

    def body(at_ref, x_ref, v_ref, o_ref, acc):
        k = pl.program_id(0)
        part = jnp.dot(x_ref[...], v_ref[...], preferred_element_type=F32)

        @pl.when(k == 0)
        def _():
            acc[...] = part

        @pl.when(k > 0)
        def _():
            acc[...] += part

        @pl.when(k == steps - 1)
        def _():
            o_ref[...] = acc[...].astype(BF)

    where = (lambda k, at: (0, at[0] * steps + k)) if offset else (lambda k, at: (0, k))
    return call(
        body,
        "project",
        at,
        (steps,),
        [x, v],
        [pl.BlockSpec((rows, tk), where), pl.BlockSpec((tk, rank), lambda k, at: (k, 0))],
        [shape((rows, rank), BF)],
        [pl.BlockSpec((rows, rank), lambda k, at: (0, 0))],
        [pltpu.VMEM((rows, rank), F32)],
        flops=2 * rows * half * rank,
    )[0]


def hidden(c, x):
    return (c.astype(F32) * x.astype(F32)).astype(BF)


def back_project(at, x, x_o, c, c_o, u):
    rows, half, rank = x.shape[0], u.shape[0], u.shape[1]
    tk = min(1024, half)
    steps = half // tk

    def body(at_ref, x_ref, xo_ref, c_ref, co_ref, u_ref, own_ref, oth_ref, b_ref, h, acc):
        k = pl.program_id(0)
        h[:rows, :] = hidden(c_ref[...], x_ref[...])
        h[rows:, :] = hidden(co_ref[...], xo_ref[...])
        b_ref[...] = jnp.sum(h[...].astype(F32), axis=0, keepdims=True)
        part = jnp.dot(h[...], u_ref[...], preferred_element_type=F32)

        @pl.when(k == 0)
        def _():
            acc[...] = part

        @pl.when(k > 0)
        def _():
            acc[...] += part

        @pl.when(k == steps - 1)
        def _():
            own_ref[...] = acc[:rows, :].astype(BF)
            oth_ref[...] = acc[rows:, :].astype(BF)

    own = pl.BlockSpec((rows, tk), lambda k, at: (0, at[0] * steps + k))
    oth = pl.BlockSpec((rows, tk), lambda k, at: (0, k))
    full = pl.BlockSpec((rows, rank), lambda k, at: (0, 0))
    return call(
        body,
        "back_project",
        at,
        (steps,),
        [x, x_o, c, c_o, u],
        [own, oth, own, oth, pl.BlockSpec((tk, rank), lambda k, at: (k, 0))],
        [shape((rows, rank), BF), shape((rows, rank), BF), shape((1, half), F32)],
        [full, full, pl.BlockSpec((1, tk), lambda k, at: (0, k))],
        [pltpu.VMEM((2 * rows, tk), BF), pltpu.VMEM((2 * rows, rank), F32)],
        flops=4 * rows * half * rank,
    )


def u_grad(at, x, x_o, c, c_o, p, p_o, half):
    rows, rank = p.shape
    tw = min(1024, half)
    steps = half // tw

    def body(at_ref, x_ref, xo_ref, c_ref, co_ref, p_ref, po_ref, o_ref):
        h = jnp.concatenate([hidden(c_ref[...], x_ref[...]), hidden(co_ref[...], xo_ref[...])], 0)
        pp = jnp.concatenate([p_ref[...], po_ref[...]], 0)
        o_ref[...] = lax.dot_general(h, pp, (((0,), (0,)), ((), ())), preferred_element_type=F32).astype(BF)

    own = pl.BlockSpec((rows, tw), lambda k, at: (0, at[0] * steps + k))
    oth = pl.BlockSpec((rows, tw), lambda k, at: (0, k))
    full = pl.BlockSpec((rows, rank), lambda k, at: (0, 0))
    return call(
        body,
        "u_grad",
        at,
        (steps,),
        [x, x_o, c, c_o, p, p_o],
        [own, oth, own, oth, full, full],
        [shape((half, rank), BF)],
        [pl.BlockSpec((tw, rank), lambda k, at: (k, 0))],
        flops=4 * rows * half * rank,
    )[0]


def v_grad(at, x, x_o, g, g_o, half):
    rows, rank = g.shape
    tw = min(1024, half)
    steps = half // tw

    def body(at_ref, x_ref, xo_ref, g_ref, go_ref, o_ref):
        xx = jnp.concatenate([x_ref[...], xo_ref[...]], 0)
        gg = jnp.concatenate([g_ref[...], go_ref[...]], 0)
        o_ref[...] = lax.dot_general(xx, gg, (((0,), (0,)), ((), ())), preferred_element_type=F32).astype(BF)

    own = pl.BlockSpec((rows, tw), lambda k, at: (0, at[0] * steps + k))
    oth = pl.BlockSpec((rows, tw), lambda k, at: (0, k))
    full = pl.BlockSpec((rows, rank), lambda k, at: (0, 0))
    return call(
        body,
        "v_grad",
        at,
        (steps,),
        [x, x_o, g, g_o],
        [own, oth, full, full],
        [shape((half, rank), BF)],
        [pl.BlockSpec((tw, rank), lambda k, at: (k, 0))],
        flops=4 * rows * half * rank,
    )[0]


def input_grad(at, c, c_o, u, v, bias, p, p_o, g, g_o):
    rows, rank = p.shape
    half, width = u.shape[0], c.shape[1]
    tw = min(1024, half)
    steps = half // tw

    def body(at_ref, c_ref, co_ref, u_ref, v_ref, b_ref, p_ref, po_ref, g_ref, go_ref, own_ref, oth_ref):
        pp = jnp.concatenate([p_ref[...], po_ref[...]], 0)
        gg = jnp.concatenate([g_ref[...], go_ref[...]], 0)
        nt = (((1,), (1,)), ((), ()))
        ex = lax.dot_general(pp, u_ref[...], nt, preferred_element_type=F32)
        bk = lax.dot_general(gg, v_ref[...], nt, preferred_element_type=F32)
        ex = ex + b_ref[...].astype(F32)
        cf, cof = c_ref[...].astype(F32), co_ref[...].astype(F32)
        own_ref[...] = (cf * ex[:rows] + cf + bk[:rows]).astype(BF)
        oth_ref[...] = (cof * ex[rows:] + cof + bk[rows:]).astype(BF)

    own = pl.BlockSpec((rows, tw), lambda k, at: (0, at[0] * steps + k))
    oth = pl.BlockSpec((rows, tw), lambda k, at: (0, k))
    full = pl.BlockSpec((rows, rank), lambda k, at: (0, 0))
    fac = pl.BlockSpec((tw, rank), lambda k, at: (k, 0))
    return call(
        body,
        "input_grad",
        at,
        (steps,),
        [c, c_o, u, v, bias, p, p_o, g, g_o],
        [own, oth, fac, fac, pl.BlockSpec((1, tw), lambda k, at: (0, at[0] * steps + k)), full, full, full, full],
        [shape((rows, width), BF), shape((rows, half), BF)],
        [own, oth],
        flops=8 * rows * half * rank,
    )


def pieces_of(at, a, b, n):
    rows, rank = a.shape
    each = rows // n

    def body(at_ref, a_ref, b_ref, *outs):
        for d in range(n):
            here = pl.ds(pl.multiple_of((at_ref[1] ^ d) * each, each), each)
            outs[d][...] = (a_ref[here, :].astype(F32) + b_ref[here, :].astype(F32)).astype(BF)

    full = pl.BlockSpec((rows, rank), lambda i, at: (0, 0))
    one = pl.BlockSpec((each, rank), lambda i, at: (0, 0))
    return call(body, "pieces_of", at, (1,), [a, b], [full, full], [shape((each, rank), BF)] * n, [one] * n, mib=16)


def add_pieces(at, parts):
    def body(at_ref, *refs):
        total = refs[0][...].astype(F32)
        for r in refs[1:-1]:
            total += r[...].astype(F32)
        refs[-1][...] = total.astype(BF)

    one = pl.BlockSpec(parts[0].shape, lambda i, at: (0, 0))
    return call(body, "add_pieces", at, (1,), parts, [one] * len(parts), [shape(parts[0].shape, BF)], [one], mib=16)[0]


def join_pieces(at, parts):
    n = len(parts)
    each, rank = parts[0].shape

    def body(at_ref, *refs):
        for d in range(n):
            here = pl.ds(pl.multiple_of((at_ref[1] ^ d) * each, each), each)
            refs[-1][here, :] = refs[d][...]

    one = pl.BlockSpec((each, rank), lambda i, at: (0, 0))
    full = pl.BlockSpec((n * each, rank), lambda i, at: (0, 0))
    return call(body, "join_pieces", at, (1,), parts, [one] * n, [shape((n * each, rank), BF)], [full], mib=16)[0]


def solution(mesh):
    n = mesh.shape["col"]
    swap = [(0, 1), (1, 0)]

    def trade(a):
        return lax.ppermute(a, "batch", swap)

    def to(a, d):
        return lax.ppermute(a, "col", [(i, i ^ d) for i in range(n)])

    def direct_sum(at, mine, theirs):
        parts = pieces_of(at, mine, theirs, n)
        parts = [parts[0]] + [to(parts[d], d) for d in range(1, n)]
        total = add_pieces(at, parts)
        return join_pieces(at, [total] + [to(total, d) for d in range(1, n)])

    def plain_sum(mine, theirs):
        both = mine.astype(F32) + theirs.astype(F32)
        if both.shape[0] % (16 * n):
            return lax.psum(both, "col").astype(BF)
        total = lax.psum_scatter(both.astype(BF), "col", scatter_dimension=0, tiled=True)
        return lax.all_gather(total, "col", axis=0, tiled=True)

    def local(x, c, u, v, bias):
        half = u.shape[0]
        core = lax.axis_index("batch")
        at = jnp.stack([core, lax.axis_index("col")]).astype(jnp.int32)
        direct = x.shape[0] % (16 * n) == 0 and n & (n - 1) == 0
        x_o = trade(cut_half(at, x, half))
        c_o = trade(cut_half(at, c, half))
        own = project(at, x, v, True)
        theirs = trade(own)
        mine = project(at, x_o, v, False)
        p_o = plain_sum(mine, theirs)
        p = trade(p_o)
        own_g, mine_g, b_sum = back_project(at, x, x_o, c, c_o, u)
        theirs_g = trade(own_g)
        g_o = direct_sum(at, mine_g, theirs_g) if direct else plain_sum(mine_g, theirs_g)
        g = trade(g_o)
        grad_u = u_grad(at, x, x_o, c, c_o, p, p_o, half)
        out, out_o = input_grad(at, c, c_o, u, v, bias[None, :], p, p_o, g, g_o)
        back = trade(out_o)
        grad_v = v_grad(at, x, x_o, g, g_o, half)
        return put_half(at, back, out), grad_u, grad_v, b_sum[0]

    return jax.shard_map(
        local,
        mesh=mesh,
        in_specs=(
            P(("group", "batch"), "col"),
            P(("group", "batch"), "col"),
            P(("col", "batch"), None),
            P(("col", "batch"), None),
            P("col"),
        ),
        out_specs=(
            P(("group", "batch"), "col"),
            P(("group", "col", "batch"), None),
            P(("group", "col", "batch"), None),
            P(("group", "col", "batch")),
        ),
        check_vma=False,
    )
```

time: 284 us -> 598 us (2.11)
  Pallas kernels: 0 us -> 494 us
  matrix products: 96.5 us -> 0 us
  blocking collectives: 98.1 us -> 31.7 us
  local copies, waits for them, and re-layouts: 48.9 us -> 6.61 us
  waiting for transfers between devices: 0.01 us -> 21.3 us
  other arithmetic: 16.2 us -> 2.63 us
  between operations: 0.71 us -> 14.2 us
    pallas_call x0 -> x12, Pallas kernels: none -> 494 us  [call(): pl.pallas_call(body, out_shape=tuple(outs), grid_spec=pltpu.PrefetchScala...]
    psum x1 -> x0, blocking collectives: 98.1 us -> none  [first_sum(): return lax.psum(part_sum, ('col', 'batch'))]
    dot_general x6 -> x0, matrix products: 96.5 us -> none  [the longest x1 21 us: cross_back(): back = jnp.dot(gproj_bf, v_rows.T, preferred_element_type=jnp.float32)]
    all_gather x0 -> x1, blocking collectives: none -> 31.7 us  [plain_sum(): return lax.all_gather(total, 'col', axis=0, tiled=True)]
    ppermute x0 -> x21, starting transfers between devices: none -> 26.5 us  [the longest x14 25.2 us: to(): return lax.ppermute(a, 'col', [(i, i ^ d) for i in range(n)])]
    all_to_all x3 -> x0, local copies, waits for them, and re-layouts: 23.3 us -> none  [the longest x1 7.77 us: local(): lax.all_to_all(cotangent, 'batch', split_axis=1, concat_axis=0, tiled=True)]
    all_to_all x3 -> x0, starting transfers between devices: 21.3 us -> none  [the longest x1 7.41 us: local(): lax.all_to_all(grad_half, 'batch', split_axis=0, concat_axis=1, tiled=True)]
    unnamed x7 -> x18, local copies, waits for them, and re-layouts: 25.6 us -> 5.88 us
  transfers between devices with their start and end apart: 3 -> 22, of which waited for: 0 -> 8; matrix products, arithmetic and copies ran while one was open for 27% -> 0% of each run, Pallas kernels for 0% -> 35%
where the time goes in v1:
time: 598 us; the launch traced here: 597 us
  Pallas kernels  494 us (83%)
  blocking collectives  31.7 us (5%)
  starting transfers between devices  26.6 us (4%)
  waiting for transfers between devices  21.3 us (4%)
  between operations  14.2 us (2%)
  local copies, waits for them, and re-layouts  6.61 us (1%)
    pallas_call x12, Pallas kernels, call(): pl.pallas_call(body, out_shape=tuple(outs), grid_spec=pltpu.PrefetchScala...  494 us
    all_gather x1, blocking collectives, plain_sum(): return lax.all_gather(total, 'col', axis=0, tiled=True)  31.7 us
    ppermute x14, starting transfers between devices, to(): return lax.ppermute(a, 'col', [(i, i ^ d) for i in range(n)])  25.2 us
  transfers between devices with their start and end apart: 22, of which 8 were waited for; matrix products, arithmetic and copies ran while one was open for 0% of the time, Pallas kernels for 35%

profile of v1, /device:TPU:0, one launch (start us, length us, event | category | flops | bytes accessed | tf_op | source)
XLA Modules:
  0.0 596.7 jit_solution(14220599306029103240)
XLA Ops:
  7.2 0.0 reduce-scatter.2.cloned.1.call-start
  7.2 0.6 pad_add_fusion.at_ref
  7.8 128.9 %cut_half.3 = bf16[256,8192]{1,0:T(8,128)(2,1)} custom-call(s32[2]{0:T(128)} %pad_add_fusion.at_ref, bf16[256,16384]{1,0:T(8,128)(2,1)} %x_ref.11), custom_call_target="tpu_custom_call" | custom-call | bytes 12582912 | tf_op jit(solution)/shard_map/cut_half/pallas_call | solution.py:25
  136.7 0.5 collective-permute-start.1
  137.2 128.9 %cut_half.2 = bf16[256,8192]{1,0:T(8,128)(2,1)} custom-call(s32[2]{0:T(128)} %pad_add_fusion.at_ref, bf16[256,16384]{1,0:T(8,128)(2,1)} %c_ref.5), custom_call_target="tpu_custom_call" | custom-call | bytes 12582912 | tf_op jit(solution)/shard_map/cut_half/pallas_call | solution.py:25
  266.1 0.1 collective-permute-start
  266.2 13.1 %project.3 = bf16[256,1024]{1,0:T(8,128)(2,1)} custom-call(s32[2]{0:T(128)} %pad_add_fusion.at_ref, bf16[256,16384]{1,0:T(8,128)(2,1)} %x_ref.11, bf16[8192,1024]{1,0:T(8,128)(2,1)} %v_ref.5), custom_call_target="tpu_custom_call" | custom-call | flops 4294967296 | bytes 25690112 | tf_op jit(solution)/shard_map/project/pallas_call | solution.py:25
  279.3 0.5 collective-permute-start.2
  279.8 2.0 copy-done.3
  281.8 13.1 %project.2 = bf16[256,1024]{1,0:T(8,128)(2,1)} custom-call(s32[2]{0:T(128)} %pad_add_fusion.at_ref, bf16[256,8192]{1,0:T(8,128)(2,1)} %copy-done.3, bf16[8192,1024]{1,0:T(8,128)(2,1)} %v_ref.5), custom_call_target="tpu_custom_call" | custom-call | flops 4294967296 | bytes 21495808 | tf_op jit(solution)/shard_map/project/pallas_call | solution.py:25
  294.9 2.0 add_convert_fusion
  297.0 0.0 reduce-scatter.2.cloned.1.call-update
  297.0 18.6 %back_project.1 = (bf16[256,1024]{1,0:T(8,128)(2,1)}, bf16[256,1024]{1,0:T(8,128)(2,1)}, f32[1,8192]{1,0:T(1,128)}) custom-call(s32[2]{0:T(128)} %pad_add_fusion.at_ref, bf16[256,16384]{1,0:T(8,128)(2,1)} %x_ref.11, bf16[256,8192]{1,0:T(8,128)(2,1)} %copy-done.3, bf16[256,16384]{1,0:T(8,128)(2,1)} %c_ref.5, bf16[256,8192]{1,0:T(8,128)(2,1)} %collective-permute-done.co_ref, ...), custom_call_target="tpu_custom_call" | custom-call | flops 8589934592 | bytes 43024384 | tf_op jit(solution)/shard_map/back_project/pallas_call | solution.py:25
  315.7 0.1 collective-permute-start.4
  315.7 2.1 collective-permute-done.4.b_ref
  317.8 1.1 copy-done.1
  318.8 0.7 pieces_of.1
  319.5 2.7 collective-permute-start.5
  322.2 1.6 collective-permute-start.6
  323.8 3.0 collective-permute-start.8
  326.8 1.3 collective-permute-start.9
  328.1 3.6 collective-permute-start.10
  331.7 5.4 collective-permute-done.9.refs_5_
  337.1 1.6 collective-permute-done.11.refs_7_
  338.8 0.6 add_pieces.1.refs_0_
  339.4 2.1 collective-permute-start.18
  341.5 1.7 collective-permute-start.17
  343.2 2.6 collective-permute-start.16
  345.8 1.3 collective-permute-start.15
  347.1 0.9 collective-permute-start.14
  348.0 3.5 collective-permute-start.13
  351.5 0.9 collective-permute-start.12
  352.4 2.0 collective-permute-done.16.refs_5_
  354.4 0.2 collective-permute-done.15.refs_4_
  354.6 1.3 collective-permute-done.13.refs_2_
  355.9 0.6 join_pieces.1.go_ref
  356.5 0.1 collective-permute-start.19
  356.6 7.5 %reduce-scatter.2.cloned.1.call-done = bf16[32,1024]{1,0:T(8,128)(2,1)} async-done(((bf16[256,1024]{1,0:T(8,128)(2,1)}), bf16[32,1024]{1,0:T(8,128)(2,1)}) %reduce-scatter.2.cloned.1.call-update) | async-done | bytes 65552 | tf_op jit(solution)/shard_map/reduce_scatter | solution.py:324
  364.1 31.7 %all_gather.3.po_ref = bf16[256,1024]{1,0:T(8,128)(2,1)S(1)} all-gather(bf16[32,1024]{1,0:T(8,128)(2,1)} %reduce-scatter.2.cloned.1.call-done), channel_id=1, replica_groups=mesh['group'=2,'col'=8,'batch'=2] {'col'}, dimensions={0}, use_global_device_ids=true | all-gather | bytes 589824 | tf_op jit(solution)/shard_map/all_gather | solution.py:325
  395.7 0.7 broadcast_in_dim.3.b_ref
  396.5 1.2 collective-permute-done.3.p_ref
  397.6 0.8 copy-done.6
  398.5 26.4 %input_grad.1 = (bf16[256,16384]{1,0:T(8,128)(2,1)}, bf16[256,8192]{1,0:T(8,128)(2,1)}) custom-call(s32[2]{0:T(128)} %pad_add_fusion.at_ref, bf16[256,16384]{1,0:T(8,128)(2,1)} %c_ref.5, bf16[256,8192]{1,0:T(8,128)(2,1)} %collective-permute-done.co_ref, bf16[8192,1024]{1,0:T(8,128)(2,1)} %u_ref.3, bf16[8192,1024]{1,0:T(8,128)(2,1)} %v_ref.5, ...), custom_call_target="tpu_custom_call" | custom-call | flops 17179869184 | bytes 60850176 | tf_op jit(solution)/shard_map/input_grad/pallas_call | solution.py:25
  424.9 0.1 collective-permute-start.20
  425.0 16.1 %v_grad.1 = bf16[8192,1024]{1,0:T(8,128)(2,1)} custom-call(s32[2]{0:T(128)} %pad_add_fusion.at_ref, bf16[256,16384]{1,0:T(8,128)(2,1)} %x_ref.11, bf16[256,8192]{1,0:T(8,128)(2,1)} %copy-done.3, bf16[256,1024]{1,0:T(8,128)(2,1)} %copy-done.8, bf16[256,1024]{1,0:T(8,128)(2,1)} %copy-done), custom_call_target="tpu_custom_call" | custom-call | flops 8589934592 | bytes 30408704 | tf_op jit(solution)/shard_map/v_grad/pallas_call | solution.py:25
  441.2 17.9 %u_grad.1 = bf16[8192,1024]{1,0:T(8,128)(2,1)} custom-call(s32[2]{0:T(128)} %pad_add_fusion.at_ref, bf16[256,16384]{1,0:T(8,128)(2,1)} %x_ref.11, bf16[256,8192]{1,0:T(8,128)(2,1)} %copy-done.3, bf16[256,16384]{1,0:T(8,128)(2,1)} %c_ref.5, bf16[256,8192]{1,0:T(8,128)(2,1)} %collective-permute-done.co_ref, bf16[256,1024]{1,0:T(8,128)(2,1)} %copy-done.6, ...), custom_call_target="tpu_custom_call" | custom-call | flops 8589934592 | bytes 42991616 | tf_op jit(solution)/shard_map/u_grad/pallas_call | solution.py:25
  459.1 2.0 copy-done.4
  461.0 128.9 %put_half.1 = bf16[256,16384]{1,0:T(8,128)(2,1)} custom-call(s32[2]{0:T(128)} %pad_add_fusion.at_ref, bf16[256,8192]{1,0:T(8,128)(2,1)} %copy-done.4, bf16[256,16384]{1,0:T(8,128)(2,1)} %get-tuple-element.28.i_ref), custom_call_target="tpu_custom_call", output_to_operand_aliasing={{}: (2, {})} | custom-call | bytes 20971520 | tf_op jit(solution)/shard_map/put_half/pallas_call | solution.py:25
  (31 shorter events, 0.1 us)
Async XLA Ops:
  7.2 356.9 %reduce-scatter.2.cloned.1.call-start = ((), (), s32[]{:S(2)}) async-start(), calls=%async_computation.1 | async-start | bytes 589824 | tf_op jit(solution)/shard_map/reduce_scatter | solution.py:324
  136.7 143.1 %collective-permute-start.1 = (bf16[256,8192]{1,0:T(8,128)(2,1)}, bf16[256,8192]{1,0:T(8,128)(2,1)S(1)}, u32[]{:S(2)}, u32[]{:S(2)}) collective-permute-start(bf16[256,8192]{1,0:T(8,128)(2,1)} %cut_half.3), channel_id=1, source_target_pairs={{0,1},{1,0},{2,3},{3,2},{4,5},{5,4},{6,7},{7,6},{8,9},{9,8},{10,11... | collective-permute-start | bytes 12582920 | tf_op jit(solution)/shard_map/ppermute | solution.py:309
  266.1 30.9 %collective-permute-start = (bf16[256,8192]{1,0:T(8,128)(2,1)}, bf16[256,8192]{1,0:T(8,128)(2,1)}, u32[]{:S(2)}, u32[]{:S(2)}) collective-permute-start(bf16[256,8192]{1,0:T(8,128)(2,1)} %cut_half.2), channel_id=1, source_target_pairs={{0,1},{1,0},{2,3},{3,2},{4,5},{5,4},{6,7},{7,6},{8,9},{9,8},{10,11... | collective-permute-start | bytes 12582920 | tf_op jit(solution)/shard_map/ppermute | solution.py:309
  279.3 15.6 %collective-permute-start.2 = (bf16[256,1024]{1,0:T(8,128)(2,1)}, bf16[256,1024]{1,0:T(8,128)(2,1)S(1)}, u32[]{:S(2)}, u32[]{:S(2)}) collective-permute-start(bf16[256,1024]{1,0:T(8,128)(2,1)} %project.3), channel_id=1, source_target_pairs={{0,1},{1,0},{2,3},{3,2},{4,5},{5,4},{6,7},{7,6},{8,9},{9,8},{10,11... | collective-permute-start | bytes 1572872 | tf_op jit(solution)/shard_map/ppermute | solution.py:309
  279.8 2.0 copy-start.3
  297.0 20.8 %copy-start.2 = (s32[2]{0:T(128)S(1)}, s32[2]{0:T(128)}, u32[]{:S(2)}) copy-start(s32[2]{0:T(128)} %pad_add_fusion.at_ref) | copy-start | bytes 28
  297.0 98.7 %copy-start.7 = (bf16[16384]{0:T(1024)(128)(2,1)S(1)}, bf16[16384]{0:T(1024)(128)(2,1)}, u32[]{:S(2)}) copy-start(bf16[16384]{0:T(1024)(128)(2,1)} %param.9) | copy-start | bytes 98308
  315.7 2.1 collective-permute-start.4
  317.8 1.1 copy-start.1
  319.5 8.6 %collective-permute-start.5 = (bf16[32,1024]{1,0:T(8,128)(2,1)S(1)}, bf16[32,1024]{1,0:T(8,128)(2,1)S(1)}, u32[]{:S(2)}, u32[]{:S(2)}) collective-permute-start(bf16[32,1024]{1,0:T(8,128)(2,1)S(1)} %get-tuple-element.20), channel_id=1, source_target_pairs={{0,2},{2,0},{4,6},{6,4},{8,10},{10,8},{12,14},{14,12},{1,3},{3,1},... | collective-permute-start | bytes 196616 | tf_op jit(solution)/shard_map/ppermute | solution.py:312
  322.2 9.5 %collective-permute-start.6 = (bf16[32,1024]{1,0:T(8,128)(2,1)S(1)}, bf16[32,1024]{1,0:T(8,128)(2,1)S(1)}, u32[]{:S(2)}, u32[]{:S(2)}) collective-permute-start(bf16[32,1024]{1,0:T(8,128)(2,1)S(1)} %get-tuple-element.21), channel_id=1, source_target_pairs={{0,4},{2,6},{4,0},{6,2},{8,12},{10,14},{12,8},{14,10},{1,5},{3,7},... | collective-permute-start | bytes 196616 | tf_op jit(solution)/shard_map/ppermute | solution.py:312
  323.8 7.9 %collective-permute-start.7 = (bf16[32,1024]{1,0:T(8,128)(2,1)S(1)}, bf16[32,1024]{1,0:T(8,128)(2,1)S(1)}, u32[]{:S(2)}, u32[]{:S(2)}) collective-permute-start(bf16[32,1024]{1,0:T(8,128)(2,1)S(1)} %get-tuple-element.22), channel_id=1, source_target_pairs={{0,6},{2,4},{4,2},{6,0},{8,14},{10,12},{12,10},{14,8},{1,7},{3,5},... | collective-permute-start | bytes 196616 | tf_op jit(solution)/shard_map/ppermute | solution.py:312
  323.8 7.9 %collective-permute-start.8 = (bf16[32,1024]{1,0:T(8,128)(2,1)S(1)}, bf16[32,1024]{1,0:T(8,128)(2,1)S(1)}, u32[]{:S(2)}, u32[]{:S(2)}) collective-permute-start(bf16[32,1024]{1,0:T(8,128)(2,1)S(1)} %get-tuple-element.23), channel_id=1, source_target_pairs={{0,8},{2,10},{4,12},{6,14},{8,0},{10,2},{12,4},{14,6},{1,9},{3,11}... | collective-permute-start | bytes 196616 | tf_op jit(solution)/shard_map/ppermute | solution.py:312
  326.8 10.3 %collective-permute-start.9 = (bf16[32,1024]{1,0:T(8,128)(2,1)S(1)}, bf16[32,1024]{1,0:T(8,128)(2,1)S(1)}, u32[]{:S(2)}, u32[]{:S(2)}) collective-permute-start(bf16[32,1024]{1,0:T(8,128)(2,1)S(1)} %get-tuple-element.24), channel_id=1, source_target_pairs={{0,10},{2,8},{4,14},{6,12},{8,2},{10,0},{12,6},{14,4},{1,11},{3,9}... | collective-permute-start | bytes 196616 | tf_op jit(solution)/shard_map/ppermute | solution.py:312
  328.1 9.1 %collective-permute-start.10 = (bf16[32,1024]{1,0:T(8,128)(2,1)S(1)}, bf16[32,1024]{1,0:T(8,128)(2,1)S(1)}, u32[]{:S(2)}, u32[]{:S(2)}) collective-permute-start(bf16[32,1024]{1,0:T(8,128)(2,1)S(1)} %get-tuple-element.25), channel_id=1, source_target_pairs={{0,12},{2,14},{4,8},{6,10},{8,4},{10,6},{12,0},{14,2},{1,13},{3,15... | collective-permute-start | bytes 196616 | tf_op jit(solution)/shard_map/ppermute | solution.py:312
  331.7 7.1 %collective-permute-start.11 = (bf16[32,1024]{1,0:T(8,128)(2,1)S(1)}, bf16[32,1024]{1,0:T(8,128)(2,1)S(1)}, u32[]{:S(2)}, u32[]{:S(2)}) collective-permute-start(bf16[32,1024]{1,0:T(8,128)(2,1)S(1)} %get-tuple-element.26), channel_id=1, source_target_pairs={{0,14},{2,12},{4,10},{6,8},{8,6},{10,4},{12,2},{14,0},{1,15},{3,13... | collective-permute-start | bytes 196616 | tf_op jit(solution)/shard_map/ppermute | solution.py:312
  339.4 8.6 %collective-permute-start.18 = (bf16[32,1024]{1,0:T(8,128)(2,1)S(1)}, bf16[32,1024]{1,0:T(8,128)(2,1)S(1)}, u32[]{:S(2)}, u32[]{:S(2)}) collective-permute-start(bf16[32,1024]{1,0:T(8,128)(2,1)S(1)} %add_pieces.1.refs_0_), channel_id=1, source_target_pairs={{0,14},{2,12},{4,10},{6,8},{8,6},{10,4},{12,2},{14,0},{1,15},{3,13... | collective-permute-start | bytes 196616 | tf_op jit(solution)/shard_map/ppermute | solution.py:312
  341.5 10.0 %collective-permute-start.17 = (bf16[32,1024]{1,0:T(8,128)(2,1)S(1)}, bf16[32,1024]{1,0:T(8,128)(2,1)S(1)}, u32[]{:S(2)}, u32[]{:S(2)}) collective-permute-start(bf16[32,1024]{1,0:T(8,128)(2,1)S(1)} %add_pieces.1.refs_0_), channel_id=1, source_target_pairs={{0,12},{2,14},{4,8},{6,10},{8,4},{10,6},{12,0},{14,2},{1,13},{3,15... | collective-permute-start | bytes 196616 | tf_op jit(solution)/shard_map/ppermute | solution.py:312
  343.2 11.2 %collective-permute-start.16 = (bf16[32,1024]{1,0:T(8,128)(2,1)S(1)}, bf16[32,1024]{1,0:T(8,128)(2,1)S(1)}, u32[]{:S(2)}, u32[]{:S(2)}) collective-permute-start(bf16[32,1024]{1,0:T(8,128)(2,1)S(1)} %add_pieces.1.refs_0_), channel_id=1, source_target_pairs={{0,10},{2,8},{4,14},{6,12},{8,2},{10,0},{12,6},{14,4},{1,11},{3,9}... | collective-permute-start | bytes 196616 | tf_op jit(solution)/shard_map/ppermute | solution.py:312
  345.8 8.8 %collective-permute-start.15 = (bf16[32,1024]{1,0:T(8,128)(2,1)S(1)}, bf16[32,1024]{1,0:T(8,128)(2,1)S(1)}, u32[]{:S(2)}, u32[]{:S(2)}) collective-permute-start(bf16[32,1024]{1,0:T(8,128)(2,1)S(1)} %add_pieces.1.refs_0_), channel_id=1, source_target_pairs={{0,8},{2,10},{4,12},{6,14},{8,0},{10,2},{12,4},{14,6},{1,9},{3,11}... | collective-permute-start | bytes 196616 | tf_op jit(solution)/shard_map/ppermute | solution.py:312
  347.1 7.5 %collective-permute-start.14 = (bf16[32,1024]{1,0:T(8,128)(2,1)S(1)}, bf16[32,1024]{1,0:T(8,128)(2,1)S(1)}, u32[]{:S(2)}, u32[]{:S(2)}) collective-permute-start(bf16[32,1024]{1,0:T(8,128)(2,1)S(1)} %add_pieces.1.refs_0_), channel_id=1, source_target_pairs={{0,6},{2,4},{4,2},{6,0},{8,14},{10,12},{12,10},{14,8},{1,7},{3,5},... | collective-permute-start | bytes 196616 | tf_op jit(solution)/shard_map/ppermute | solution.py:312
  348.0 7.9 %collective-permute-start.13 = (bf16[32,1024]{1,0:T(8,128)(2,1)S(1)}, bf16[32,1024]{1,0:T(8,128)(2,1)S(1)}, u32[]{:S(2)}, u32[]{:S(2)}) collective-permute-start(bf16[32,1024]{1,0:T(8,128)(2,1)S(1)} %add_pieces.1.refs_0_), channel_id=1, source_target_pairs={{0,4},{2,6},{4,0},{6,2},{8,12},{10,14},{12,8},{14,10},{1,5},{3,7},... | collective-permute-start | bytes 196616 | tf_op jit(solution)/shard_map/ppermute | solution.py:312
  351.5 4.4 collective-permute-start.12
  356.5 41.1 %copy-start = (bf16[256,1024]{1,0:T(8,128)(2,1)}, bf16[256,1024]{1,0:T(8,128)(2,1)S(1)}, u32[]{:S(2)}) copy-start(bf16[256,1024]{1,0:T(8,128)(2,1)S(1)} %join_pieces.1.go_ref) | copy-start | bytes 1572868
  356.5 40.0 %collective-permute-start.19 = (bf16[256,1024]{1,0:T(8,128)(2,1)S(1)}, bf16[256,1024]{1,0:T(8,128)(2,1)S(1)}, u32[]{:S(2)}, u32[]{:S(2)}) collective-permute-start(bf16[256,1024]{1,0:T(8,128)(2,1)S(1)} %join_pieces.1.go_ref), channel_id=1, source_target_pairs={{0,1},{1,0},{2,3},{3,2},{4,5},{5,4},{6,7},{7,6},{8,9},{9,8},{10,11... | collective-permute-start | bytes 1572872 | tf_op jit(solution)/shard_map/ppermute | solution.py:309
  395.7 1.9 copy-start.5
  395.7 1.9 collective-permute-start.3
  396.5 1.2 copy-start.8
  397.6 0.8 copy-start.6
  424.9 34.2 %collective-permute-start.20 = (bf16[256,8192]{1,0:T(8,128)(2,1)}, bf16[256,8192]{1,0:T(8,128)(2,1)S(1)}, u32[]{:S(2)}, u32[]{:S(2)}) collective-permute-start(bf16[256,8192]{1,0:T(8,128)(2,1)} %get-tuple-element.27), channel_id=1, source_target_pairs={{0,1},{1,0},{2,3},{3,2},{4,5},{5,4},{6,7},{7,6},{8,9},{9,8},{10,11... | collective-permute-start | bytes 12582920 | tf_op jit(solution)/shard_map/ppermute | solution.py:309
  459.1 2.0 copy-start.4
Sparse Core Ops, SparseCore 0:
  297.1 66.9 reduce-scatter.1

commit v2 on v0

v2 whole, which is shorter than its diff:
```python
import jax
import jax.numpy as jnp
from jax import lax
from jax.experimental import pallas as pl
from jax.experimental.pallas import tpu as pltpu
from jax.sharding import PartitionSpec as P

BF, F32 = jnp.bfloat16, jnp.float32
MIB = 1 << 20
NT = (((1,), (1,)), ((), ()))
TN = (((0,), (0,)), ((), ()))


def call(body, name, at, ins, outs, scratch=(), flops=0, aliases=None, mib=4, after=()):
    specs = {"v": pl.BlockSpec(memory_space=pltpu.VMEM), "h": pl.BlockSpec(memory_space=pl.ANY)}
    spaces = {"v": pltpu.VMEM, "h": pltpu.HBM}
    nbytes = sum(a.size * a.dtype.itemsize for a, _ in ins)
    skip = 1 + len(ins)
    ins = list(ins) + [(a, "v") for a in after]
    args = [pltpu.with_memory_space_constraint(a, spaces[w]) for a, w in ins]
    return pl.pallas_call(
        lambda *refs: body(*refs[:skip], *refs[skip + len(after) :]),
        out_shape=tuple(spaces[w](dims, dtype) for dims, dtype, w in outs),
        in_specs=[pl.BlockSpec(memory_space=pltpu.SMEM)] + [specs[w] for _, w in ins],
        out_specs=tuple(specs[w] for _, _, w in outs),
        scratch_shapes=list(scratch),
        input_output_aliases=aliases or {},
        compiler_params=pltpu.CompilerParams(vmem_limit_bytes=mib * MIB),
        cost_estimate=pl.CostEstimate(flops=int(flops), bytes_accessed=int(nbytes), transcendentals=0),
        name=name,
    )(at, *args)


def at_block(i, size):
    return pl.ds(pl.multiple_of(i * size, size), size)


def dma(n):
    return pltpu.SemaphoreType.DMA((n,))


def cut_half(at, x, half, after=()):
    rows = x.shape[0]
    n = 4
    step = rows // n

    def body(at_ref, x_ref, o_ref, sems):
        copies = [
            pltpu.make_async_copy(
                x_ref.at[pl.ds(i * step, step), at_block(1 - at_ref[0], half)], o_ref.at[pl.ds(i * step, step), :], sems.at[i]
            )
            for i in range(n)
        ]
        for c in copies:
            c.start()
        for c in copies:
            c.wait()

    return call(body, "cut_half", at, [(x, "h")], [((rows, half), BF, "v")], [dma(n)], after=after)[0]


def put_half(at, part, out):
    rows, half = part.shape
    n = 4
    step = rows // n

    def body(at_ref, p_ref, i_ref, o_ref, sems):
        copies = [
            pltpu.make_async_copy(
                p_ref.at[pl.ds(i * step, step), :], o_ref.at[pl.ds(i * step, step), at_block(1 - at_ref[0], half)], sems.at[i]
            )
            for i in range(n)
        ]
        for c in copies:
            c.start()
        for c in copies:
            c.wait()

    return call(body, "put_half", at, [(part, "v"), (out, "h")], [(out.shape, BF, "h")], [dma(n)], aliases={2: 0}, mib=4)[0]


def project_own(at, x, v, after=()):
    rows, (half, rank) = x.shape[0], v.shape
    tk = min(1024, half)
    n = half // tk

    def body(at_ref, x_ref, v_ref, p_ref, xv_ref, vv_ref, acc, x_sem, v_sem):
        def x_copy(k):
            src = x_ref.at[:, pl.ds(pl.multiple_of(at_ref[0] * half + k * tk, tk), tk)]
            return pltpu.make_async_copy(src, xv_ref.at[:, at_block(k, tk)], x_sem.at[k])

        def v_copy(k):
            return pltpu.make_async_copy(v_ref.at[at_block(k, tk), :], vv_ref.at[at_block(k, tk), :], v_sem.at[k])

        for k in range(n):
            x_copy(k).start()
            v_copy(k).start()
        acc[...] = jnp.zeros_like(acc)

        @pl.loop(0, n)
        def _(k):
            x_copy(k).wait()
            v_copy(k).wait()
            acc[...] += jnp.dot(xv_ref[:, at_block(k, tk)], vv_ref[at_block(k, tk), :], preferred_element_type=F32)

        p_ref[...] = acc[...].astype(BF)

    return call(
        body,
        "project_own",
        at,
        [(x, "h"), (v, "h")],
        [((rows, rank), BF, "v"), ((rows, half), BF, "v"), ((half, rank), BF, "v")],
        [pltpu.VMEM((rows, rank), F32), dma(n), dma(n)],
        flops=2 * rows * half * rank,
        mib=5,
        after=after,
    )


def project_other(at, x_o, v):
    rows, (half, rank) = x_o.shape[0], v.shape
    tk = min(1024, half)

    def body(at_ref, x_ref, v_ref, p_ref):
        p_ref[...] = jnp.zeros_like(p_ref)

        @pl.loop(0, half // tk)
        def _(k):
            p_ref[...] += jnp.dot(x_ref[:, at_block(k, tk)], v_ref[at_block(k, tk), :], preferred_element_type=F32)

    return call(
        body, "project_other", at, [(x_o, "v"), (v, "v")], [((rows, rank), F32, "v")], flops=2 * rows * half * rank
    )[0]


def hidden(c, x):
    return (c.astype(F32) * x.astype(F32)).astype(BF)


def back_project(at, x, x_o, c, c_o, u, after=()):
    rows, (half, rank) = x.shape[0], u.shape
    tk = min(512, half)
    n = half // tk
    slots = min(4, n)

    def body(at_ref, x_ref, xo_ref, c_ref, co_ref, u_ref, own_ref, oth_ref, b_ref, cv_ref, uv, h, acc, c_sem, u_sem):
        def c_copy(k):
            src = c_ref.at[:, pl.ds(pl.multiple_of(at_ref[0] * half + k * tk, tk), tk)]
            return pltpu.make_async_copy(src, cv_ref.at[:, at_block(k, tk)], c_sem.at[k])

        def u_copy(k):
            slot = lax.rem(k, slots)
            return pltpu.make_async_copy(u_ref.at[at_block(k, tk), :], uv.at[slot], u_sem.at[slot])

        for k in range(n):
            c_copy(k).start()
            if k < slots:
                u_copy(k).start()
        acc[...] = jnp.zeros_like(acc)

        @pl.loop(0, n)
        def _(k):
            here = at_block(k, tk)
            c_copy(k).wait()
            h[:rows, :] = hidden(cv_ref[:, here], x_ref[:, here])
            h[rows:, :] = hidden(co_ref[:, here], xo_ref[:, here])
            b_ref[:, here] = jnp.sum(h[...].astype(F32), axis=0, keepdims=True)
            u_copy(k).wait()
            acc[...] += jnp.dot(h[...], uv[lax.rem(k, slots)], preferred_element_type=F32)

            @pl.when(k + slots < n)
            def _():
                u_copy(k + slots).start()

        own_ref[...] = acc[:rows, :].astype(BF)
        oth_ref[...] = acc[rows:, :]

    return call(
        body,
        "back_project",
        at,
        [(x, "v"), (x_o, "v"), (c, "h"), (c_o, "v"), (u, "h")],
        [((rows, rank), BF, "v"), ((rows, rank), F32, "v"), ((1, half), F32, "v"), ((rows, half), BF, "v")],
        [
            pltpu.VMEM((slots, tk, rank), BF),
            pltpu.VMEM((2 * rows, tk), BF),
            pltpu.VMEM((2 * rows, rank), F32),
            dma(n),
            dma(slots),
        ],
        flops=4 * rows * half * rank,
        mib=12,
        after=after,
    )


def factor_grad(at, name, ins, get, p, p_o, half):
    rows, rank = p.shape
    tw = min(512, half)
    n = half // tw
    m = len(ins)

    def body(at_ref, *refs):
        p_ref, po_ref, o_ref, stage, both, left, sems = refs[m:]
        both[:rows, :] = p_ref[...]
        both[rows:, :] = po_ref[...]

        def out(k, slot):
            return pltpu.make_async_copy(stage.at[slot], o_ref.at[at_block(k, tw), :], sems.at[slot])

        @pl.loop(0, n)
        def _(k):
            slot = lax.rem(k, 2)
            here = at_block(k, tw)
            own, oth = get([r[:, here] for r in refs[:m]])
            left[:rows, :] = own
            left[rows:, :] = oth

            @pl.when(k >= 2)
            def _():
                out(k, slot).wait()

            stage[slot] = lax.dot_general(left[...], both[...], TN, preferred_element_type=F32).astype(BF)
            out(k, slot).start()

        for k in range(max(0, n - 2), n):
            out(k, k % 2).wait()

    return call(
        body,
        name,
        at,
        [(a, "v") for a in ins] + [(p, "v"), (p_o, "v")],
        [((half, rank), BF, "h")],
        [pltpu.VMEM((2, tw, rank), BF), pltpu.VMEM((2 * rows, rank), BF), pltpu.VMEM((2 * rows, tw), BF), dma(2)],
        flops=4 * rows * half * rank,
        mib=8,
    )[0]


def input_grad(at, c, c_o, u, v, bias, p, p_o, g, g_o, width):
    rows, rank = p.shape
    half = u.shape[0]
    tw = min(512, half)
    n = half // tw
    slots = min(3, n)

    def body(
        at_ref, c_ref, co_ref, u_ref, v_ref, b_ref, p_ref, po_ref, g_ref, go_ref, own_ref, oth_ref, stage, uv, vv, pp, gg, sems, u_sem, v_sem
    ):
        def u_copy(k):
            slot = lax.rem(k, slots)
            return pltpu.make_async_copy(u_ref.at[at_block(k, tw), :], uv.at[slot], u_sem.at[slot])

        def v_copy(k):
            slot = lax.rem(k, slots)
            return pltpu.make_async_copy(v_ref.at[at_block(k, tw), :], vv.at[slot], v_sem.at[slot])

        for k in range(slots):
            u_copy(k).start()
            v_copy(k).start()
        pp[:rows, :] = p_ref[...]
        pp[rows:, :] = po_ref[...]
        gg[:rows, :] = g_ref[...]
        gg[rows:, :] = go_ref[...]

        def out(k, slot):
            there = pl.ds(pl.multiple_of(at_ref[0] * half + k * tw, tw), tw)
            return pltpu.make_async_copy(stage.at[slot], own_ref.at[:, there], sems.at[slot])

        @pl.loop(0, n)
        def _(k):
            slot = lax.rem(k, 2)
            here = at_block(k, tw)
            there = pl.ds(pl.multiple_of(at_ref[0] * half + k * tw, tw), tw)
            u_copy(k).wait()
            ex = lax.dot_general(pp[...], uv[lax.rem(k, slots)], NT, preferred_element_type=F32) + b_ref[:, there].astype(F32)
            v_copy(k).wait()
            bk = lax.dot_general(gg[...], vv[lax.rem(k, slots)], NT, preferred_element_type=F32)
            cf, cof = c_ref[:, here].astype(F32), co_ref[:, here].astype(F32)

            @pl.when(k >= 2)
            def _():
                out(k, slot).wait()

            stage[slot] = (cf * ex[:rows] + cf + bk[:rows]).astype(BF)
            oth_ref[:, here] = (cof * ex[rows:] + cof + bk[rows:]).astype(BF)
            out(k, slot).start()

            @pl.when(k + slots < n)
            def _():
                u_copy(k + slots).start()
                v_copy(k + slots).start()

        for k in range(max(0, n - 2), n):
            out(k, k % 2).wait()

    return call(
        body,
        "input_grad",
        at,
        [(a, "h" if a is u or a is v else "v") for a in (c, c_o, u, v, bias, p, p_o, g, g_o)],
        [((rows, width), BF, "h"), ((rows, half), BF, "v")],
        [
            pltpu.VMEM((2, rows, tw), BF),
            pltpu.VMEM((slots, tw, rank), BF),
            pltpu.VMEM((slots, tw, rank), BF),
            pltpu.VMEM((2 * rows, rank), BF),
            pltpu.VMEM((2 * rows, rank), BF),
            dma(2),
            dma(slots),
            dma(slots),
        ],
        flops=8 * rows * half * rank,
        mib=16,
    )


def plus(a, b):
    return (a.astype(F32) + b.astype(F32)).astype(BF)


def pair_pieces(at, a, b, n):
    rows, rank = a.shape
    each = rows // n

    def body(at_ref, a_ref, b_ref, o_ref):
        for j in range(n):
            here = slice(j * each, (j + 1) * each)
            o_ref[j] = plus(a_ref[here, :], b_ref[here, :])

    return call(body, "pair_pieces", at, [(a, "v"), (b, "v")], [((n, each, rank), BF, "v")], mib=4)[0]


def sum_spread(at, a):
    n = a.shape[0]

    def body(at_ref, a_ref, o_ref):
        total = a_ref[0].astype(F32)
        for j in range(1, n):
            total += a_ref[j].astype(F32)
        total = total.astype(BF)
        for j in range(n):
            o_ref[j] = total

    return call(body, "sum_spread", at, [(a, "v")], [(a.shape, BF, "v")], mib=4)[0]


def pair_halves(at, a, b):
    rows, rank = a.shape
    each = rows // 2

    def body(at_ref, a_ref, b_ref, keep_ref, send_ref):
        bit = at_ref[1] & 1
        for i, o_ref in ((bit, keep_ref), (1 - bit, send_ref)):
            here = at_block(i, each)
            o_ref[...] = plus(a_ref[here, :], b_ref[here, :])

    return call(body, "pair_halves", at, [(a, "v"), (b, "v")], [((each, rank), BF, "v")] * 2, mib=4)


def pieces_of(at, a, b, m):
    rows, rank = a.shape
    each = rows // m

    def body(at_ref, a_ref, b_ref, *outs):
        for d in range(m):
            here = at_block((at_ref[1] >> 1) ^ d, each)
            outs[d][...] = plus(a_ref[here, :], b_ref[here, :])

    return call(body, "pieces_of", at, [(a, "v"), (b, "v")], [((each, rank), BF, "v")] * m, mib=4)


def add_pieces(at, parts):
    def body(at_ref, *refs):
        total = refs[0][...].astype(F32)
        for r in refs[1:-1]:
            total += r[...].astype(F32)
        refs[-1][...] = total.astype(BF)

    return call(body, "add_pieces", at, [(a, "v") for a in parts], [(parts[0].shape, BF, "v")], mib=4)[0]


def join_pieces(at, parts, shift):
    n = len(parts)
    each, rank = parts[0].shape

    def body(at_ref, *refs):
        for d in range(n):
            refs[-1][at_block(((at_ref[1] >> shift) & (n - 1)) ^ d, each), :] = refs[d][...]

    return call(body, "join_pieces", at, [(a, "v") for a in parts], [((n * each, rank), BF, "v")], mib=4)[0]


def solution(mesh):
    n = mesh.shape["col"]
    swap = [(0, 1), (1, 0)]

    def trade(a):
        return lax.ppermute(a, "batch", swap)

    def to(a, d):
        return lax.ppermute(a, "col", [(i, i ^ d) for i in range(n)])

    def staged_sum(at, mine, theirs):
        m = n // 2
        keep, send = pair_halves(at, mine, theirs)
        parts = pieces_of(at, keep, to(send, 1), m)
        total = add_pieces(at, [parts[0]] + [to(parts[d], 2 * d) for d in range(1, m)])
        half = join_pieces(at, [total] + [to(total, 2 * d) for d in range(1, m)], 1)
        return join_pieces(at, [half, to(half, 1)], 0)

    def traded_sum(at, mine, theirs):
        def spread(a):
            return lax.all_to_all(a, "col", split_axis=0, concat_axis=0, tiled=True)

        return spread(sum_spread(at, spread(pair_pieces(at, mine, theirs, n)))).reshape(mine.shape)

    def plain_sum(mine, theirs):
        return lax.psum(mine.astype(F32) + theirs.astype(F32), "col").astype(BF)

    def local(x, c, u, v, bias):
        half, width = u.shape[0], x.shape[1]
        core = lax.axis_index("batch")
        at = jnp.stack([core, lax.axis_index("col")]).astype(jnp.int32)
        direct = x.shape[0] % (16 * n) == 0 and n & (n - 1) == 0 and n > 2
        x_s = cut_half(at, x, half)
        x_o = trade(x_s)
        c_s = cut_half(at, c, half, [x_s])
        c_o = trade(c_s)
        own, x_own, v_in = project_own(at, x, v, [c_s])
        theirs = trade(own)
        mine = project_other(at, x_o, v_in)
        p_o = staged_sum(at, mine, theirs) if direct else plain_sum(mine, theirs)
        p = trade(p_o)
        own_g, mine_g, b_sum, c_own = back_project(at, x_own, x_o, c, c_o, u, [mine])
        theirs_g = trade(own_g)
        g_o = traded_sum(at, mine_g, theirs_g) if direct else plain_sum(mine_g, theirs_g)
        g = trade(g_o)
        grad_u = factor_grad(
            at,
            "u_grad",
            [x_own, x_o, c_own, c_o],
            lambda t: (hidden(t[2], t[0]), hidden(t[3], t[1])),
            p,
            p_o,
            half,
        )
        out, out_o = input_grad(at, c_own, c_o, u, v, bias[None, :], p, p_o, g, g_o, width)
        back = trade(out_o)
        grad_v = factor_grad(at, "v_grad", [x_own, x_o], lambda t: (t[0], t[1]), g, g_o, half)
        return put_half(at, back, out), grad_u, grad_v, b_sum[0]

    return jax.shard_map(
        local,
        mesh=mesh,
        in_specs=(
            P(("group", "batch"), "col"),
            P(("group", "batch"), "col"),
            P(("col", "batch"), None),
            P(("col", "batch"), None),
            P("col"),
        ),
        out_specs=(
            P(("group", "batch"), "col"),
            P(("group", "col", "batch"), None),
            P(("group", "col", "batch"), None),
            P(("group", "col", "batch")),
        ),
        check_vma=False,
    )
```

time: 284 us -> 187 us (0.66)
  Pallas kernels: 0 us -> 111 us
  blocking collectives: 98.1 us -> 0 us
  matrix products: 96.5 us -> 0 us
  waiting for transfers between devices: 0.01 us -> 44.1 us
  local copies, waits for them, and re-layouts: 48.9 us -> 7.06 us
  other arithmetic: 16.2 us -> 0.08 us
    pallas_call x0 -> x16, Pallas kernels: none -> 111 us  [call(): pl.pallas_call(lambda *refs: body(*refs[:skip], *refs[skip + len(after):]...]
    psum x1 -> x0, blocking collectives: 98.1 us -> none  [first_sum(): return lax.psum(part_sum, ('col', 'batch'))]
    dot_general x6 -> x0, matrix products: 96.5 us -> none  [the longest x1 21 us: cross_back(): back = jnp.dot(gproj_bf, v_rows.T, preferred_element_type=jnp.float32)]
    ppermute x0 -> x15, waiting for transfers between devices: none -> 29.3 us  [the longest x8 25.7 us: to(): return lax.ppermute(a, 'col', [(i, i ^ d) for i in range(n)])]
    all_to_all x3 -> x0, local copies, waits for them, and re-layouts: 23.3 us -> none  [the longest x1 7.77 us: local(): lax.all_to_all(cotangent, 'batch', split_axis=1, concat_axis=0, tiled=True)]
    unnamed x7 -> x19, local copies, waits for them, and re-layouts: 25.6 us -> 7.03 us
    all_to_all x3 -> x2, waiting for transfers between devices: 0.01 us -> 14.8 us  [spread(): return lax.all_to_all(a, 'col', split_axis=0, concat_axis=0, tiled=True)]
    ppermute x0 -> x15, starting transfers between devices: none -> 13.3 us  [the longest x8 11.5 us: to(): return lax.ppermute(a, 'col', [(i, i ^ d) for i in range(n)])]
  transfers between devices with their start and end apart: 3 -> 17, of which waited for: 0 -> 11; matrix products, arithmetic and copies ran while one was open for 27% -> 0% of each run, Pallas kernels for 0% -> 29%
where the time goes in v2:
time: 187 us
  Pallas kernels  111 us (59%)
  waiting for transfers between devices  44.1 us (24%)
  starting transfers between devices  24.1 us (13%)
  local copies, waits for them, and re-layouts  7.06 us (4%)
    pallas_call x16, Pallas kernels, call(): pl.pallas_call(lambda *refs: body(*refs[:skip], *refs[skip + len(after):]...  111 us
    ppermute x8, waiting for transfers between devices, to(): return lax.ppermute(a, 'col', [(i, i ^ d) for i in range(n)])  25.7 us
    all_to_all x2, waiting for transfers between devices, spread(): return lax.all_to_all(a, 'col', split_axis=0, concat_axis=0, tiled=True)  14.8 us
    ppermute x8, starting transfers between devices, to(): return lax.ppermute(a, 'col', [(i, i ^ d) for i in range(n)])  11.5 us
    all_to_all x2, starting transfers between devices, spread(): return lax.all_to_all(a, 'col', split_axis=0, concat_axis=0, tiled=True)  10.8 us
    unnamed x19, local copies, waits for them, and re-layouts  7.03 us
  transfers between devices with their start and end apart: 17, of which 11 were waited for; matrix products, arithmetic and copies ran while one was open for 0% of the time, Pallas kernels for 29%

profile of v2, /device:TPU:0, one launch (start us, length us, event | category | flops | bytes accessed | tf_op | source)
XLA Modules:
  0.0 186.7 jit_solution(5317940233785232716)
XLA Ops:
  0.6 0.1 pad_add_fusion.refs_0_
  0.7 2.8 %cut_half.2.refs_2_ = bf16[256,8192]{1,0:T(8,128)(2,1)S(1)} custom-call(s32[2]{0:T(128)S(1)} %pad_add_fusion.refs_0_, bf16[256,16384]{1,0:T(8,128)(2,1)} %refs_1_.5), custom_call_target="tpu_custom_call" | custom-call | bytes 8388608 | tf_op jit(solution)/shard_map/cut_half/pallas_call | solution.py:21
  3.5 0.5 collective-permute-start
  4.0 2.8 %cut_half.3.refs_3_ = bf16[256,8192]{1,0:T(8,128)(2,1)S(1)} custom-call(s32[2]{0:T(128)S(1)} %pad_add_fusion.refs_0_, bf16[256,16384]{1,0:T(8,128)(2,1)} %refs_3_.2, bf16[256,8192]{1,0:T(8,128)(2,1)S(1)} %cut_half.2.refs_2_), custom_call_target="tpu_custom_call" | custom-call | bytes 8388608 | tf_op jit(solution)/shard_map/cut_half/pallas_call | solution.py:21
  6.7 0.1 collective-permute-start.1
  6.9 9.3 %project_own.1 = (bf16[256,1024]{1,0:T(8,128)(2,1)}, bf16[256,8192]{1,0:T(8,128)(2,1)S(1)}, bf16[8192,1024]{1,0:T(8,128)(2,1)S(1)}) custom-call(s32[2]{0:T(128)S(1)} %pad_add_fusion.refs_0_, bf16[256,16384]{1,0:T(8,128)(2,1)} %refs_1_.5, bf16[8192,1024]{1,0:T(8,128)(2,1)} %refs_4_.1, bf16[256,8192]{1,0:T(8,128)(2,1)S(1)} %cut_half.3.refs_3_), custom_call_target="tpu_custom_call" | custom-call | flops 4294967296 | bytes 25165824 | tf_op jit(solution)/shard_map/project_own/pallas_call | solution.py:21
  16.2 0.0 copy-start.2
  16.2 6.4 %project_other.1.refs_6_.refs_1_ = f32[256,1024]{1,0:T(8,128)S(1)} custom-call(s32[2]{0:T(128)S(1)} %pad_add_fusion.refs_0_, bf16[256,8192]{1,0:T(8,128)(2,1)S(1)} %collective-permute-done.refs_1_.refs_2_, bf16[8192,1024]{1,0:T(8,128)(2,1)S(1)} %get-tuple-element.20.refs_2_), custom_call_target="tpu_custom_call" | custom-call | flops 4294967296 | bytes 20971520 | tf_op jit(solution)/shard_map/project_other/pallas_call | solution.py:21
  22.7 20.2 %back_project.1 = (bf16[256,1024]{1,0:T(8,128)(2,1)S(1)}, f32[256,1024]{1,0:T(8,128)S(1)}, f32[1,8192]{1,0:T(1,128)S(1)}, bf16[256,8192]{1,0:T(8,128)(2,1)S(1)}) custom-call(s32[2]{0:T(128)S(1)} %pad_add_fusion.refs_0_, bf16[256,8192]{1,0:T(8,128)(2,1)S(1)} %get-tuple-element.19.refs_1_, bf16[256,8192]{1,0:T(8,128)(2,1)S(1)} %collective-permute-done.refs_1_.refs_2_, ...), custom_call_target="tpu_custom_call" | custom-call | flops 8589934592 | bytes 37748736 | tf_op jit(solution)/shard_map/back_project/pallas_call | solution.py:21
  42.9 2.0 %copy-done.6 = bf16[256,8192]{1,0:T(8,128)(2,1)} copy-done((bf16[256,8192]{1,0:T(8,128)(2,1)}, bf16[256,8192]{1,0:T(8,128)(2,1)S(1)}, u32[]{:S(2)}) %copy-start.6) | copy-done | bytes 4194328
  44.9 0.4 collective-permute-start.12
  45.3 1.5 collective-permute-done.12.refs_2_
  46.9 1.4 pair_pieces.1
  48.3 7.2 %all-to-all-start = ((bf16[8,32,1024]{2,1,0:T(8,128)(2,1)}), bf16[8,32,1024]{2,1,0:T(8,128)(2,1)S(1)}, u32[]{:S(2)}, u32[]{:S(2)}) async-start(bf16[8,32,1024]{2,1,0:T(8,128)(2,1)} %pair_pieces.1), calls=%async_computation | async-start | bytes 1048576 | tf_op jit(solution)/shard_map/all_to_all | solution.py:416
  55.5 14.8 %all-to-all-done.refs_1_ = bf16[8,32,1024]{2,1,0:T(8,128)(2,1)S(1)} async-done(((bf16[8,32,1024]{2,1,0:T(8,128)(2,1)}), bf16[8,32,1024]{2,1,0:T(8,128)(2,1)S(1)}, u32[]{:S(2)}, u32[]{:S(2)}) %all-to-all-start) | async-done | bytes 524320 | tf_op jit(solution)/shard_map/all_to_all | solution.py:416
  70.3 1.4 sum_spread.1
  71.7 3.6 %all-to-all-start.1 = ((bf16[8,32,1024]{2,1,0:T(8,128)(2,1)}), bf16[8,32,1024]{2,1,0:T(8,128)(2,1)S(1)}, u32[]{:S(2)}, u32[]{:S(2)}) async-start(bf16[8,32,1024]{2,1,0:T(8,128)(2,1)} %sum_spread.1), calls=%async_computation.1 | async-start | bytes 1048576 | tf_op jit(solution)/shard_map/all_to_all | solution.py:416
  75.3 0.7 pair_halves.1
  76.0 2.1 %collective-permute-start.3 = (bf16[128,1024]{1,0:T(8,128)(2,1)S(1)}, bf16[128,1024]{1,0:T(8,128)(2,1)S(1)}, u32[]{:S(2)}, u32[]{:S(2)}) collective-permute-start(bf16[128,1024]{1,0:T(8,128)(2,1)S(1)} %get-tuple-element.24), channel_id=1, source_target_pairs={{0,2},{2,0},{4,6},{6,4},{8,10},{10,8},{12,14},{14,12},{1,3},{3,1},... | collective-permute-start | bytes 786440 | tf_op jit(solution)/shard_map/ppermute | solution.py:404
  78.1 11.0 %collective-permute-done.3.refs_2_ = bf16[128,1024]{1,0:T(8,128)(2,1)S(1)} collective-permute-done((bf16[128,1024]{1,0:T(8,128)(2,1)S(1)}, bf16[128,1024]{1,0:T(8,128)(2,1)S(1)}, u32[]{:S(2)}, u32[]{:S(2)}) %collective-permute-start.3) | collective-permute-done | bytes 262176 | tf_op jit(solution)/shard_map/ppermute | solution.py:404
  89.1 0.6 pieces_of.1
  89.7 1.2 collective-permute-start.4
  90.9 2.7 %collective-permute-start.5 = (bf16[32,1024]{1,0:T(8,128)(2,1)S(1)}, bf16[32,1024]{1,0:T(8,128)(2,1)S(1)}, u32[]{:S(2)}, u32[]{:S(2)}) collective-permute-start(bf16[32,1024]{1,0:T(8,128)(2,1)S(1)} %get-tuple-element.27), channel_id=1, source_target_pairs={{0,8},{2,10},{4,12},{6,14},{8,0},{10,2},{12,4},{14,6},{1,9},{3,11}... | collective-permute-start | bytes 196616 | tf_op jit(solution)/shard_map/ppermute | solution.py:404
  93.6 0.6 collective-permute-start.6
  94.1 0.5 collective-permute-done.4.refs_2_
  94.6 3.3 %collective-permute-done.5.refs_3_ = bf16[32,1024]{1,0:T(8,128)(2,1)S(1)} collective-permute-done((bf16[32,1024]{1,0:T(8,128)(2,1)S(1)}, bf16[32,1024]{1,0:T(8,128)(2,1)S(1)}, u32[]{:S(2)}, u32[]{:S(2)}) %collective-permute-start.5) | collective-permute-done | bytes 65568 | tf_op jit(solution)/shard_map/ppermute | solution.py:404
  98.0 1.7 collective-permute-done.6.refs_4_
  99.7 0.6 add_pieces.1.refs_1_
  100.2 1.6 collective-permute-start.9
  101.9 2.8 %collective-permute-start.7 = (bf16[32,1024]{1,0:T(8,128)(2,1)S(1)}, bf16[32,1024]{1,0:T(8,128)(2,1)S(1)}, u32[]{:S(2)}, u32[]{:S(2)}) collective-permute-start(bf16[32,1024]{1,0:T(8,128)(2,1)S(1)} %add_pieces.1.refs_1_), channel_id=1, source_target_pairs={{0,4},{2,6},{4,0},{6,2},{8,12},{10,14},{12,8},{14,10},{1,5},{3,7},... | collective-permute-start | bytes 196616 | tf_op jit(solution)/shard_map/ppermute | solution.py:404
  104.7 1.8 collective-permute-done.9.refs_4_
  106.5 1.4 collective-permute-done.8.refs_3_
  107.9 0.6 join_pieces.2.refs_1_
  108.4 0.5 collective-permute-start.10
  108.9 6.0 %collective-permute-done.10.refs_2_ = bf16[128,1024]{1,0:T(8,128)(2,1)S(1)} collective-permute-done((bf16[128,1024]{1,0:T(8,128)(2,1)S(1)}, bf16[128,1024]{1,0:T(8,128)(2,1)S(1)}, u32[]{:S(2)}, u32[]{:S(2)}) %collective-permute-start.10) | collective-permute-done | bytes 262176 | tf_op jit(solution)/shard_map/ppermute | solution.py:404
  114.9 0.6 join_pieces.3.refs_7_.refs_6_
  115.5 0.1 collective-permute-start.11
  115.6 0.5 collective-permute-start.13
  116.1 1.4 collective-permute-done.11.refs_6_.refs_5_
  117.4 0.7 collective-permute-done.13.refs_8_.refs_3_
  118.2 2.2 %copy-done.5 = bf16[256,8192]{1,0:T(8,128)(2,1)S(1)} copy-done((bf16[256,8192]{1,0:T(8,128)(2,1)S(1)}, bf16[256,8192]{1,0:T(8,128)(2,1)}, u32[]{:S(2)}) %copy-start.5) | copy-done | bytes 4194328
  120.4 2.2 %copy-done.7 = bf16[256,8192]{1,0:T(8,128)(2,1)S(1)} copy-done((bf16[256,8192]{1,0:T(8,128)(2,1)S(1)}, bf16[256,8192]{1,0:T(8,128)(2,1)}, u32[]{:S(2)}) %copy-start.7) | copy-done | bytes 4194328
  122.6 30.2 %input_grad.1 = (bf16[256,16384]{1,0:T(8,128)(2,1)}, bf16[256,8192]{1,0:T(8,128)(2,1)S(1)}) custom-call(s32[2]{0:T(128)S(1)} %pad_add_fusion.refs_0_, bf16[256,8192]{1,0:T(8,128)(2,1)S(1)} %copy-done.7, bf16[256,8192]{1,0:T(8,128)(2,1)S(1)} %copy-done.5, bf16[8192,1024]{1,0:T(8,128)(2,1)} %refs_3_.3, bf16[8192,1024]{1,0:T(8,128)(2,1)} %refs_4_.1, ...), custom_call_target="tpu_custom_call" | custom-call | flops 17179869184 | bytes 44072960 | tf_op jit(solution)/shard_map/input_grad/pallas_call | solution.py:21
  152.8 0.2 collective-permute-start.14
  153.0 0.6 copy.11
  153.6 15.4 %u_grad.1 = bf16[8192,1024]{1,0:T(8,128)(2,1)} custom-call(s32[2]{0:T(128)S(1)} %pad_add_fusion.refs_0_, bf16[256,8192]{1,0:T(8,128)(2,1)S(1)} %copy-done.3, bf16[256,8192]{1,0:T(8,128)(2,1)S(1)} %copy-done.1, bf16[256,8192]{1,0:T(8,128)(2,1)S(1)} %copy-done.7, bf16[256,8192]{1,0:T(8,128)(2,1)S(1)} %copy-done.5, ...), custom_call_target="tpu_custom_call" | custom-call | flops 8589934592 | bytes 17825792 | tf_op jit(solution)/shard_map/u_grad/pallas_call | solution.py:21
  169.0 15.1 %v_grad.1 = bf16[8192,1024]{1,0:T(8,128)(2,1)} custom-call(s32[2]{0:T(128)S(1)} %pad_add_fusion.refs_0_, bf16[256,8192]{1,0:T(8,128)(2,1)S(1)} %copy-done.3, bf16[256,8192]{1,0:T(8,128)(2,1)S(1)} %copy-done.1, bf16[256,1024]{1,0:T(8,128)(2,1)S(1)} %collective-permute-done.13.refs_8_.refs_3_, bf16[256,1024]{1,0:T(8,128)(2,1)S(1)} %bitcast.7), custom_call_target="tpu_custom_call" | custom-call | flops 8589934592 | bytes 9437184 | tf_op jit(solution)/shard_map/v_grad/pallas_call | solution.py:21
  184.1 2.6 %put_half.1 = bf16[256,16384]{1,0:T(8,128)(2,1)} custom-call(s32[2]{0:T(128)S(1)} %pad_add_fusion.refs_0_, bf16[256,8192]{1,0:T(8,128)(2,1)S(1)} %collective-permute-done.14.refs_1_, bf16[256,16384]{1,0:T(8,128)(2,1)} %get-tuple-element.32.refs_2_), custom_call_target="tpu_custom_call", output_to_operand_aliasing={{}: (2, {})} | custom-call | bytes 12582912 | tf_op jit(solution)/shard_map/put_half/pallas_call | solution.py:21
  (23 shorter events, 0.1 us)
Async XLA Ops:
  3.5 12.8 %collective-permute-start = (bf16[256,8192]{1,0:T(8,128)(2,1)S(1)}, bf16[256,8192]{1,0:T(8,128)(2,1)S(1)}, u32[]{:S(2)}, u32[]{:S(2)}) collective-permute-start(bf16[256,8192]{1,0:T(8,128)(2,1)S(1)} %cut_half.2.refs_2_), channel_id=1, source_target_pairs={{0,1},{1,0},{2,3},{3,2},{4,5},{5,4},{6,7},{7,6},{8,9},{9,8},{10,11... | collective-permute-start | bytes 12582920 | tf_op jit(solution)/shard_map/ppermute | solution.py:401
  6.7 15.9 %collective-permute-start.1 = (bf16[256,8192]{1,0:T(8,128)(2,1)S(1)}, bf16[256,8192]{1,0:T(8,128)(2,1)S(1)}, u32[]{:S(2)}, u32[]{:S(2)}) collective-permute-start(bf16[256,8192]{1,0:T(8,128)(2,1)S(1)} %cut_half.3.refs_3_), channel_id=1, source_target_pairs={{0,1},{1,0},{2,3},{3,2},{4,5},{5,4},{6,7},{7,6},{8,9},{9,8},{10,11... | collective-permute-start | bytes 12582920 | tf_op jit(solution)/shard_map/ppermute | solution.py:401
  16.2 6.5 %copy-start.2 = (bf16[256,8192]{1,0:T(8,128)(2,1)}, bf16[256,8192]{1,0:T(8,128)(2,1)S(1)}, u32[]{:S(2)}) copy-start(bf16[256,8192]{1,0:T(8,128)(2,1)S(1)} %get-tuple-element.19.refs_1_) | copy-start | bytes 12582916
  16.2 6.4 %copy-start = (bf16[256,8192]{1,0:T(8,128)(2,1)}, bf16[256,8192]{1,0:T(8,128)(2,1)S(1)}, u32[]{:S(2)}) copy-start(bf16[256,8192]{1,0:T(8,128)(2,1)S(1)} %collective-permute-done.refs_1_.refs_2_) | copy-start | bytes 12582916
  22.6 20.2 %copy-start.4 = (bf16[256,8192]{1,0:T(8,128)(2,1)}, bf16[256,8192]{1,0:T(8,128)(2,1)S(1)}, u32[]{:S(2)}) copy-start(bf16[256,8192]{1,0:T(8,128)(2,1)S(1)} %collective-permute-done.1.refs_4_.refs_2_) | copy-start | bytes 12582916
  42.9 2.0 %copy-start.6 = (bf16[256,8192]{1,0:T(8,128)(2,1)}, bf16[256,8192]{1,0:T(8,128)(2,1)S(1)}, u32[]{:S(2)}) copy-start(bf16[256,8192]{1,0:T(8,128)(2,1)S(1)} %get-tuple-element.21.refs_1_.refs_3_) | copy-start | bytes 12582916
  44.9 71.2 %copy-start.8 = (bf16[16384]{0:T(1024)(128)(2,1)S(1)}, bf16[16384]{0:T(1024)(128)(2,1)}, u32[]{:S(2)}) copy-start(bf16[16384]{0:T(1024)(128)(2,1)} %param.9) | copy-start | bytes 98308
  44.9 2.0 %collective-permute-start.12 = (bf16[256,1024]{1,0:T(8,128)(2,1)S(1)}, bf16[256,1024]{1,0:T(8,128)(2,1)S(1)}, u32[]{:S(2)}, u32[]{:S(2)}) collective-permute-start(bf16[256,1024]{1,0:T(8,128)(2,1)S(1)} %get-tuple-element.30), channel_id=1, source_target_pairs={{0,1},{1,0},{2,3},{3,2},{4,5},{5,4},{6,7},{7,6},{8,9},{9,8},{10,11... | collective-permute-start | bytes 1572872 | tf_op jit(solution)/shard_map/ppermute | solution.py:401
  48.3 22.0 %all-to-all-start = ((bf16[8,32,1024]{2,1,0:T(8,128)(2,1)}), bf16[8,32,1024]{2,1,0:T(8,128)(2,1)S(1)}, u32[]{:S(2)}, u32[]{:S(2)}) async-start(bf16[8,32,1024]{2,1,0:T(8,128)(2,1)} %pair_pieces.1), calls=%async_computation | async-start | bytes 1048576 | tf_op jit(solution)/shard_map/all_to_all | solution.py:416
  55.5 19.8 %collective-permute-start.2 = (bf16[256,1024]{1,0:T(8,128)(2,1)}, bf16[256,1024]{1,0:T(8,128)(2,1)S(1)}, u32[]{:S(2)}, u32[]{:S(2)}) collective-permute-start(bf16[256,1024]{1,0:T(8,128)(2,1)} %get-tuple-element.22), channel_id=1, source_target_pairs={{0,1},{1,0},{2,3},{3,2},{4,5},{5,4},{6,7},{7,6},{8,9},{9,8},{10,11... | collective-permute-start | bytes 1572872 | tf_op jit(solution)/shard_map/ppermute | solution.py:401
  71.7 43.9 %all-to-all-start.1 = ((bf16[8,32,1024]{2,1,0:T(8,128)(2,1)}), bf16[8,32,1024]{2,1,0:T(8,128)(2,1)S(1)}, u32[]{:S(2)}, u32[]{:S(2)}) async-start(bf16[8,32,1024]{2,1,0:T(8,128)(2,1)} %sum_spread.1), calls=%async_computation.1 | async-start | bytes 1048576 | tf_op jit(solution)/shard_map/all_to_all | solution.py:416
  76.0 13.1 %collective-permute-start.3 = (bf16[128,1024]{1,0:T(8,128)(2,1)S(1)}, bf16[128,1024]{1,0:T(8,128)(2,1)S(1)}, u32[]{:S(2)}, u32[]{:S(2)}) collective-permute-start(bf16[128,1024]{1,0:T(8,128)(2,1)S(1)} %get-tuple-element.24), channel_id=1, source_target_pairs={{0,2},{2,0},{4,6},{6,4},{8,10},{10,8},{12,14},{14,12},{1,3},{3,1},... | collective-permute-start | bytes 786440 | tf_op jit(solution)/shard_map/ppermute | solution.py:404
  89.7 5.0 %collective-permute-start.4 = (bf16[32,1024]{1,0:T(8,128)(2,1)S(1)}, bf16[32,1024]{1,0:T(8,128)(2,1)S(1)}, u32[]{:S(2)}, u32[]{:S(2)}) collective-permute-start(bf16[32,1024]{1,0:T(8,128)(2,1)S(1)} %get-tuple-element.26), channel_id=1, source_target_pairs={{0,4},{2,6},{4,0},{6,2},{8,12},{10,14},{12,8},{14,10},{1,5},{3,7},... | collective-permute-start | bytes 196616 | tf_op jit(solution)/shard_map/ppermute | solution.py:404
  90.9 7.1 %collective-permute-start.5 = (bf16[32,1024]{1,0:T(8,128)(2,1)S(1)}, bf16[32,1024]{1,0:T(8,128)(2,1)S(1)}, u32[]{:S(2)}, u32[]{:S(2)}) collective-permute-start(bf16[32,1024]{1,0:T(8,128)(2,1)S(1)} %get-tuple-element.27), channel_id=1, source_target_pairs={{0,8},{2,10},{4,12},{6,14},{8,0},{10,2},{12,4},{14,6},{1,9},{3,11}... | collective-permute-start | bytes 196616 | tf_op jit(solution)/shard_map/ppermute | solution.py:404
  93.6 6.1 %collective-permute-start.6 = (bf16[32,1024]{1,0:T(8,128)(2,1)S(1)}, bf16[32,1024]{1,0:T(8,128)(2,1)S(1)}, u32[]{:S(2)}, u32[]{:S(2)}) collective-permute-start(bf16[32,1024]{1,0:T(8,128)(2,1)S(1)} %get-tuple-element.28), channel_id=1, source_target_pairs={{0,12},{2,14},{4,8},{6,10},{8,4},{10,6},{12,0},{14,2},{1,13},{3,15... | collective-permute-start | bytes 196616 | tf_op jit(solution)/shard_map/ppermute | solution.py:404
  100.2 6.3 %collective-permute-start.9 = (bf16[32,1024]{1,0:T(8,128)(2,1)S(1)}, bf16[32,1024]{1,0:T(8,128)(2,1)S(1)}, u32[]{:S(2)}, u32[]{:S(2)}) collective-permute-start(bf16[32,1024]{1,0:T(8,128)(2,1)S(1)} %add_pieces.1.refs_1_), channel_id=1, source_target_pairs={{0,12},{2,14},{4,8},{6,10},{8,4},{10,6},{12,0},{14,2},{1,13},{3,15... | collective-permute-start | bytes 196616 | tf_op jit(solution)/shard_map/ppermute | solution.py:404
  101.9 6.0 %collective-permute-start.8 = (bf16[32,1024]{1,0:T(8,128)(2,1)S(1)}, bf16[32,1024]{1,0:T(8,128)(2,1)S(1)}, u32[]{:S(2)}, u32[]{:S(2)}) collective-permute-start(bf16[32,1024]{1,0:T(8,128)(2,1)S(1)} %add_pieces.1.refs_1_), channel_id=1, source_target_pairs={{0,8},{2,10},{4,12},{6,14},{8,0},{10,2},{12,4},{14,6},{1,9},{3,11}... | collective-permute-start | bytes 196616 | tf_op jit(solution)/shard_map/ppermute | solution.py:404
  101.9 6.0 %collective-permute-start.7 = (bf16[32,1024]{1,0:T(8,128)(2,1)S(1)}, bf16[32,1024]{1,0:T(8,128)(2,1)S(1)}, u32[]{:S(2)}, u32[]{:S(2)}) collective-permute-start(bf16[32,1024]{1,0:T(8,128)(2,1)S(1)} %add_pieces.1.refs_1_), channel_id=1, source_target_pairs={{0,4},{2,6},{4,0},{6,2},{8,12},{10,14},{12,8},{14,10},{1,5},{3,7},... | collective-permute-start | bytes 196616 | tf_op jit(solution)/shard_map/ppermute | solution.py:404
  108.4 6.4 %collective-permute-start.10 = (bf16[128,1024]{1,0:T(8,128)(2,1)S(1)}, bf16[128,1024]{1,0:T(8,128)(2,1)S(1)}, u32[]{:S(2)}, u32[]{:S(2)}) collective-permute-start(bf16[128,1024]{1,0:T(8,128)(2,1)S(1)} %join_pieces.2.refs_1_), channel_id=1, source_target_pairs={{0,2},{2,0},{4,6},{6,4},{8,10},{10,8},{12,14},{14,12},{1,3},{3,1},... | collective-permute-start | bytes 786440 | tf_op jit(solution)/shard_map/ppermute | solution.py:404
  115.5 2.0 %collective-permute-start.11 = (bf16[256,1024]{1,0:T(8,128)(2,1)S(1)}, bf16[256,1024]{1,0:T(8,128)(2,1)S(1)}, u32[]{:S(2)}, u32[]{:S(2)}) collective-permute-start(bf16[256,1024]{1,0:T(8,128)(2,1)S(1)} %join_pieces.3.refs_7_.refs_6_), channel_id=1, source_target_pairs={{0,1},{1,0},{2,3},{3,2},{4,5},{5,4},{6,7},{7,6},{8,9},{9,8},{10,11... | collective-permute-start | bytes 1572872 | tf_op jit(solution)/shard_map/ppermute | solution.py:401
  115.6 2.6 %collective-permute-start.13 = (bf16[256,1024]{1,0:T(8,128)(2,1)S(1)}, bf16[256,1024]{1,0:T(8,128)(2,1)S(1)}, u32[]{:S(2)}, u32[]{:S(2)}) collective-permute-start(bf16[256,1024]{1,0:T(8,128)(2,1)S(1)} %bitcast.5), channel_id=1, source_target_pairs={{0,1},{1,0},{2,3},{3,2},{4,5},{5,4},{6,7},{7,6},{8,9},{9,8},{10,11... | collective-permute-start | bytes 1572872 | tf_op jit(solution)/shard_map/ppermute | solution.py:401
  118.2 2.2 %copy-start.5 = (bf16[256,8192]{1,0:T(8,128)(2,1)S(1)}, bf16[256,8192]{1,0:T(8,128)(2,1)}, u32[]{:S(2)}) copy-start(bf16[256,8192]{1,0:T(8,128)(2,1)} %copy-done.4) | copy-start | bytes 12582916
  120.4 2.2 %copy-start.7 = (bf16[256,8192]{1,0:T(8,128)(2,1)S(1)}, bf16[256,8192]{1,0:T(8,128)(2,1)}, u32[]{:S(2)}) copy-start(bf16[256,8192]{1,0:T(8,128)(2,1)} %copy-done.6) | copy-start | bytes 12582916
  122.6 31.0 %copy-start.1 = (bf16[256,8192]{1,0:T(8,128)(2,1)S(1)}, bf16[256,8192]{1,0:T(8,128)(2,1)}, u32[]{:S(2)}) copy-start(bf16[256,8192]{1,0:T(8,128)(2,1)} %copy-done) | copy-start | bytes 12582916
  122.6 31.0 %copy-start.3 = (bf16[256,8192]{1,0:T(8,128)(2,1)S(1)}, bf16[256,8192]{1,0:T(8,128)(2,1)}, u32[]{:S(2)}) copy-start(bf16[256,8192]{1,0:T(8,128)(2,1)} %copy-done.2) | copy-start | bytes 12582916
  152.8 31.4 %collective-permute-start.14 = (bf16[256,8192]{1,0:T(8,128)(2,1)S(1)}, bf16[256,8192]{1,0:T(8,128)(2,1)S(1)}, u32[]{:S(2)}, u32[]{:S(2)}) collective-permute-start(bf16[256,8192]{1,0:T(8,128)(2,1)S(1)} %get-tuple-element.31), channel_id=1, source_target_pairs={{0,1},{1,0},{2,3},{3,2},{4,5},{5,4},{6,7},{7,6},{8,9},{9,8},{10,11... | collective-permute-start | bytes 12582920 | tf_op jit(solution)/shard_map/ppermute | solution.py:401

commit v3 on v0

v3 whole, which is shorter than its diff:
```python
import jax
import jax.numpy as jnp
from jax import lax
from jax.experimental import pallas as pl
from jax.experimental.pallas import tpu as pltpu
from jax.sharding import PartitionSpec as P

BF, F32 = jnp.bfloat16, jnp.float32
MIB = 1 << 20
NT = (((1,), (1,)), ((), ()))


def call(body, name, at, ins, outs, scratch=(), flops=0, aliases=None, mib=4, after=()):
    specs = {"v": pl.BlockSpec(memory_space=pltpu.VMEM), "h": pl.BlockSpec(memory_space=pl.ANY)}
    spaces = {"v": pltpu.VMEM, "h": pltpu.HBM}
    nbytes = sum(a.size * a.dtype.itemsize for a, _ in ins)
    skip = 1 + len(ins)
    ins = list(ins) + [a if isinstance(a, tuple) else (a, "v") for a in after]
    args = [pltpu.with_memory_space_constraint(a, spaces[w]) for a, w in ins]
    return pl.pallas_call(
        lambda *refs: body(*refs[:skip], *refs[skip + len(after) :]),
        out_shape=tuple(spaces[w](dims, dtype) for dims, dtype, w in outs),
        in_specs=[pl.BlockSpec(memory_space=pltpu.SMEM)] + [specs[w] for _, w in ins],
        out_specs=tuple(specs[w] for _, _, w in outs),
        scratch_shapes=list(scratch),
        input_output_aliases=aliases or {},
        compiler_params=pltpu.CompilerParams(vmem_limit_bytes=mib * MIB),
        cost_estimate=pl.CostEstimate(flops=int(flops), bytes_accessed=int(nbytes), transcendentals=0),
        name=name,
    )(at, *args)


def at_block(i, size):
    return pl.ds(pl.multiple_of(i * size, size), size)


def dma(n):
    return pltpu.SemaphoreType.DMA((n,))


def copy(src, dst, sem):
    return pltpu.make_async_copy(src, dst, sem)


def cut_half(at, x, half):
    rows = x.shape[0]
    n = 8
    step = rows // n

    def body(at_ref, x_ref, o_ref, sems):
        def cut(i):
            here = pl.ds(i * step, step)
            return copy(x_ref.at[here, at_block(1 - at_ref[0], half)], o_ref.at[here, :], sems.at[i])

        for i in range(n):
            cut(i).start()
        for i in range(n):
            cut(i).wait()

    return call(body, "cut_half", at, [(x, "h")], [((rows, half), BF, "v")], [dma(n)])[0]


VPARTS = 4


def project_own(at, x, v, c, after=()):
    rows, (half, rank) = x.shape[0], v.shape
    tk = half // VPARTS

    def body(at_ref, x_ref, v_ref, c_ref, p_ref, xv_ref, cs_ref, *refs):
        vv, (acc, x_sem, v_sem, c_sem) = refs[:VPARTS], refs[VPARTS:]

        def cut(ref, dst, core, k, sem):
            src = ref.at[:, pl.ds(pl.multiple_of(core * half + k * tk, tk), tk)]
            return copy(src, dst.at[:, pl.ds(k * tk, tk)], sem.at[k])

        def x_copy(k):
            return cut(x_ref, xv_ref, at_ref[0], k, x_sem)

        def c_copy(k):
            return cut(c_ref, cs_ref, 1 - at_ref[0], k, c_sem)

        def v_copy(k):
            return copy(v_ref.at[pl.ds(k * tk, tk), :], vv[k], v_sem.at[k])

        for k in range(VPARTS):
            x_copy(k).start()
            v_copy(k).start()
        for k in range(VPARTS):
            c_copy(k).start()
        for k in range(VPARTS):
            x_copy(k).wait()
            v_copy(k).wait()
            part = jnp.dot(xv_ref[:, pl.ds(k * tk, tk)], vv[k][...], preferred_element_type=F32)
            if k == VPARTS - 1:
                p_ref[...] = (acc[...] + part).astype(BF)
            else:
                acc[...] = acc[...] + part if k else part
        for k in range(VPARTS):
            c_copy(k).wait()

    return call(
        body,
        "project_own",
        at,
        [(x, "h"), (v, "h"), (c, "h")],
        [((rows, rank), BF, "v"), ((rows, half), BF, "v"), ((rows, half), BF, "v")] + [((tk, rank), BF, "v")] * VPARTS,
        [pltpu.VMEM((rows, rank), F32)] + [dma(VPARTS)] * 3,
        flops=2 * rows * half * rank,
        mib=6,
        after=after,
    )


def write_halves(at_ref, total, outs):
    if len(outs) == 1:
        outs[0][...] = total(slice(None))
        return
    each = outs[0].shape[0]
    bit = at_ref[1] & 1
    for i, o_ref in ((bit, outs[0]), (1 - bit, outs[1])):
        o_ref[...] = total(at_block(i, each)).astype(BF)


def halves_of(rows, rank, direct):
    return [((rows // 2, rank), BF, "v")] * 2 if direct else [((rows, rank), F32, "v")]


def project_other(at, x_o, vs, theirs, direct):
    rows = x_o.shape[0]
    tk, rank = vs[0].shape

    def body(at_ref, x_ref, t_ref, *refs):
        vv, outs, acc = refs[:VPARTS], refs[VPARTS:-1], refs[-1]
        for k in range(VPARTS):
            part = jnp.dot(x_ref[:, pl.ds(k * tk, tk)], vv[k][...], preferred_element_type=F32)
            acc[...] = part + (acc[...] if k else t_ref[...].astype(F32))
        write_halves(at_ref, lambda here: acc[here, :], outs)

    return call(
        body,
        "project_other",
        at,
        [(x_o, "v"), (theirs, "v")] + [(a, "v") for a in vs],
        halves_of(rows, rank, direct),
        [pltpu.VMEM((rows, rank), F32)],
        flops=2 * rows * tk * VPARTS * rank,
        mib=6,
    )


def hidden(c, x):
    return (c.astype(F32) * x.astype(F32)).astype(BF)


def back_project(at, s, x, x_o, c, c_o, u, so_far, after=()):
    rows, (half, rank) = x.shape[0], u.shape
    part = half // 2
    tk = min(512, part)
    n = part // tk
    slots = min(4, n)
    first = so_far is None

    def body(at_ref, x_ref, xo_ref, c_ref, co_ref, u_ref, *rest):
        if first:
            acc, b_ref, cv_ref, uv, h, c_sem, u_sem = rest
        else:
            so_ref, own_ref, oth_ref, b_ref, cv_ref, uv, h, acc, c_sem, u_sem = rest

        def c_copy(k):
            src = c_ref.at[:, pl.ds(pl.multiple_of(at_ref[0] * half + s * part + k * tk, tk), tk)]
            return copy(src, cv_ref.at[:, at_block(k, tk)], c_sem.at[k])

        def u_copy(k):
            slot = lax.rem(k, slots)
            return copy(u_ref.at[pl.ds(pl.multiple_of(s * part + k * tk, tk), tk), :], uv.at[slot], u_sem.at[slot])

        def make(k, slot):
            here = at_block(k, tk)
            there = pl.ds(pl.multiple_of(s * part + k * tk, tk), tk)
            own = hidden(cv_ref[:, here], x_ref[:, there])
            oth = hidden(co_ref[:, there], xo_ref[:, there])
            h[slot, :rows, :] = own
            h[slot, rows:, :] = oth
            b_ref[:, here] = jnp.sum(own.astype(F32), axis=0, keepdims=True) + jnp.sum(oth.astype(F32), axis=0, keepdims=True)

        def add(slot, k):
            acc[...] += jnp.dot(h[slot], uv[lax.rem(k, slots)], preferred_element_type=F32)

        for k in range(n):
            c_copy(k).start()
            if k < slots:
                u_copy(k).start()
        acc[...] = jnp.zeros_like(acc) if first else so_ref[...]
        c_copy(0).wait()
        make(0, 0)

        @pl.loop(0, n - 1)
        def _(k):
            c_copy(k + 1).wait()
            u_copy(k).wait()
            make(k + 1, lax.rem(k + 1, 2))
            add(lax.rem(k, 2), k)

            @pl.when(k + slots < n)
            def _():
                u_copy(k + slots).start()

        u_copy(n - 1).wait()
        add((n - 1) % 2, n - 1)
        if not first:
            own_ref[...] = acc[:rows, :].astype(BF)
            oth_ref[...] = acc[rows:, :]

    ends = [((1, part), F32, "v"), ((rows, part), BF, "v")]
    whole = pltpu.VMEM((2 * rows, rank), F32)
    return call(
        body,
        "back_project",
        at,
        [(x, "v"), (x_o, "v"), (c, "h"), (c_o, "v"), (u, "h")] + ([] if first else [(so_far, "v")]),
        ([((2 * rows, rank), F32, "v")] if first else [((rows, rank), BF, "v"), ((rows, rank), F32, "v")]) + ends,
        [pltpu.VMEM((slots, tk, rank), BF), pltpu.VMEM((2, 2 * rows, tk), BF)]
        + ([] if first else [whole])
        + [dma(n), dma(slots)],
        flops=2 * rows * half * rank,
        mib=12,
        after=after,
    )


def turn_x(at, x, x_o, after=()):
    rows, half = x.shape
    tw = min(512, half)

    def body(at_ref, x_ref, xo_ref, o_ref):
        @pl.loop(0, half // tw)
        def _(k):
            here = at_block(k, tw)
            o_ref[here, :rows] = x_ref[:, here].T
            o_ref[here, rows:] = xo_ref[:, here].T

    return call(body, "turn_x", at, [(x, "v"), (x_o, "v")], [((half, 2 * rows), BF, "v")], mib=6, after=after)[0]


def turn_hidden(at, x, x_o, cs, c_o, after=()):
    rows, half = x.shape
    part = half // 2
    tw = min(512, part)

    def body(at_ref, x_ref, xo_ref, c0_ref, c1_ref, co_ref, o_ref):
        for s, c_ref in enumerate((c0_ref, c1_ref)):

            @pl.loop(0, part // tw)
            def _(k):
                here = at_block(k, tw)
                there = pl.ds(pl.multiple_of(s * part + k * tw, tw), tw)
                o_ref[there, :rows] = hidden(c_ref[:, here], x_ref[:, there]).T
                o_ref[there, rows:] = hidden(co_ref[:, there], xo_ref[:, there]).T

    return call(
        body,
        "turn_hidden",
        at,
        [(a, "v") for a in (x, x_o, *cs, c_o)],
        [((half, 2 * rows), BF, "v")],
        mib=6,
        after=after,
    )[0]


def fill(at_ref, both, refs):
    if len(refs) == 2:
        rows = refs[0].shape[0]
        both[:rows, :] = refs[0][...]
        both[rows:, :] = refs[1][...]
        return
    each = refs[0].shape[0]
    bit = at_ref[1] & 1
    for i, (keep, other) in enumerate((refs[:2], refs[2:])):
        both[at_block(2 * i + bit, each), :] = keep[...]
        both[at_block(2 * i + 1 - bit, each), :] = other[...]


def factor_grad(at, name, s, turned, p, so_far, placed=None, after=()):
    half, rows2 = turned.shape
    rank = p[0].shape[1]
    part = half // 2
    tw = min(1024, part)
    n = part // tw
    np_ = len(p)
    recv, full = placed or ((), None)
    nr = len(recv)
    ins = [(turned, "v")] + [(a, "v") for a in p]
    aliases = {}
    if so_far is not None:
        aliases[1 + len(ins)] = 0
        ins.append((so_far, "h"))
    if placed:
        ins += [(a, "v") for a in recv]
        aliases[1 + len(ins)] = 1
        ins.append((full, "h"))

    def body(at_ref, t_ref, *refs):
        p_refs, refs = refs[:np_], refs[np_ + (so_far is not None) :]
        r_refs, refs = refs[:nr], refs[nr + (nr > 0) :]
        o_ref, refs = refs[0], refs[1:]
        if nr:
            f_ref, refs = refs[0], refs[1:]
        stage, both, sems, put_sem = refs

        def put(i):
            w = recv[i].shape[1]
            there = pl.ds(pl.multiple_of((1 - at_ref[0]) * half + i * w, w), w)
            return copy(r_refs[i], f_ref.at[:, there], put_sem.at[i])

        def out(k, slot):
            there = pl.ds(pl.multiple_of(s * part + k * tw, tw), tw)
            return copy(stage.at[slot], o_ref.at[there, :], sems.at[slot])

        for i in range(nr):
            put(i).start()
        fill(at_ref, both, p_refs)

        @pl.loop(0, n)
        def _(k):
            slot = lax.rem(k, 2)

            @pl.when(k >= 2)
            def _():
                out(k, slot).wait()

            left = t_ref[pl.ds(pl.multiple_of(s * part + k * tw, tw), tw), :]
            stage[slot] = jnp.dot(left, both[...], preferred_element_type=F32).astype(BF)
            out(k, slot).start()

        for k in range(max(0, n - 2), n):
            out(k, k % 2).wait()
        for i in range(nr):
            put(i).wait()

    outs = [((half, rank), BF, "h")] + ([(full.shape, BF, "h")] if placed else [])
    return call(
        body,
        name,
        at,
        ins,
        outs,
        [pltpu.VMEM((2, tw, rank), BF), pltpu.VMEM((rows2, rank), BF), dma(2), dma(max(1, nr))],
        flops=rows2 * half * rank,
        aliases=aliases,
        mib=12,
        after=after,
    )


def expand(at, s, u, p, after=()):
    half, rank = u.shape
    rows2 = sum(a.shape[0] for a in p)
    part = half // 2
    tw = min(1024, part)
    n = part // tw
    slots = min(3, n)

    def body(at_ref, u_ref, *refs):
        o_ref, uv, both, u_sem = refs[len(p) :]

        def u_copy(k):
            slot = lax.rem(k, slots)
            return copy(u_ref.at[pl.ds(pl.multiple_of(s * part + k * tw, tw), tw), :], uv.at[slot], u_sem.at[slot])

        for k in range(slots):
            u_copy(k).start()
        fill(at_ref, both, refs[: len(p)])

        @pl.loop(0, n)
        def _(k):
            u_copy(k).wait()
            o_ref[:, at_block(k, tw)] = lax.dot_general(both[...], uv[lax.rem(k, slots)], NT, preferred_element_type=F32)

            @pl.when(k + slots < n)
            def _():
                u_copy(k + slots).start()

    return call(
        body,
        "expand",
        at,
        [(u, "h")] + [(a, "v") for a in p],
        [((rows2, part), F32, "v")],
        [pltpu.VMEM((slots, tw, rank), BF), pltpu.VMEM((rows2, rank), BF), dma(slots)],
        flops=rows2 * half * rank,
        mib=10,
        after=after,
    )[0]


def input_grad(at, s, c, c_o, ex, v, bias, g, so_far, width, after=()):
    rows, half = c_o.shape
    rank = v.shape[1]
    part = half // 2
    tw = min(512, part)
    n = part // tw
    slots = min(4, n)
    ng = len(g)

    def body(at_ref, c_ref, co_ref, ex_ref, v_ref, b_ref, *refs):
        g_refs, refs = refs[:ng], refs[ng + (so_far is not None) :]
        own_ref, oth_ref, stage, vv, bk, both, sems, v_sem = refs

        def v_copy(k):
            slot = lax.rem(k, slots)
            return copy(v_ref.at[pl.ds(pl.multiple_of(s * part + k * tw, tw), tw), :], vv.at[slot], v_sem.at[slot])

        def columns(k):
            return pl.ds(pl.multiple_of(at_ref[0] * half + s * part + k * tw, tw), tw)

        def out(k, slot):
            return copy(stage.at[slot], own_ref.at[:, columns(k)], sems.at[slot])

        def finish(k, slot):
            here = at_block(k, tw)
            there = pl.ds(pl.multiple_of(s * part + k * tw, tw), tw)
            b = b_ref[:, columns(k)].astype(F32)
            cf, cof = c_ref[:, here].astype(F32), co_ref[:, there].astype(F32)
            stage[slot] = (cf * (ex_ref[:rows, here] + b) + cf + bk[slot, :rows, :]).astype(BF)
            oth_ref[:, here] = (cof * (ex_ref[rows:, here] + b) + cof + bk[slot, rows:, :]).astype(BF)

        def product(k, slot):
            bk[slot] = lax.dot_general(both[...], vv[lax.rem(k, slots)], NT, preferred_element_type=F32)

        for k in range(slots):
            v_copy(k).start()
        fill(at_ref, both, g_refs)
        v_copy(0).wait()
        product(0, 0)

        @pl.loop(1, n)
        def _(k):
            now, last = lax.rem(k, 2), lax.rem(k + 1, 2)
            v_copy(k).wait()

            @pl.when(k >= 3)
            def _():
                out(k - 1, last).wait()

            finish(k - 1, last)
            product(k, now)
            out(k - 1, last).start()

            @pl.when(k - 1 + slots < n)
            def _():
                v_copy(k - 1 + slots).start()

        if n >= 3:
            out(n - 1, (n - 1) % 2).wait()
        finish(n - 1, (n - 1) % 2)
        out(n - 1, (n - 1) % 2).start()
        for k in range(max(0, n - 2), n):
            out(k, k % 2).wait()

    ins = [(c, "v"), (c_o, "v"), (ex, "v"), (v, "h"), (bias, "v")] + [(a, "v") for a in g]
    aliases = {}
    if so_far is not None:
        aliases = {1 + len(ins): 0}
        ins.append((so_far, "h"))
    return call(
        body,
        "input_grad",
        at,
        ins,
        [((rows, width), BF, "h"), ((rows, part), BF, "v")],
        [
            pltpu.VMEM((2, rows, tw), BF),
            pltpu.VMEM((slots, tw, rank), BF),
            pltpu.VMEM((2, 2 * rows, tw), F32),
            pltpu.VMEM((2 * rows, rank), BF),
            dma(2),
            dma(slots),
        ],
        flops=2 * rows * half * rank,
        aliases=aliases,
        mib=12,
        after=after,
    )


def plus(a, b):
    return a.astype(F32) + b.astype(F32)


def pair_halves(at, a, b, direct, after=()):
    rows, rank = a.shape

    def body(at_ref, a_ref, b_ref, *outs):
        write_halves(at_ref, lambda here: plus(a_ref[here, :], b_ref[here, :]), outs)

    return call(body, "pair_halves", at, [(a, "v"), (b, "v")], halves_of(rows, rank, direct), after=after)


def pieces_of(at, a, b, m, after=()):
    rows, rank = a.shape
    each = rows // m

    def body(at_ref, a_ref, b_ref, *outs):
        for d in range(m):
            here = at_block((at_ref[1] >> 1) ^ d, each)
            outs[d][...] = plus(a_ref[here, :], b_ref[here, :]).astype(BF)

    return call(body, "pieces_of", at, [(a, "v"), (b, "v")], [((each, rank), BF, "v")] * m, after=after)


def add_pieces(at, parts, after=()):
    def body(at_ref, *refs):
        total = refs[0][...].astype(F32)
        for r in refs[1:-1]:
            total += r[...].astype(F32)
        refs[-1][...] = total.astype(BF)

    return call(body, "add_pieces", at, [(a, "v") for a in parts], [(parts[0].shape, BF, "v")], after=after)[0]


def join_pieces(at, parts, after=()):
    m = len(parts)
    each, rank = parts[0].shape

    def body(at_ref, *refs):
        for d in range(m):
            refs[-1][at_block((at_ref[1] >> 1) ^ d, each), :] = refs[d][...]

    return call(body, "join_pieces", at, [(a, "v") for a in parts], [((m * each, rank), BF, "v")], after=after)[0]


def solution(mesh):
    n = mesh.shape["col"]
    m = n // 2
    swap = [(0, 1), (1, 0)]

    def trade(a):
        return lax.ppermute(a, "batch", swap)

    def to(a, d):
        return lax.ppermute(a, "col", [(i, i ^ d) for i in range(n)])

    def spread(parts):
        return [parts[0]] + [to(parts[d], 2 * d) for d in range(1, m)]

    def ends(half):
        other = to(half, 1)
        return [trade(half), trade(other), half, other]

    def local(x, c, u, v, bias):
        half, width = u.shape[0], x.shape[1]
        core = lax.axis_index("batch")
        at = jnp.stack([core, lax.axis_index("col")]).astype(jnp.int32)
        direct = x.shape[0] % (16 * n) == 0 and n & (n - 1) == 0 and n > 2

        def plain(total):
            total = lax.psum(total, "col").astype(BF)
            return [trade(total), total]

        x_s = cut_half(at, x, half)
        x_o = trade(x_s)
        own, x_own, c_s, *v_in = project_own(at, x, v, c, [x_s])
        theirs = trade(own)
        c_o = trade(c_s)
        sums = project_other(at, x_o, v_in, theirs, direct)
        acc, b0, c0 = back_project(at, 0, x_own, x_o, c, c_o, u, None, [sums[0]])
        if direct:
            parts = pieces_of(at, sums[0], to(sums[1], 1), m, [acc])
            own_g, mine_g, b1, c1 = back_project(at, 1, x_own, x_o, c, c_o, u, acc, [parts[0]])
            parts = spread(parts)
            theirs_g = trade(own_g)
            total = add_pieces(at, parts, [own_g])
            sums_g = pair_halves(at, mine_g, theirs_g, direct, [total])
            x_t = turn_x(at, x_own, x_o, [sums_g[0]])
            p = ends(join_pieces(at, spread([total] * m), [x_t]))
            parts_g = pieces_of(at, sums_g[0], to(sums_g[1], 1), m, [p[2]])
            h_t = turn_hidden(at, x_own, x_o, (c0, c1), c_o, [parts_g[0]])
            total_g = add_pieces(at, spread(parts_g), [h_t])
            (grad_u,) = factor_grad(at, "u_grad", 0, h_t, p, None, after=[total_g])
            (grad_u,) = factor_grad(at, "u_grad", 1, h_t, p, grad_u)
            half_g = join_pieces(at, spread([total_g] * m), [(grad_u, "h")])
            g = ends(half_g)
            ex0 = expand(at, 0, u, p, [half_g])
            ex1 = expand(at, 1, u, p, [ex0])
        else:
            own_g, mine_g, b1, c1 = back_project(at, 1, x_own, x_o, c, c_o, u, acc)
            (sums_g,) = pair_halves(at, mine_g, trade(own_g), direct)
            p, g = plain(sums[0]), plain(sums_g)
            x_t = turn_x(at, x_own, x_o)
            h_t = turn_hidden(at, x_own, x_o, (c0, c1), c_o)
            (grad_u,) = factor_grad(at, "u_grad", 0, h_t, p, None)
            (grad_u,) = factor_grad(at, "u_grad", 1, h_t, p, grad_u)
            ex0, ex1 = expand(at, 0, u, p), expand(at, 1, u, p)
        bias = bias[None, :]
        out, oth0 = input_grad(at, 0, c0, c_o, ex0, v, bias, g, None, width, [ex1])
        out, oth1 = input_grad(at, 1, c1, c_o, ex1, v, bias, g, out, width)
        back = [trade(oth0), trade(oth1)]
        (grad_v,) = factor_grad(at, "v_grad", 0, x_t, g, None, after=[oth1])
        grad_v, out = factor_grad(at, "v_grad", 1, x_t, g, grad_v, (back, out))
        return out, grad_u, grad_v, jnp.concatenate([b0[0], b1[0]])

    return jax.shard_map(
        local,
        mesh=mesh,
        in_specs=(
            P(("group", "batch"), "col"),
            P(("group", "batch"), "col"),
            P(("col", "batch"), None),
            P(("col", "batch"), None),
            P("col"),
        ),
        out_specs=(
            P(("group", "batch"), "col"),
            P(("group", "col", "batch"), None),
            P(("group", "col", "batch"), None),
            P(("group", "col", "batch")),
        ),
        check_vma=False,
    )
```

time: 284 us -> 163 us (0.57)
  Pallas kernels: 0 us -> 111 us
  blocking collectives: 98.1 us -> 0 us
  matrix products: 96.5 us -> 0 us
  local copies, waits for them, and re-layouts: 48.9 us -> 0.04 us
  waiting for transfers between devices: 0.01 us -> 24.4 us
  other arithmetic: 16.2 us -> 0.69 us
  starting transfers between devices: 21.3 us -> 25.5 us
    pallas_call x0 -> x22, Pallas kernels: none -> 111 us  [call(): pl.pallas_call(lambda *refs: body(*refs[:skip], *refs[skip + len(after):]...]
    psum x1 -> x0, blocking collectives: 98.1 us -> none  [first_sum(): return lax.psum(part_sum, ('col', 'batch'))]
    dot_general x6 -> x0, matrix products: 96.5 us -> none  [the longest x1 21 us: cross_back(): back = jnp.dot(gproj_bf, v_rows.T, preferred_element_type=jnp.float32)]
    unnamed x7 -> x2, local copies, waits for them, and re-layouts: 25.6 us -> 0.01 us
    ppermute x0 -> x26, starting transfers between devices: none -> 25.5 us  [the longest x16 23.1 us: to(): return lax.ppermute(a, 'col', [(i, i ^ d) for i in range(n)])]
    ppermute x0 -> x26, waiting for transfers between devices: none -> 24.4 us  [the longest x16 17 us: to(): return lax.ppermute(a, 'col', [(i, i ^ d) for i in range(n)])]
    all_to_all x3 -> x0, local copies, waits for them, and re-layouts: 23.3 us -> none  [the longest x1 7.77 us: local(): lax.all_to_all(cotangent, 'batch', split_axis=1, concat_axis=0, tiled=True)]
    all_to_all x3 -> x0, starting transfers between devices: 21.3 us -> none  [the longest x1 7.41 us: local(): lax.all_to_all(grad_half, 'batch', split_axis=0, concat_axis=1, tiled=True)]
  transfers between devices with their start and end apart: 3 -> 26, of which waited for: 0 -> 6; matrix products, arithmetic and copies ran while one was open for 27% -> 0% of each run, Pallas kernels for 0% -> 43%
where the time goes in v3:
time: 163 us; the launch traced here: 162 us
  Pallas kernels  111 us (68%)
  starting transfers between devices  25.5 us (16%)
  waiting for transfers between devices  24.4 us (15%)
    pallas_call x22, Pallas kernels, call(): pl.pallas_call(lambda *refs: body(*refs[:skip], *refs[skip + len(after):]...  111 us
    ppermute x16, starting transfers between devices, to(): return lax.ppermute(a, 'col', [(i, i ^ d) for i in range(n)])  23.1 us
    ppermute x16, waiting for transfers between devices, to(): return lax.ppermute(a, 'col', [(i, i ^ d) for i in range(n)])  17 us
    ppermute x10, waiting for transfers between devices, trade(): return lax.ppermute(a, 'batch', swap)  7.42 us
  transfers between devices with their start and end apart: 26, of which 6 were waited for; matrix products, arithmetic and copies ran while one was open for 0% of the time, Pallas kernels for 43%

profile of v3, /device:TPU:0, one launch (start us, length us, event | category | flops | bytes accessed | tf_op | source)
XLA Modules:
  0.0 162.4 jit_solution(5067843287794153387)
XLA Ops:
  0.7 2.8 %cut_half.1.refs_4_ = bf16[256,8192]{1,0:T(8,128)(2,1)S(1)} custom-call(s32[2]{0:T(128)S(1)} %pad_add_fusion.refs_0_, bf16[256,16384]{1,0:T(8,128)(2,1)} %refs_1_.5), custom_call_target="tpu_custom_call" | custom-call | bytes 8388608 | tf_op jit(solution)/shard_map/cut_half/pallas_call | solution.py:20
  3.5 0.5 collective-permute-start
  4.0 9.9 %project_own.1 = (bf16[256,1024]{1,0:T(8,128)(2,1)S(1)}, bf16[256,8192]{1,0:T(8,128)(2,1)S(1)}, bf16[256,8192]{1,0:T(8,128)(2,1)S(1)}, bf16[2048,1024]{1,0:T(8,1...) custom-call(s32[2]{0:T(128)S(1)} %pad_add_fusion.refs_0_, ...), custom_call_target="tpu_custom_call" | custom-call | flops 4294967296 | bytes 33554432 | tf_op jit(solution)/shard_map/project_own/pallas_call | solution.py:20
  13.9 0.1 collective-permute-start.1
  14.0 0.5 collective-permute-start.2
  14.5 7.4 %collective-permute-done.2.refs_2_ = bf16[256,1024]{1,0:T(8,128)(2,1)S(1)} collective-permute-done((bf16[256,1024]{1,0:T(8,128)(2,1)S(1)}, bf16[256,1024]{1,0:T(8,128)(2,1)S(1)}, u32[]{:S(2)}, u32[]{:S(2)}) %collective-permute-start.2) | collective-permute-done | bytes 524320 | tf_op jit(solution)/shard_map/ppermute | solution.py:540
  21.9 5.2 %project_other.1 = (bf16[128,1024]{1,0:T(8,128)(2,1)S(1)}, bf16[128,1024]{1,0:T(8,128)(2,1)S(1)}) custom-call(s32[2]{0:T(128)S(1)} %pad_add_fusion.refs_0_, bf16[256,8192]{1,0:T(8,128)(2,1)S(1)} %collective-permute-done.refs_1_.refs_2_, bf16[256,1024]{1,0:T(8,128)(2,1)S(1)} %collective-permute-done.2.refs_2_, ...), custom_call_target="tpu_custom_call" | custom-call | flops 4294967296 | bytes 21495808 | tf_op jit(solution)/shard_map/project_other/pallas_call | solution.py:20
  27.1 2.7 %collective-permute-start.3 = (bf16[128,1024]{1,0:T(8,128)(2,1)S(1)}, bf16[128,1024]{1,0:T(8,128)(2,1)S(1)}, u32[]{:S(2)}, u32[]{:S(2)}) collective-permute-start(bf16[128,1024]{1,0:T(8,128)(2,1)S(1)} %get-tuple-element.45), channel_id=1, source_target_pairs={{0,2},{2,0},{4,6},{6,4},{8,10},{10,8},{12,14},{14,12},{1,3},{3,1},... | collective-permute-start | bytes 786440 | tf_op jit(solution)/shard_map/ppermute | solution.py:543
  29.8 8.8 %back_project.2 = (f32[512,1024]{1,0:T(8,128)S(1)}, f32[1,4096]{1,0:T(1,128)S(1)}, bf16[256,4096]{1,0:T(8,128)(2,1)S(1)}) custom-call(s32[2]{0:T(128)S(1)} %pad_add_fusion.refs_0_, bf16[256,8192]{1,0:T(8,128)(2,1)S(1)} %get-tuple-element.36.refs_1_, bf16[256,8192]{1,0:T(8,128)(2,1)S(1)} %collective-permute-done.refs_1_.refs_2_, bf16[256,16384]{1,0:T(8,128)(2,1)} %refs_3_.5, ...), custom_call_target="tpu_custom_call" | custom-call | flops 4294967296 | bytes 37748736 | tf_op jit(solution)/shard_map/back_project/pallas_call | solution.py:20
  38.6 0.6 pieces_of.2
  39.2 8.4 %back_project.3 = (bf16[256,1024]{1,0:T(8,128)(2,1)S(1)}, f32[256,1024]{1,0:T(8,128)S(1)}, f32[1,4096]{1,0:T(1,128)S(1)}, bf16[256,4096]{1,0:T(8,128)(2,1)S(1)}) custom-call(s32[2]{0:T(128)S(1)} %pad_add_fusion.refs_0_, bf16[256,8192]{1,0:T(8,128)(2,1)S(1)} %get-tuple-element.36.refs_1_, bf16[256,8192]{1,0:T(8,128)(2,1)S(1)} %collective-permute-done.refs_1_.refs_2_, ...), custom_call_target="tpu_custom_call" | custom-call | flops 4294967296 | bytes 39845888 | tf_op jit(solution)/shard_map/back_project/pallas_call | solution.py:20
  47.6 0.1 collective-permute-start.4
  47.7 1.6 collective-permute-start.5
  49.3 2.6 %collective-permute-start.6 = (bf16[32,1024]{1,0:T(8,128)(2,1)S(1)}, bf16[32,1024]{1,0:T(8,128)(2,1)S(1)}, u32[]{:S(2)}, u32[]{:S(2)}) collective-permute-start(bf16[32,1024]{1,0:T(8,128)(2,1)S(1)} %get-tuple-element.50), channel_id=1, source_target_pairs={{0,8},{2,10},{4,12},{6,14},{8,0},{10,2},{12,4},{14,6},{1,9},{3,11}... | collective-permute-start | bytes 196616 | tf_op jit(solution)/shard_map/ppermute | solution.py:543
  51.9 0.2 collective-permute-start.7
  52.2 4.8 %collective-permute-done.6.refs_3_ = bf16[32,1024]{1,0:T(8,128)(2,1)S(1)} collective-permute-done((bf16[32,1024]{1,0:T(8,128)(2,1)S(1)}, bf16[32,1024]{1,0:T(8,128)(2,1)S(1)}, u32[]{:S(2)}, u32[]{:S(2)}) %collective-permute-start.6) | collective-permute-done | bytes 65568 | tf_op jit(solution)/shard_map/ppermute | solution.py:543
  57.0 1.0 collective-permute-done.7.refs_4_
  58.0 0.6 add_pieces.2.refs_3_.refs_1_
  58.6 2.4 %collective-permute-start.11 = (bf16[32,1024]{1,0:T(8,128)(2,1)S(1)}, bf16[32,1024]{1,0:T(8,128)(2,1)S(1)}, u32[]{:S(2)}, u32[]{:S(2)}) collective-permute-start(bf16[32,1024]{1,0:T(8,128)(2,1)S(1)} %add_pieces.2.refs_3_.refs_1_), channel_id=1, source_target_pairs={{0,12},{2,14},{4,8},{6,10},{8,4},{10,6},{12,0},{14,2},{1,13},{3,15... | collective-permute-start | bytes 196616 | tf_op jit(solution)/shard_map/ppermute | solution.py:543
  61.0 0.3 collective-permute-start.10
  61.4 1.7 %collective-permute-start.9 = (bf16[32,1024]{1,0:T(8,128)(2,1)S(1)}, bf16[32,1024]{1,0:T(8,128)(2,1)S(1)}, u32[]{:S(2)}, u32[]{:S(2)}) collective-permute-start(bf16[32,1024]{1,0:T(8,128)(2,1)S(1)} %add_pieces.2.refs_3_.refs_1_), channel_id=1, source_target_pairs={{0,4},{2,6},{4,0},{6,2},{8,12},{10,14},{12,8},{14,10},{1,5},{3,7},... | collective-permute-start | bytes 196616 | tf_op jit(solution)/shard_map/ppermute | solution.py:543
  63.1 0.6 pair_halves.1
  63.7 3.6 %turn_x.1.refs_5_.refs_1_ = bf16[8192,512]{1,0:T(8,128)(2,1)S(1)} custom-call(s32[2]{0:T(128)S(1)} %pad_add_fusion.refs_0_, bf16[256,8192]{1,0:T(8,128)(2,1)S(1)} %get-tuple-element.36.refs_1_, bf16[256,8192]{1,0:T(8,128)(2,1)S(1)} %collective-permute-done.refs_1_.refs_2_, bf16[128,1024]{1,0:T(8,128)(2,1)S(1)} %get-tuple-element.52.refs_3_.refs_1_), custom_call_target="tpu_custom_call" | custom-call | bytes 8388608 | tf_op jit(solution)/shard_map/turn_x/pallas_call | solution.py:20
  67.4 0.6 join_pieces.2.refs_3_.refs_4_
  67.9 0.6 collective-permute-start.19
  68.5 1.5 collective-permute-start.8
  70.0 7.2 %collective-permute-done.19.refs_5_ = bf16[128,1024]{1,0:T(8,128)(2,1)S(1)} collective-permute-done((bf16[128,1024]{1,0:T(8,128)(2,1)S(1)}, bf16[128,1024]{1,0:T(8,128)(2,1)S(1)}, u32[]{:S(2)}, u32[]{:S(2)}) %collective-permute-start.19) | collective-permute-done | bytes 262176 | tf_op jit(solution)/shard_map/ppermute | solution.py:543
  77.3 3.9 %collective-permute-done.8.refs_2_ = bf16[128,1024]{1,0:T(8,128)(2,1)S(1)} collective-permute-done((bf16[128,1024]{1,0:T(8,128)(2,1)S(1)}, bf16[128,1024]{1,0:T(8,128)(2,1)S(1)}, u32[]{:S(2)}, u32[]{:S(2)}) %collective-permute-start.8) | collective-permute-done | bytes 262176 | tf_op jit(solution)/shard_map/ppermute | solution.py:543
  81.1 0.6 pieces_of.3
  81.8 0.8 collective-permute-start.13
  82.6 3.6 %collective-permute-start.14 = (bf16[32,1024]{1,0:T(8,128)(2,1)S(1)}, bf16[32,1024]{1,0:T(8,128)(2,1)S(1)}, u32[]{:S(2)}, u32[]{:S(2)}) collective-permute-start(bf16[32,1024]{1,0:T(8,128)(2,1)S(1)} %get-tuple-element.57), channel_id=1, source_target_pairs={{0,12},{2,14},{4,8},{6,10},{8,4},{10,6},{12,0},{14,2},{1,13},{3,15... | collective-permute-start | bytes 196616 | tf_op jit(solution)/shard_map/ppermute | solution.py:543
  86.2 3.7 %turn_hidden.1.refs_5_.refs_1_ = bf16[8192,512]{1,0:T(8,128)(2,1)S(1)} custom-call(s32[2]{0:T(128)S(1)} %pad_add_fusion.refs_0_, bf16[256,8192]{1,0:T(8,128)(2,1)S(1)} %get-tuple-element.36.refs_1_, bf16[256,8192]{1,0:T(8,128)(2,1)S(1)} %collective-permute-done.refs_1_.refs_2_, bf16[256,4096]{1,0:T(8,128)(2,1)S(1)} %get-tuple-element.58.refs_3_.refs_1_, ...), custom_call_target="tpu_custom_call" | custom-call | bytes 16777216 | tf_op jit(solution)/shard_map/turn_hidden/pallas_call | solution.py:20
  90.0 0.6 add_pieces.3.refs_6_.refs_1_
  90.6 2.5 %collective-permute-start.17 = (bf16[32,1024]{1,0:T(8,128)(2,1)S(1)}, bf16[32,1024]{1,0:T(8,128)(2,1)S(1)}, u32[]{:S(2)}, u32[]{:S(2)}) collective-permute-start(bf16[32,1024]{1,0:T(8,128)(2,1)S(1)} %add_pieces.3.refs_6_.refs_1_), channel_id=1, source_target_pairs={{0,12},{2,14},{4,8},{6,10},{8,4},{10,6},{12,0},{14,2},{1,13},{3,15... | collective-permute-start | bytes 196616 | tf_op jit(solution)/shard_map/ppermute | solution.py:543
  93.0 2.0 %collective-permute-start.15 = (bf16[32,1024]{1,0:T(8,128)(2,1)S(1)}, bf16[32,1024]{1,0:T(8,128)(2,1)S(1)}, u32[]{:S(2)}, u32[]{:S(2)}) collective-permute-start(bf16[32,1024]{1,0:T(8,128)(2,1)S(1)} %add_pieces.3.refs_6_.refs_1_), channel_id=1, source_target_pairs={{0,4},{2,6},{4,0},{6,2},{8,12},{10,14},{12,8},{14,10},{1,5},{3,7},... | collective-permute-start | bytes 196616 | tf_op jit(solution)/shard_map/ppermute | solution.py:543
  95.0 7.1 %u_grad.2.refs_6_ = bf16[8192,1024]{1,0:T(8,128)(2,1)} custom-call(s32[2]{0:T(128)S(1)} %pad_add_fusion.refs_0_, bf16[8192,512]{1,0:T(8,128)(2,1)S(1)} %turn_hidden.1.refs_5_.refs_1_, bf16[128,1024]{1,0:T(8,128)(2,1)S(1)} %collective-permute-done.18.refs_2_, bf16[128,1024]{1,0:T(8,128)(2,1)S(1)} %collective-permute-done.20.refs_3_, ...), custom_call_target="tpu_custom_call" | custom-call | flops 4294967296 | bytes 9437184 | tf_op jit(solution)/shard_map/u_grad/pallas_call | solution.py:20
  102.1 7.1 %u_grad.3.refs_5_ = bf16[8192,1024]{1,0:T(8,128)(2,1)} custom-call(s32[2]{0:T(128)S(1)} %pad_add_fusion.refs_0_, bf16[8192,512]{1,0:T(8,128)(2,1)S(1)} %turn_hidden.1.refs_5_.refs_1_, bf16[128,1024]{1,0:T(8,128)(2,1)S(1)} %collective-permute-done.18.refs_2_, bf16[128,1024]{1,0:T(8,128)(2,1)S(1)} %collective-permute-done.20.refs_3_, ...), custom_call_target="tpu_custom_call", output_to_operand_aliasing={{}: (6, {})} | custom-call | flops 4294967296 | bytes 26214400 | tf_op jit(solution)/shard_map/u_grad/pallas_call | solution.py:20
  109.2 0.6 join_pieces.3.refs_6_.refs_8_.refs_4_
  109.8 0.6 collective-permute-start.22
  110.4 7.3 %expand.2.refs_6_.refs_3_ = f32[512,4096]{1,0:T(8,128)S(1)} custom-call(s32[2]{0:T(128)S(1)} %pad_add_fusion.refs_0_, bf16[8192,1024]{1,0:T(8,128)(2,1)} %refs_1_.7, bf16[128,1024]{1,0:T(8,128)(2,1)S(1)} %collective-permute-done.18.refs_2_, bf16[128,1024]{1,0:T(8,128)(2,1)S(1)} %collective-permute-done.20.refs_3_, ...), custom_call_target="tpu_custom_call" | custom-call | flops 4294967296 | bytes 17825792 | tf_op jit(solution)/shard_map/expand/pallas_call | solution.py:20
  117.7 0.6 collective-permute-start.23
  118.3 7.3 %expand.3.refs_10_.refs_3_ = f32[512,4096]{1,0:T(8,128)S(1)} custom-call(s32[2]{0:T(128)S(1)} %pad_add_fusion.refs_0_, bf16[8192,1024]{1,0:T(8,128)(2,1)} %refs_1_.7, bf16[128,1024]{1,0:T(8,128)(2,1)S(1)} %collective-permute-done.18.refs_2_, bf16[128,1024]{1,0:T(8,128)(2,1)S(1)} %collective-permute-done.20.refs_3_, ...), custom_call_target="tpu_custom_call" | custom-call | flops 4294967296 | bytes 17825792 | tf_op jit(solution)/shard_map/expand/pallas_call | solution.py:20
  125.6 10.5 %input_grad.2 = (bf16[256,16384]{1,0:T(8,128)(2,1)}, bf16[256,4096]{1,0:T(8,128)(2,1)S(1)}) custom-call(s32[2]{0:T(128)S(1)} %pad_add_fusion.refs_0_, bf16[256,4096]{1,0:T(8,128)(2,1)S(1)} %get-tuple-element.58.refs_3_.refs_1_, bf16[256,8192]{1,0:T(8,128)(2,1)S(1)} %collective-permute-done.1.refs_4_.refs_5_.refs_2_, f32[512,4096]{1,0:T(8,128)S(1)} %expand.2.refs_6_.refs_3_, ...), custom_call_target="tpu_custom_call" | custom-call | flops 4294967296 | bytes 32538624 | tf_op jit(solution)/shard_map/input_grad/pallas_call | solution.py:20
  136.1 10.7 %input_grad.3 = (bf16[256,16384]{1,0:T(8,128)(2,1)}, bf16[256,4096]{1,0:T(8,128)(2,1)S(1)}) custom-call(s32[2]{0:T(128)S(1)} %pad_add_fusion.refs_0_, bf16[256,4096]{1,0:T(8,128)(2,1)S(1)} %get-tuple-element.59.refs_4_.refs_1_, bf16[256,8192]{1,0:T(8,128)(2,1)S(1)} %collective-permute-done.1.refs_4_.refs_5_.refs_2_, ...), custom_call_target="tpu_custom_call", output_to_operand_aliasing={{0}: (10, {})} | custom-call | flops 4294967296 | bytes 40927232 | tf_op jit(solution)/shard_map/input_grad/pallas_call | solution.py:20
  146.9 0.5 collective-permute-start.24
  147.4 0.6 pad_maximum_fusion
  148.0 7.1 %v_grad.2.refs_6_ = bf16[8192,1024]{1,0:T(8,128)(2,1)} custom-call(s32[2]{0:T(128)S(1)} %pad_add_fusion.refs_0_, bf16[8192,512]{1,0:T(8,128)(2,1)S(1)} %turn_x.1.refs_5_.refs_1_, bf16[128,1024]{1,0:T(8,128)(2,1)S(1)} %collective-permute-done.21.refs_6_.refs_2_, bf16[128,1024]{1,0:T(8,128)(2,1)S(1)} %collective-permute-done.23.refs_7_.refs_3_, ...), custom_call_target="tpu_custom_call" | custom-call | flops 4294967296 | bytes 9437184 | tf_op jit(solution)/shard_map/v_grad/pallas_call | solution.py:20
  155.1 7.1 %v_grad.3 = (bf16[8192,1024]{1,0:T(8,128)(2,1)}, bf16[256,16384]{1,0:T(8,128)(2,1)}) custom-call(s32[2]{0:T(128)S(1)} %pad_add_fusion.refs_0_, bf16[8192,512]{1,0:T(8,128)(2,1)S(1)} %turn_x.1.refs_5_.refs_1_, bf16[128,1024]{1,0:T(8,128)(2,1)S(1)} %collective-permute-done.21.refs_6_.refs_2_, ...), custom_call_target="tpu_custom_call", output_to_operand_aliasing={{0}: (6, {}), {1}: (9, {})} | custom-call | flops 4294967296 | bytes 38797312 | tf_op jit(solution)/shard_map/v_grad/pallas_call | solution.py:20
  (31 shorter events, 0.4 us)
Async XLA Ops:
  3.5 18.4 %collective-permute-start = (bf16[256,8192]{1,0:T(8,128)(2,1)S(1)}, bf16[256,8192]{1,0:T(8,128)(2,1)S(1)}, u32[]{:S(2)}, u32[]{:S(2)}) collective-permute-start(bf16[256,8192]{1,0:T(8,128)(2,1)S(1)} %cut_half.1.refs_4_), channel_id=1, source_target_pairs={{0,1},{1,0},{2,3},{3,2},{4,5},{5,4},{6,7},{7,6},{8,9},{9,8},{10,11... | collective-permute-start | bytes 12582920 | tf_op jit(solution)/shard_map/ppermute | solution.py:540
  13.9 15.9 %collective-permute-start.1 = (bf16[256,8192]{1,0:T(8,128)(2,1)S(1)}, bf16[256,8192]{1,0:T(8,128)(2,1)S(1)}, u32[]{:S(2)}, u32[]{:S(2)}) collective-permute-start(bf16[256,8192]{1,0:T(8,128)(2,1)S(1)} %get-tuple-element.37), channel_id=1, source_target_pairs={{0,1},{1,0},{2,3},{3,2},{4,5},{5,4},{6,7},{7,6},{8,9},{9,8},{10,11... | collective-permute-start | bytes 12582920 | tf_op jit(solution)/shard_map/ppermute | solution.py:540
  14.0 7.9 %collective-permute-start.2 = (bf16[256,1024]{1,0:T(8,128)(2,1)S(1)}, bf16[256,1024]{1,0:T(8,128)(2,1)S(1)}, u32[]{:S(2)}, u32[]{:S(2)}) collective-permute-start(bf16[256,1024]{1,0:T(8,128)(2,1)S(1)} %get-tuple-element.38), channel_id=1, source_target_pairs={{0,1},{1,0},{2,3},{3,2},{4,5},{5,4},{6,7},{7,6},{8,9},{9,8},{10,11... | collective-permute-start | bytes 1572872 | tf_op jit(solution)/shard_map/ppermute | solution.py:540
  27.1 11.5 %collective-permute-start.3 = (bf16[128,1024]{1,0:T(8,128)(2,1)S(1)}, bf16[128,1024]{1,0:T(8,128)(2,1)S(1)}, u32[]{:S(2)}, u32[]{:S(2)}) collective-permute-start(bf16[128,1024]{1,0:T(8,128)(2,1)S(1)} %get-tuple-element.45), channel_id=1, source_target_pairs={{0,2},{2,0},{4,6},{6,4},{8,10},{10,8},{12,14},{14,12},{1,3},{3,1},... | collective-permute-start | bytes 786440 | tf_op jit(solution)/shard_map/ppermute | solution.py:543
  47.6 15.5 %collective-permute-start.4 = (bf16[256,1024]{1,0:T(8,128)(2,1)S(1)}, bf16[256,1024]{1,0:T(8,128)(2,1)S(1)}, u32[]{:S(2)}, u32[]{:S(2)}) collective-permute-start(bf16[256,1024]{1,0:T(8,128)(2,1)S(1)} %get-tuple-element.48.refs_5_), channel_id=1, source_target_pairs={{0,1},{1,0},{2,3},{3,2},{4,5},{5,4},{6,7},{7,6},{8,9},{9,8},{10,11... | collective-permute-start | bytes 1572872 | tf_op jit(solution)/shard_map/ppermute | solution.py:540
  47.7 4.4 %collective-permute-start.5 = (bf16[32,1024]{1,0:T(8,128)(2,1)S(1)}, bf16[32,1024]{1,0:T(8,128)(2,1)S(1)}, u32[]{:S(2)}, u32[]{:S(2)}) collective-permute-start(bf16[32,1024]{1,0:T(8,128)(2,1)S(1)} %get-tuple-element.49), channel_id=1, source_target_pairs={{0,4},{2,6},{4,0},{6,2},{8,12},{10,14},{12,8},{14,10},{1,5},{3,7},... | collective-permute-start | bytes 196616 | tf_op jit(solution)/shard_map/ppermute | solution.py:543
  49.3 7.7 %collective-permute-start.6 = (bf16[32,1024]{1,0:T(8,128)(2,1)S(1)}, bf16[32,1024]{1,0:T(8,128)(2,1)S(1)}, u32[]{:S(2)}, u32[]{:S(2)}) collective-permute-start(bf16[32,1024]{1,0:T(8,128)(2,1)S(1)} %get-tuple-element.50), channel_id=1, source_target_pairs={{0,8},{2,10},{4,12},{6,14},{8,0},{10,2},{12,4},{14,6},{1,9},{3,11}... | collective-permute-start | bytes 196616 | tf_op jit(solution)/shard_map/ppermute | solution.py:543
  51.9 6.1 %collective-permute-start.7 = (bf16[32,1024]{1,0:T(8,128)(2,1)S(1)}, bf16[32,1024]{1,0:T(8,128)(2,1)S(1)}, u32[]{:S(2)}, u32[]{:S(2)}) collective-permute-start(bf16[32,1024]{1,0:T(8,128)(2,1)S(1)} %get-tuple-element.51), channel_id=1, source_target_pairs={{0,12},{2,14},{4,8},{6,10},{8,4},{10,6},{12,0},{14,2},{1,13},{3,15... | collective-permute-start | bytes 196616 | tf_op jit(solution)/shard_map/ppermute | solution.py:543
  58.6 8.7 %collective-permute-start.11 = (bf16[32,1024]{1,0:T(8,128)(2,1)S(1)}, bf16[32,1024]{1,0:T(8,128)(2,1)S(1)}, u32[]{:S(2)}, u32[]{:S(2)}) collective-permute-start(bf16[32,1024]{1,0:T(8,128)(2,1)S(1)} %add_pieces.2.refs_3_.refs_1_), channel_id=1, source_target_pairs={{0,12},{2,14},{4,8},{6,10},{8,4},{10,6},{12,0},{14,2},{1,13},{3,15... | collective-permute-start | bytes 196616 | tf_op jit(solution)/shard_map/ppermute | solution.py:543
  61.0 6.3 %collective-permute-start.10 = (bf16[32,1024]{1,0:T(8,128)(2,1)S(1)}, bf16[32,1024]{1,0:T(8,128)(2,1)S(1)}, u32[]{:S(2)}, u32[]{:S(2)}) collective-permute-start(bf16[32,1024]{1,0:T(8,128)(2,1)S(1)} %add_pieces.2.refs_3_.refs_1_), channel_id=1, source_target_pairs={{0,8},{2,10},{4,12},{6,14},{8,0},{10,2},{12,4},{14,6},{1,9},{3,11}... | collective-permute-start | bytes 196616 | tf_op jit(solution)/shard_map/ppermute | solution.py:543
  61.4 6.0 %collective-permute-start.9 = (bf16[32,1024]{1,0:T(8,128)(2,1)S(1)}, bf16[32,1024]{1,0:T(8,128)(2,1)S(1)}, u32[]{:S(2)}, u32[]{:S(2)}) collective-permute-start(bf16[32,1024]{1,0:T(8,128)(2,1)S(1)} %add_pieces.2.refs_3_.refs_1_), channel_id=1, source_target_pairs={{0,4},{2,6},{4,0},{6,2},{8,12},{10,14},{12,8},{14,10},{1,5},{3,7},... | collective-permute-start | bytes 196616 | tf_op jit(solution)/shard_map/ppermute | solution.py:543
  67.3 18.9 %copy-start = (bf16[16384]{0:T(1024)(128)(2,1)S(1)}, bf16[16384]{0:T(1024)(128)(2,1)}, u32[]{:S(2)}) copy-start(bf16[16384]{0:T(1024)(128)(2,1)} %param.9) | copy-start | bytes 98308
  67.9 9.3 %collective-permute-start.19 = (bf16[128,1024]{1,0:T(8,128)(2,1)S(1)}, bf16[128,1024]{1,0:T(8,128)(2,1)S(1)}, u32[]{:S(2)}, u32[]{:S(2)}) collective-permute-start(bf16[128,1024]{1,0:T(8,128)(2,1)S(1)} %join_pieces.2.refs_3_.refs_4_), channel_id=1, source_target_pairs={{0,2},{2,0},{4,6},{6,4},{8,10},{10,8},{12,14},{14,12},{1,3},{3,1},... | collective-permute-start | bytes 786440 | tf_op jit(solution)/shard_map/ppermute | solution.py:543
  68.5 12.6 %collective-permute-start.8 = (bf16[128,1024]{1,0:T(8,128)(2,1)S(1)}, bf16[128,1024]{1,0:T(8,128)(2,1)S(1)}, u32[]{:S(2)}, u32[]{:S(2)}) collective-permute-start(bf16[128,1024]{1,0:T(8,128)(2,1)S(1)} %get-tuple-element.53), channel_id=1, source_target_pairs={{0,2},{2,0},{4,6},{6,4},{8,10},{10,8},{12,14},{14,12},{1,3},{3,1},... | collective-permute-start | bytes 786440 | tf_op jit(solution)/shard_map/ppermute | solution.py:543
  70.0 25.0 %collective-permute-start.18 = (bf16[128,1024]{1,0:T(8,128)(2,1)S(1)}, bf16[128,1024]{1,0:T(8,128)(2,1)S(1)}, u32[]{:S(2)}, u32[]{:S(2)}) collective-permute-start(bf16[128,1024]{1,0:T(8,128)(2,1)S(1)} %join_pieces.2.refs_3_.refs_4_), channel_id=1, source_target_pairs={{0,1},{1,0},{2,3},{3,2},{4,5},{5,4},{6,7},{7,6},{8,9},{9,8},{10,11... | collective-permute-start | bytes 786440 | tf_op jit(solution)/shard_map/ppermute | solution.py:540
  77.2 17.8 %collective-permute-start.20 = (bf16[128,1024]{1,0:T(8,128)(2,1)S(1)}, bf16[128,1024]{1,0:T(8,128)(2,1)S(1)}, u32[]{:S(2)}, u32[]{:S(2)}) collective-permute-start(bf16[128,1024]{1,0:T(8,128)(2,1)S(1)} %collective-permute-done.19.refs_5_), channel_id=1, source_target_pairs={{0,1},{1,0},{2,3},{3,2},{4,5},{5,4},{6,7},{7,6},{8,9},{9,8},{10,11... | collective-permute-start | bytes 786440 | tf_op jit(solution)/shard_map/ppermute | solution.py:540
  81.7 8.2 %collective-permute-start.12 = (bf16[32,1024]{1,0:T(8,128)(2,1)S(1)}, bf16[32,1024]{1,0:T(8,128)(2,1)S(1)}, u32[]{:S(2)}, u32[]{:S(2)}) collective-permute-start(bf16[32,1024]{1,0:T(8,128)(2,1)S(1)} %get-tuple-element.55), channel_id=1, source_target_pairs={{0,4},{2,6},{4,0},{6,2},{8,12},{10,14},{12,8},{14,10},{1,5},{3,7},... | collective-permute-start | bytes 196616 | tf_op jit(solution)/shard_map/ppermute | solution.py:543
  81.8 8.1 %collective-permute-start.13 = (bf16[32,1024]{1,0:T(8,128)(2,1)S(1)}, bf16[32,1024]{1,0:T(8,128)(2,1)S(1)}, u32[]{:S(2)}, u32[]{:S(2)}) collective-permute-start(bf16[32,1024]{1,0:T(8,128)(2,1)S(1)} %get-tuple-element.56), channel_id=1, source_target_pairs={{0,8},{2,10},{4,12},{6,14},{8,0},{10,2},{12,4},{14,6},{1,9},{3,11}... | collective-permute-start | bytes 196616 | tf_op jit(solution)/shard_map/ppermute | solution.py:543
  82.6 7.3 %collective-permute-start.14 = (bf16[32,1024]{1,0:T(8,128)(2,1)S(1)}, bf16[32,1024]{1,0:T(8,128)(2,1)S(1)}, u32[]{:S(2)}, u32[]{:S(2)}) collective-permute-start(bf16[32,1024]{1,0:T(8,128)(2,1)S(1)} %get-tuple-element.57), channel_id=1, source_target_pairs={{0,12},{2,14},{4,8},{6,10},{8,4},{10,6},{12,0},{14,2},{1,13},{3,15... | collective-permute-start | bytes 196616 | tf_op jit(solution)/shard_map/ppermute | solution.py:543
  90.6 18.6 %collective-permute-start.17 = (bf16[32,1024]{1,0:T(8,128)(2,1)S(1)}, bf16[32,1024]{1,0:T(8,128)(2,1)S(1)}, u32[]{:S(2)}, u32[]{:S(2)}) collective-permute-start(bf16[32,1024]{1,0:T(8,128)(2,1)S(1)} %add_pieces.3.refs_6_.refs_1_), channel_id=1, source_target_pairs={{0,12},{2,14},{4,8},{6,10},{8,4},{10,6},{12,0},{14,2},{1,13},{3,15... | collective-permute-start | bytes 196616 | tf_op jit(solution)/shard_map/ppermute | solution.py:543
  93.0 16.2 %collective-permute-start.16 = (bf16[32,1024]{1,0:T(8,128)(2,1)S(1)}, bf16[32,1024]{1,0:T(8,128)(2,1)S(1)}, u32[]{:S(2)}, u32[]{:S(2)}) collective-permute-start(bf16[32,1024]{1,0:T(8,128)(2,1)S(1)} %add_pieces.3.refs_6_.refs_1_), channel_id=1, source_target_pairs={{0,8},{2,10},{4,12},{6,14},{8,0},{10,2},{12,4},{14,6},{1,9},{3,11}... | collective-permute-start | bytes 196616 | tf_op jit(solution)/shard_map/ppermute | solution.py:543
  93.0 16.2 %collective-permute-start.15 = (bf16[32,1024]{1,0:T(8,128)(2,1)S(1)}, bf16[32,1024]{1,0:T(8,128)(2,1)S(1)}, u32[]{:S(2)}, u32[]{:S(2)}) collective-permute-start(bf16[32,1024]{1,0:T(8,128)(2,1)S(1)} %add_pieces.3.refs_6_.refs_1_), channel_id=1, source_target_pairs={{0,4},{2,6},{4,0},{6,2},{8,12},{10,14},{12,8},{14,10},{1,5},{3,7},... | collective-permute-start | bytes 196616 | tf_op jit(solution)/shard_map/ppermute | solution.py:543
  109.8 7.9 %collective-permute-start.22 = (bf16[128,1024]{1,0:T(8,128)(2,1)S(1)}, bf16[128,1024]{1,0:T(8,128)(2,1)S(1)}, u32[]{:S(2)}, u32[]{:S(2)}) collective-permute-start(bf16[128,1024]{1,0:T(8,128)(2,1)S(1)} %join_pieces.3.refs_6_.refs_8_.refs_4_), channel_id=1, source_target_pairs={{0,2},{2,0},{4,6},{6,4},{8,10},{10,8},{12,14},{14,12},{1,3},{3,1},... | collective-permute-start | bytes 786440 | tf_op jit(solution)/shard_map/ppermute | solution.py:543
  110.4 15.2 %collective-permute-start.21 = (bf16[128,1024]{1,0:T(8,128)(2,1)S(1)}, bf16[128,1024]{1,0:T(8,128)(2,1)S(1)}, u32[]{:S(2)}, u32[]{:S(2)}) collective-permute-start(bf16[128,1024]{1,0:T(8,128)(2,1)S(1)} %join_pieces.3.refs_6_.refs_8_.refs_4_), channel_id=1, source_target_pairs={{0,1},{1,0},{2,3},{3,2},{4,5},{5,4},{6,7},{7,6},{8,9},{9,8},{10,11... | collective-permute-start | bytes 786440 | tf_op jit(solution)/shard_map/ppermute | solution.py:540
  117.7 7.9 %collective-permute-start.23 = (bf16[128,1024]{1,0:T(8,128)(2,1)S(1)}, bf16[128,1024]{1,0:T(8,128)(2,1)S(1)}, u32[]{:S(2)}, u32[]{:S(2)}) collective-permute-start(bf16[128,1024]{1,0:T(8,128)(2,1)S(1)} %collective-permute-done.22.refs_9_.refs_5_), channel_id=1, source_target_pairs={{0,1},{1,0},{2,3},{3,2},{4,5},{5,4},{6,7},{7,6},{8,9},{9,8},{10,11... | collective-permute-start | bytes 786440 | tf_op jit(solution)/shard_map/ppermute | solution.py:540
  146.8 8.3 %collective-permute-start.25 = (bf16[256,4096]{1,0:T(8,128)(2,1)S(1)}, bf16[256,4096]{1,0:T(8,128)(2,1)S(1)}, u32[]{:S(2)}, u32[]{:S(2)}) collective-permute-start(bf16[256,4096]{1,0:T(8,128)(2,1)S(1)} %get-tuple-element.61.refs_6_), channel_id=1, source_target_pairs={{0,1},{1,0},{2,3},{3,2},{4,5},{5,4},{6,7},{7,6},{8,9},{9,8},{10,11... | collective-permute-start | bytes 6291464 | tf_op jit(solution)/shard_map/ppermute | solution.py:540
  146.9 8.2 %collective-permute-start.24 = (bf16[256,4096]{1,0:T(8,128)(2,1)S(1)}, bf16[256,4096]{1,0:T(8,128)(2,1)S(1)}, u32[]{:S(2)}, u32[]{:S(2)}) collective-permute-start(bf16[256,4096]{1,0:T(8,128)(2,1)S(1)} %get-tuple-element.62), channel_id=1, source_target_pairs={{0,1},{1,0},{2,3},{3,2},{4,5},{5,4},{6,7},{7,6},{8,9},{9,8},{10,11... | collective-permute-start | bytes 6291464 | tf_op jit(solution)/shard_map/ppermute | solution.py:540

commit v4 on v3

--- a/solution.py
+++ b/solution.py
@@ -153,12 +153,12 @@
     return (c.astype(F32) * x.astype(F32)).astype(BF)
 
 
-def back_project(at, s, x, x_o, c, c_o, u, so_far, after=()):
+def back_project(at, s, x, x_o, c, c_o, u, so_far, after=(), tk=1024):
     rows, (half, rank) = x.shape[0], u.shape
     part = half // 2
-    tk = min(512, part)
+    tk = min(tk, part)
     n = part // tk
-    slots = min(4, n)
+    slots = min(2, n)
     first = so_far is None
 
     def body(at_ref, x_ref, xo_ref, c_ref, co_ref, u_ref, *rest):
@@ -224,7 +224,7 @@
         + ([] if first else [whole])
         + [dma(n), dma(slots)],
         flops=2 * rows * half * rank,
-        mib=12,
+        mib=16,
         after=after,
     )
 
@@ -282,11 +282,11 @@
         both[at_block(2 * i + 1 - bit, each), :] = other[...]
 
 
-def factor_grad(at, name, s, turned, p, so_far, placed=None, after=()):
+def factor_grad(at, name, s, turned, p, so_far, placed=None, after=(), tw=1024):
     half, rows2 = turned.shape
     rank = p[0].shape[1]
     part = half // 2
-    tw = min(1024, part)
+    tw = min(tw, part)
     n = part // tw
     np_ = len(p)
     recv, full = placed or ((), None)
@@ -349,16 +349,16 @@
         [pltpu.VMEM((2, tw, rank), BF), pltpu.VMEM((rows2, rank), BF), dma(2), dma(max(1, nr))],
         flops=rows2 * half * rank,
         aliases=aliases,
-        mib=12,
+        mib=16,
         after=after,
     )
 
 
-def expand(at, s, u, p, after=()):
+def expand(at, s, u, p, after=(), tw=1024):
     half, rank = u.shape
     rows2 = sum(a.shape[0] for a in p)
     part = half // 2
-    tw = min(1024, part)
+    tw = min(tw, part)
     n = part // tw
     slots = min(3, n)
 
@@ -395,18 +395,18 @@
     )[0]
 
 
-def input_grad(at, s, c, c_o, ex, v, bias, g, so_far, width, after=()):
+def input_grad(at, s, c, c_o, ex, v, bias, g, so_far, width, after=(), tw=1024):
     rows, half = c_o.shape
     rank = v.shape[1]
     part = half // 2
-    tw = min(512, part)
+    tw = min(tw, part)
     n = part // tw
-    slots = min(4, n)
+    slots = min(2, n)
     ng = len(g)
 
     def body(at_ref, c_ref, co_ref, ex_ref, v_ref, b_ref, *refs):
         g_refs, refs = refs[:ng], refs[ng + (so_far is not None) :]
-        own_ref, oth_ref, stage, vv, bk, both, sems, v_sem = refs
+        own_ref, oth_ref, stage, vv, both, sems, v_sem = refs
 
         def v_copy(k):
             slot = lax.rem(k, slots)
@@ -418,44 +418,32 @@
         def out(k, slot):
             return copy(stage.at[slot], own_ref.at[:, columns(k)], sems.at[slot])
 
-        def finish(k, slot):
-            here = at_block(k, tw)
-            there = pl.ds(pl.multiple_of(s * part + k * tw, tw), tw)
-            b = b_ref[:, columns(k)].astype(F32)
-            cf, cof = c_ref[:, here].astype(F32), co_ref[:, there].astype(F32)
-            stage[slot] = (cf * (ex_ref[:rows, here] + b) + cf + bk[slot, :rows, :]).astype(BF)
-            oth_ref[:, here] = (cof * (ex_ref[rows:, here] + b) + cof + bk[slot, rows:, :]).astype(BF)
-
-        def product(k, slot):
-            bk[slot] = lax.dot_general(both[...], vv[lax.rem(k, slots)], NT, preferred_element_type=F32)
-
         for k in range(slots):
             v_copy(k).start()
         fill(at_ref, both, g_refs)
-        v_copy(0).wait()
-        product(0, 0)
-
-        @pl.loop(1, n)
+
+        @pl.loop(0, n)
         def _(k):
-            now, last = lax.rem(k, 2), lax.rem(k + 1, 2)
+            slot = lax.rem(k, 2)
+            here = at_block(k, tw)
+            there = pl.ds(pl.multiple_of(s * part + k * tw, tw), tw)
             v_copy(k).wait()
 
-            @pl.when(k >= 3)
+            @pl.when(k >= 2)
             def _():
-                out(k - 1, last).wait()
-
-            finish(k - 1, last)
-            product(k, now)
-            out(k - 1, last).start()
-
-            @pl.when(k - 1 + slots < n)
+                out(k, slot).wait()
+
+            bk = lax.dot_general(both[...], vv[lax.rem(k, slots)], NT, preferred_element_type=F32)
+            b = b_ref[:, columns(k)].astype(F32)
+            cf, cof = c_ref[:, here].astype(F32), co_ref[:, there].astype(F32)
+            stage[slot] = (cf * (ex_ref[:rows, here] + b) + cf + bk[:rows]).astype(BF)
+            oth_ref[:, here] = (cof * (ex_ref[rows:, here] + b) + cof + bk[rows:]).astype(BF)
+            out(k, slot).start()
+
+            @pl.when(k + slots < n)
             def _():
-                v_copy(k - 1 + slots).start()
-
-        if n >= 3:
-            out(n - 1, (n - 1) % 2).wait()
-        finish(n - 1, (n - 1) % 2)
-        out(n - 1, (n - 1) % 2).start()
+                v_copy(k + slots).start()
+
         for k in range(max(0, n - 2), n):
             out(k, k % 2).wait()
 
@@ -473,14 +461,13 @@
         [
             pltpu.VMEM((2, rows, tw), BF),
             pltpu.VMEM((slots, tw, rank), BF),
-            pltpu.VMEM((2, 2 * rows, tw), F32),
             pltpu.VMEM((2 * rows, rank), BF),
             dma(2),
             dma(slots),
         ],
         flops=2 * rows * half * rank,
         aliases=aliases,
-        mib=12,
+        mib=16,
         after=after,
     )
 
@@ -502,33 +489,33 @@
     rows, rank = a.shape
     each = rows // m
 
-    def body(at_ref, a_ref, b_ref, *outs):
-        for d in range(m):
-            here = at_block((at_ref[1] >> 1) ^ d, each)
-            outs[d][...] = plus(a_ref[here, :], b_ref[here, :]).astype(BF)
-
-    return call(body, "pieces_of", at, [(a, "v"), (b, "v")], [((each, rank), BF, "v")] * m, after=after)
+    def body(at_ref, a_ref, b_ref, o_ref):
+        for j in range(m):
+            here = slice(j * each, (j + 1) * each)
+            o_ref[j] = plus(a_ref[here, :], b_ref[here, :]).astype(BF)
+
+    return call(body, "pieces_of", at, [(a, "v"), (b, "v")], [((m, each, rank), BF, "v")], after=after)[0]
 
 
 def add_pieces(at, parts, after=()):
-    def body(at_ref, *refs):
-        total = refs[0][...].astype(F32)
-        for r in refs[1:-1]:
-            total += r[...].astype(F32)
-        refs[-1][...] = total.astype(BF)
-
-    return call(body, "add_pieces", at, [(a, "v") for a in parts], [(parts[0].shape, BF, "v")], after=after)[0]
-
-
-def join_pieces(at, parts, after=()):
-    m = len(parts)
-    each, rank = parts[0].shape
-
-    def body(at_ref, *refs):
-        for d in range(m):
-            refs[-1][at_block((at_ref[1] >> 1) ^ d, each), :] = refs[d][...]
-
-    return call(body, "join_pieces", at, [(a, "v") for a in parts], [((m * each, rank), BF, "v")], after=after)[0]
+    m = parts.shape[0]
+
+    def body(at_ref, a_ref, o_ref):
+        total = a_ref[0].astype(F32)
+        for j in range(1, m):
+            total += a_ref[j].astype(F32)
+        total = total.astype(BF)
+        for j in range(m):
+            o_ref[j] = total
+
+    return call(body, "add_pieces", at, [(parts, "v")], [(parts.shape, BF, "v")], after=after)[0]
+
+
+def hold(at, a, after):
+    def body(at_ref, a_ref, o_ref):
+        pass
+
+    return call(body, "hold", at, [(a, "v")], [(a.shape, a.dtype, "v")], aliases={1: 0}, after=after)[0]
 
 
 def solution(mesh):
@@ -543,7 +530,11 @@
         return lax.ppermute(a, "col", [(i, i ^ d) for i in range(n)])
 
     def spread(parts):
-        return [parts[0]] + [to(parts[d], 2 * d) for d in range(1, m)]
+        groups = [[bit + 2 * j for j in range(m)] for bit in range(2)]
+        return lax.all_to_all(parts, "col", split_axis=0, concat_axis=0, axis_index_groups=groups, tiled=True)
+
+    def whole(parts):
+        return parts.reshape(-1, parts.shape[-1])
 
     def ends(half):
         other = to(half, 1)
@@ -563,27 +554,27 @@
         x_o = trade(x_s)
         own, x_own, c_s, *v_in = project_own(at, x, v, c, [x_s])
         theirs = trade(own)
-        c_o = trade(c_s)
+        c_o = trade(hold(at, c_s, [theirs]))
         sums = project_other(at, x_o, v_in, theirs, direct)
         acc, b0, c0 = back_project(at, 0, x_own, x_o, c, c_o, u, None, [sums[0]])
         if direct:
             parts = pieces_of(at, sums[0], to(sums[1], 1), m, [acc])
-            own_g, mine_g, b1, c1 = back_project(at, 1, x_own, x_o, c, c_o, u, acc, [parts[0]])
-            parts = spread(parts)
+            own_g, mine_g, b1, c1 = back_project(at, 1, x_own, x_o, c, c_o, u, acc, [parts])
             theirs_g = trade(own_g)
-            total = add_pieces(at, parts, [own_g])
-            sums_g = pair_halves(at, mine_g, theirs_g, direct, [total])
-            x_t = turn_x(at, x_own, x_o, [sums_g[0]])
-            p = ends(join_pieces(at, spread([total] * m), [x_t]))
-            parts_g = pieces_of(at, sums_g[0], to(sums_g[1], 1), m, [p[2]])
-            h_t = turn_hidden(at, x_own, x_o, (c0, c1), c_o, [parts_g[0]])
-            total_g = add_pieces(at, spread(parts_g), [h_t])
-            (grad_u,) = factor_grad(at, "u_grad", 0, h_t, p, None, after=[total_g])
-            (grad_u,) = factor_grad(at, "u_grad", 1, h_t, p, grad_u)
-            half_g = join_pieces(at, spread([total_g] * m), [(grad_u, "h")])
+            total = add_pieces(at, spread(parts), [own_g])
+            x_t = turn_x(at, x_own, x_o, [total])
+            sums_g = pair_halves(at, mine_g, theirs_g, direct, [x_t])
+            half_p = hold(at, whole(spread(total)), [sums_g[0]])
+            p = ends(half_p)
+            h_t = turn_hidden(at, x_own, x_o, (c0, c1), c_o, [half_p])
+            parts_g = pieces_of(at, sums_g[0], to(sums_g[1], 1), m, [h_t])
+            (grad_u,) = factor_grad(at, "u_grad", 0, h_t, p, None, after=[parts_g], tw=512)
+            total_g = add_pieces(at, spread(parts_g), [(grad_u, "h")])
+            (grad_u,) = factor_grad(at, "u_grad", 1, h_t, p, grad_u, after=[total_g])
+            half_g = hold(at, whole(spread(total_g)), [(grad_u, "h")])
             g = ends(half_g)
             ex0 = expand(at, 0, u, p, [half_g])
-            ex1 = expand(at, 1, u, p, [ex0])
+            ex1 = expand(at, 1, u, p, [ex0], tw=512)
         else:
             own_g, mine_g, b1, c1 = back_project(at, 1, x_own, x_o, c, c_o, u, acc)
             (sums_g,) = pair_halves(at, mine_g, trade(own_g), direct)
@@ -595,7 +586,7 @@
             ex0, ex1 = expand(at, 0, u, p), expand(at, 1, u, p)
         bias = bias[None, :]
         out, oth0 = input_grad(at, 0, c0, c_o, ex0, v, bias, g, None, width, [ex1])
-        out, oth1 = input_grad(at, 1, c1, c_o, ex1, v, bias, g, out, width)
+        out, oth1 = input_grad(at, 1, c1, c_o, ex1, v, bias, g, out, width, tw=512)
         back = [trade(oth0), trade(oth1)]
         (grad_v,) = factor_grad(at, "v_grad", 0, x_t, g, None, after=[oth1])
         grad_v, out = factor_grad(at, "v_grad", 1, x_t, g, grad_v, (back, out))

time: 163 us -> 205 us (1.26)
  local copies, waits for them, and re-layouts: 0.04 us -> 44.1 us
  waiting for transfers between devices: 24.4 us -> 13.7 us
  Pallas kernels: 111 us -> 116 us
  starting transfers between devices: 25.5 us -> 28.2 us
    unnamed x2 -> x76, local copies, waits for them, and re-layouts: 0.01 us -> 44.1 us
    all_to_all x0 -> x4, starting transfers between devices: none -> 20.2 us  [spread(): lax.all_to_all(parts, 'col', split_axis=0, concat_axis=0, axis_index_grou...]
    ppermute x16 -> x4, starting transfers between devices: 23.1 us -> 5.8 us  [to(): return lax.ppermute(a, 'col', [(i, i ^ d) for i in range(n)])]
    ppermute x16 -> x4, waiting for transfers between devices: 17 us -> 7.17 us  [to(): return lax.ppermute(a, 'col', [(i, i ^ d) for i in range(n)])]
    pallas_call x22 -> x23, Pallas kernels: 111 us -> 116 us  [call(): pl.pallas_call(lambda *refs: body(*refs[:skip], *refs[skip + len(after):]...]
  transfers between devices with their start and end apart: 26 -> 18, of which waited for: 6 -> 3; matrix products, arithmetic and copies ran while one was open for 0% -> 0% of each run, Pallas kernels for 43% -> 36%
where the time goes in v4:
time: 205 us; the launch traced here: 204 us
  Pallas kernels  116 us (57%)
  local copies, waits for them, and re-layouts  44.1 us (22%)
  starting transfers between devices  28.2 us (14%)
  waiting for transfers between devices  13.7 us (7%)
    pallas_call x23, Pallas kernels, call(): pl.pallas_call(lambda *refs: body(*refs[:skip], *refs[skip + len(after):]...  116 us
    unnamed x76, local copies, waits for them, and re-layouts  44.1 us
    all_to_all x4, starting transfers between devices, spread(): lax.all_to_all(parts, 'col', split_axis=0, concat_axis=0, axis_index_grou...  20.2 us
    ppermute x4, waiting for transfers between devices, to(): return lax.ppermute(a, 'col', [(i, i ^ d) for i in range(n)])  7.17 us
    ppermute x10, waiting for transfers between devices, trade(): return lax.ppermute(a, 'batch', swap)  6.49 us
    ppermute x4, starting transfers between devices, to(): return lax.ppermute(a, 'col', [(i, i ^ d) for i in range(n)])  5.8 us
  transfers between devices with their start and end apart: 18, of which 3 were waited for; matrix products, arithmetic and copies ran while one was open for 0% of the time, Pallas kernels for 36%

profile of v4, /device:TPU:0, one launch (start us, length us, event | category | flops | bytes accessed | tf_op | source)
XLA Modules:
  0.0 203.7 jit_solution(7164251443749439011)
XLA Ops:
  0.7 2.8 %cut_half.1.refs_4_ = bf16[256,8192]{1,0:T(8,128)(2,1)S(1)} custom-call(s32[2]{0:T(128)S(1)} %pad_add_fusion.refs_0_, bf16[256,16384]{1,0:T(8,128)(2,1)} %refs_1_.5), custom_call_target="tpu_custom_call" | custom-call | bytes 8388608 | tf_op jit(solution)/shard_map/cut_half/pallas_call | solution.py:20
  3.5 9.9 %project_own.1 = (bf16[256,1024]{1,0:T(8,128)(2,1)S(1)}, bf16[256,8192]{1,0:T(8,128)(2,1)S(1)}, bf16[256,8192]{1,0:T(8,128)(2,1)S(1)}, bf16[2048,1024]{1,0:T(8,1...) custom-call(s32[2]{0:T(128)S(1)} %pad_add_fusion.refs_0_, ...), custom_call_target="tpu_custom_call" | custom-call | flops 4294967296 | bytes 33554432 | tf_op jit(solution)/shard_map/project_own/pallas_call | solution.py:20
  14.0 1.5 collective-permute-done.1.refs_2_
  16.4 5.0 %collective-permute-done.refs_1_.refs_2_ = bf16[256,8192]{1,0:T(8,128)(2,1)S(1)} collective-permute-done((bf16[256,8192]{1,0:T(8,128)(2,1)S(1)}, bf16[256,8192]{1,0:T(8,128)(2,1)S(1)}, u32[]{:S(2)}, u32[]{:S(2)}) %collective-permute-start) | collective-permute-done | bytes 4194336 | tf_op jit(solution)/shard_map/ppermute | solution.py:527
  21.4 5.2 %project_other.1 = (bf16[128,1024]{1,0:T(8,128)(2,1)S(1)}, bf16[128,1024]{1,0:T(8,128)(2,1)S(1)}) custom-call(s32[2]{0:T(128)S(1)} %pad_add_fusion.refs_0_, bf16[256,8192]{1,0:T(8,128)(2,1)S(1)} %collective-permute-done.refs_1_.refs_2_, bf16[256,1024]{1,0:T(8,128)(2,1)S(1)} %collective-permute-done.1.refs_2_, ...), custom_call_target="tpu_custom_call" | custom-call | flops 4294967296 | bytes 21495808 | tf_op jit(solution)/shard_map/project_other/pallas_call | solution.py:20
  26.6 2.9 %collective-permute-start.2 = (bf16[128,1024]{1,0:T(8,128)(2,1)S(1)}, bf16[128,1024]{1,0:T(8,128)(2,1)S(1)}, u32[]{:S(2)}, u32[]{:S(2)}) collective-permute-start(bf16[128,1024]{1,0:T(8,128)(2,1)S(1)} %get-tuple-element.35), channel_id=1, source_target_pairs={{0,2},{2,0},{4,6},{6,4},{8,10},{10,8},{12,14},{14,12},{1,3},{3,1},... | collective-permute-start | bytes 786440 | tf_op jit(solution)/shard_map/ppermute | solution.py:530
  29.6 9.2 %back_project.2 = (f32[512,1024]{1,0:T(8,128)S(1)}, f32[1,4096]{1,0:T(1,128)S(1)}, bf16[256,4096]{1,0:T(8,128)(2,1)S(1)}) custom-call(s32[2]{0:T(128)S(1)} %pad_add_fusion.refs_0_, bf16[256,8192]{1,0:T(8,128)(2,1)S(1)} %get-tuple-element.28.refs_1_, bf16[256,8192]{1,0:T(8,128)(2,1)S(1)} %collective-permute-done.refs_1_.refs_2_, bf16[256,16384]{1,0:T(8,128)(2,1)} %refs_3_.5, ...), custom_call_target="tpu_custom_call" | custom-call | flops 4294967296 | bytes 37748736 | tf_op jit(solution)/shard_map/back_project/pallas_call | solution.py:20
  38.8 1.4 copy-done.16
  40.2 1.3 pieces_of.2.refs_7_
  41.4 4.9 %all-to-all-start = ((bf16[4,32,1024]{2,1,0:T(8,128)(2,1)}), bf16[4,32,1024]{2,1,0:T(8,128)(2,1)S(1)}, u32[]{:S(2)}, u32[]{:S(2)}) async-start(bf16[4,32,1024]{2,1,0:T(8,128)(2,1)} %pieces_of.2.refs_7_), calls=%async_computation | async-start | bytes 524288 | tf_op jit(solution)/shard_map/all_to_all | solution.py:534
  46.3 2.2 %copy-done.5 = bf16[256,8192]{1,0:T(8,128)(2,1)S(1)} copy-done((bf16[256,8192]{1,0:T(8,128)(2,1)S(1)}, bf16[256,8192]{1,0:T(8,128)(2,1)}, u32[]{:S(2)}) %copy-start.5) | copy-done | bytes 4194328
  48.5 2.2 %copy-done.9 = bf16[256,8192]{1,0:T(8,128)(2,1)S(1)} copy-done((bf16[256,8192]{1,0:T(8,128)(2,1)S(1)}, bf16[256,8192]{1,0:T(8,128)(2,1)}, u32[]{:S(2)}) %copy-start.9) | copy-done | bytes 4194328
  50.7 2.2 %copy-done.13 = bf16[256,8192]{1,0:T(8,128)(2,1)S(1)} copy-done((bf16[256,8192]{1,0:T(8,128)(2,1)S(1)}, bf16[256,8192]{1,0:T(8,128)(2,1)}, u32[]{:S(2)}) %copy-start.13) | copy-done | bytes 4194328
  52.9 9.4 %back_project.3 = (bf16[256,1024]{1,0:T(8,128)(2,1)}, f32[256,1024]{1,0:T(8,128)S(1)}, f32[1,4096]{1,0:T(1,128)S(1)}, bf16[256,4096]{1,0:T(8,128)(2,1)S(1)}) custom-call(s32[2]{0:T(128)S(1)} %pad_add_fusion.refs_0_, bf16[256,8192]{1,0:T(8,128)(2,1)S(1)} %copy-done.13, bf16[256,8192]{1,0:T(8,128)(2,1)S(1)} %copy-done.5, bf16[256,16384]{1,0:T(8,128)(2,1)} %refs_3_.5, ...), custom_call_target="tpu_custom_call" | custom-call | flops 4294967296 | bytes 39845888 | tf_op jit(solution)/shard_map/back_project/pallas_call | solution.py:20
  62.3 1.4 copy-done.18
  63.7 2.2 %add_pieces.2.refs_3_ = bf16[4,32,1024]{2,1,0:T(8,128)(2,1)} custom-call(s32[2]{0:T(128)S(1)} %pad_add_fusion.refs_0_, bf16[4,32,1024]{2,1,0:T(8,128)(2,1)S(1)} %all-to-all-done.refs_1_, bf16[256,1024]{1,0:T(8,128)(2,1)} %get-tuple-element.38.refs_2_), custom_call_target="tpu_custom_call" | custom-call | bytes 262144 | tf_op jit(solution)/shard_map/add_pieces/pallas_call | solution.py:20
  65.8 5.1 %all-to-all-start.1 = ((bf16[4,32,1024]{2,1,0:T(8,128)(2,1)}), bf16[4,32,1024]{2,1,0:T(8,128)(2,1)S(1)}, u32[]{:S(2)}, u32[]{:S(2)}) async-start(bf16[4,32,1024]{2,1,0:T(8,128)(2,1)} %add_pieces.2.refs_3_), calls=%async_computation.1 | async-start | bytes 524288 | tf_op jit(solution)/shard_map/all_to_all | solution.py:534
  70.9 2.2 %copy-done.6 = bf16[256,8192]{1,0:T(8,128)(2,1)S(1)} copy-done((bf16[256,8192]{1,0:T(8,128)(2,1)S(1)}, bf16[256,8192]{1,0:T(8,128)(2,1)}, u32[]{:S(2)}) %copy-start.6) | copy-done | bytes 4194328
  73.1 2.2 %copy-done.14 = bf16[256,8192]{1,0:T(8,128)(2,1)S(1)} copy-done((bf16[256,8192]{1,0:T(8,128)(2,1)S(1)}, bf16[256,8192]{1,0:T(8,128)(2,1)}, u32[]{:S(2)}) %copy-start.14) | copy-done | bytes 4194328
  75.3 4.0 %turn_x.1.refs_3_.refs_1_ = bf16[8192,512]{1,0:T(8,128)(2,1)S(1)} custom-call(s32[2]{0:T(128)S(1)} %pad_add_fusion.refs_0_, bf16[256,8192]{1,0:T(8,128)(2,1)S(1)} %copy-done.14, bf16[256,8192]{1,0:T(8,128)(2,1)S(1)} %copy-done.6, bf16[4,32,1024]{2,1,0:T(8,128)(2,1)} %add_pieces.2.refs_3_), custom_call_target="tpu_custom_call" | custom-call | bytes 8388608 | tf_op jit(solution)/shard_map/turn_x/pallas_call | solution.py:20
  80.1 1.2 copy-done.30
  81.4 1.0 copy-done.34
  82.4 1.3 pair_halves.1
  83.7 3.4 %copy-done = bf16[8192,512]{1,0:T(8,128)(2,1)} copy-done((bf16[8192,512]{1,0:T(8,128)(2,1)}, bf16[8192,512]{1,0:T(8,128)(2,1)S(1)}, u32[]{:S(2)}) %copy-start) | copy-done | bytes 8388632
  88.5 1.3 collective-permute-start.5
  89.8 7.2 %collective-permute-done.7.refs_5_ = bf16[128,1024]{1,0:T(8,128)(2,1)S(1)} collective-permute-done((bf16[128,1024]{1,0:T(8,128)(2,1)S(1)}, bf16[128,1024]{1,0:T(8,128)(2,1)S(1)}, u32[]{:S(2)}, u32[]{:S(2)}) %collective-permute-start.7) | collective-permute-done | bytes 262176 | tf_op jit(solution)/shard_map/ppermute | solution.py:530
  97.0 2.2 %copy-done.7 = bf16[256,8192]{1,0:T(8,128)(2,1)S(1)} copy-done((bf16[256,8192]{1,0:T(8,128)(2,1)S(1)}, bf16[256,8192]{1,0:T(8,128)(2,1)}, u32[]{:S(2)}) %copy-start.7) | copy-done | bytes 4194328
  99.2 2.2 %copy-done.10 = bf16[256,8192]{1,0:T(8,128)(2,1)S(1)} copy-done((bf16[256,8192]{1,0:T(8,128)(2,1)S(1)}, bf16[256,8192]{1,0:T(8,128)(2,1)}, u32[]{:S(2)}) %copy-start.10) | copy-done | bytes 4194328
  101.4 2.2 %copy-done.15 = bf16[256,8192]{1,0:T(8,128)(2,1)S(1)} copy-done((bf16[256,8192]{1,0:T(8,128)(2,1)S(1)}, bf16[256,8192]{1,0:T(8,128)(2,1)}, u32[]{:S(2)}) %copy-start.15) | copy-done | bytes 4194328
  103.6 1.6 copy-done.19
  105.2 3.7 %turn_hidden.1.refs_3_.refs_1_ = bf16[8192,512]{1,0:T(8,128)(2,1)S(1)} custom-call(s32[2]{0:T(128)S(1)} %pad_add_fusion.refs_0_, bf16[256,8192]{1,0:T(8,128)(2,1)S(1)} %copy-done.15, bf16[256,8192]{1,0:T(8,128)(2,1)S(1)} %copy-done.7, bf16[256,4096]{1,0:T(8,128)(2,1)S(1)} %copy-done.17, bf16[256,4096]{1,0:T(8,128)(2,1)S(1)} %copy-done.19, ...), custom_call_target="tpu_custom_call" | custom-call | bytes 16777216 | tf_op jit(solution)/shard_map/turn_hidden/pallas_call | solution.py:20
  109.5 3.4 %copy-done.1 = bf16[8192,512]{1,0:T(8,128)(2,1)} copy-done((bf16[8192,512]{1,0:T(8,128)(2,1)}, bf16[8192,512]{1,0:T(8,128)(2,1)S(1)}, u32[]{:S(2)}) %copy-start.1) | copy-done | bytes 8388632
  113.6 5.1 %all-to-all-start.2 = ((bf16[4,32,1024]{2,1,0:T(8,128)(2,1)}), bf16[4,32,1024]{2,1,0:T(8,128)(2,1)}, u32[]{:S(2)}, u32[]{:S(2)}) async-start(bf16[4,32,1024]{2,1,0:T(8,128)(2,1)} %copy-done.27), calls=%async_computation.2 | async-start | bytes 524288 | tf_op jit(solution)/shard_map/all_to_all | solution.py:534
  118.8 3.5 %copy-done.2 = bf16[8192,512]{1,0:T(8,128)(2,1)S(1)} copy-done((bf16[8192,512]{1,0:T(8,128)(2,1)S(1)}, bf16[8192,512]{1,0:T(8,128)(2,1)}, u32[]{:S(2)}) %copy-start.2) | copy-done | bytes 8388632
  122.2 0.9 copy-done.28
  123.2 8.1 %u_grad.2.refs_2_.refs_6_ = bf16[8192,1024]{1,0:T(8,128)(2,1)} custom-call(s32[2]{0:T(128)S(1)} %pad_add_fusion.refs_0_, bf16[8192,512]{1,0:T(8,128)(2,1)S(1)} %copy-done.2, bf16[128,1024]{1,0:T(8,128)(2,1)S(1)} %collective-permute-done.6.refs_2_, bf16[128,1024]{1,0:T(8,128)(2,1)S(1)} %collective-permute-done.8.refs_3_, ...), custom_call_target="tpu_custom_call" | custom-call | flops 4294967296 | bytes 9437184 | tf_op jit(solution)/shard_map/u_grad/pallas_call | solution.py:20
  131.3 1.0 add_pieces.3.refs_7_
  133.0 5.1 %all-to-all-start.3 = ((bf16[4,32,1024]{2,1,0:T(8,128)(2,1)}), bf16[4,32,1024]{2,1,0:T(8,128)(2,1)S(1)}, u32[]{:S(2)}, u32[]{:S(2)}) async-start(bf16[4,32,1024]{2,1,0:T(8,128)(2,1)} %copy-done.25), calls=%async_computation.3 | async-start | bytes 524288 | tf_op jit(solution)/shard_map/all_to_all | solution.py:534
  138.1 3.4 %copy-done.3 = bf16[8192,512]{1,0:T(8,128)(2,1)S(1)} copy-done((bf16[8192,512]{1,0:T(8,128)(2,1)S(1)}, bf16[8192,512]{1,0:T(8,128)(2,1)}, u32[]{:S(2)}) %copy-start.3) | copy-done | bytes 8388632
  142.4 7.0 %u_grad.3.refs_2_ = bf16[8192,1024]{1,0:T(8,128)(2,1)} custom-call(s32[2]{0:T(128)S(1)} %pad_add_fusion.refs_0_, bf16[8192,512]{1,0:T(8,128)(2,1)S(1)} %copy-done.3, bf16[128,1024]{1,0:T(8,128)(2,1)S(1)} %collective-permute-done.6.refs_2_, bf16[128,1024]{1,0:T(8,128)(2,1)S(1)} %collective-permute-done.8.refs_3_, ...), custom_call_target="tpu_custom_call", output_to_operand_aliasing={{}: (6, {})} | custom-call | flops 4294967296 | bytes 26214400 | tf_op jit(solution)/shard_map/u_grad/pallas_call | solution.py:20
  150.8 7.3 %expand.2.refs_6_.refs_3_ = f32[512,4096]{1,0:T(8,128)S(1)} custom-call(s32[2]{0:T(128)S(1)} %pad_add_fusion.refs_0_, bf16[8192,1024]{1,0:T(8,128)(2,1)} %refs_1_.7, bf16[128,1024]{1,0:T(8,128)(2,1)S(1)} %collective-permute-done.6.refs_2_, bf16[128,1024]{1,0:T(8,128)(2,1)S(1)} %collective-permute-done.8.refs_3_, bf16[128,1024]{1,0:T(8,128)(2,1)S(1)} %hold.4.refs_6_.refs_4_, ...), custom_call_target="tpu_custom_call" | custom-call | flops 4294967296 | bytes 17825792 | tf_op jit(solution)/shard_map/expand/pallas_call | solution.py:20
  158.7 1.2 copy-done.22
  160.0 0.9 copy-done.24
  160.9 7.8 %expand.3.refs_10_.refs_3_ = f32[512,4096]{1,0:T(8,128)S(1)} custom-call(s32[2]{0:T(128)S(1)} %pad_add_fusion.refs_0_, bf16[8192,1024]{1,0:T(8,128)(2,1)} %refs_1_.7, bf16[128,1024]{1,0:T(8,128)(2,1)S(1)} %copy-done.22, bf16[128,1024]{1,0:T(8,128)(2,1)S(1)} %copy-done.24, bf16[128,1024]{1,0:T(8,128)(2,1)S(1)} %hold.4.refs_6_.refs_4_, ...), custom_call_target="tpu_custom_call" | custom-call | flops 4294967296 | bytes 17825792 | tf_op jit(solution)/shard_map/expand/pallas_call | solution.py:20
  168.7 8.7 %input_grad.2 = (bf16[256,16384]{1,0:T(8,128)(2,1)}, bf16[256,4096]{1,0:T(8,128)(2,1)S(1)}) custom-call(s32[2]{0:T(128)S(1)} %pad_add_fusion.refs_0_, bf16[256,4096]{1,0:T(8,128)(2,1)S(1)} %copy-done.17, bf16[256,8192]{1,0:T(8,128)(2,1)S(1)} %copy-done.11, f32[512,4096]{1,0:T(8,128)S(1)} %expand.2.refs_6_.refs_3_, bf16[8192,1024]{1,0:T(8,128)(2,1)} %refs_4_.3, ...), custom_call_target="tpu_custom_call" | custom-call | flops 4294967296 | bytes 32538624 | tf_op jit(solution)/shard_map/input_grad/pallas_call | solution.py:20
  177.4 10.7 %input_grad.3 = (bf16[256,16384]{1,0:T(8,128)(2,1)}, bf16[256,4096]{1,0:T(8,128)(2,1)S(1)}) custom-call(s32[2]{0:T(128)S(1)} %pad_add_fusion.refs_0_, bf16[256,4096]{1,0:T(8,128)(2,1)S(1)} %copy-done.20, bf16[256,8192]{1,0:T(8,128)(2,1)S(1)} %copy-done.11, f32[512,4096]{1,0:T(8,128)S(1)} %expand.3.refs_10_.refs_3_, ...), custom_call_target="tpu_custom_call", output_to_operand_aliasing={{0}: (10, {})} | custom-call | flops 4294967296 | bytes 40927232 | tf_op jit(solution)/shard_map/input_grad/pallas_call | solution.py:20
  189.4 7.0 %v_grad.2.refs_6_ = bf16[8192,1024]{1,0:T(8,128)(2,1)} custom-call(s32[2]{0:T(128)S(1)} %pad_add_fusion.refs_0_, bf16[8192,512]{1,0:T(8,128)(2,1)S(1)} %bitcast.7, bf16[128,1024]{1,0:T(8,128)(2,1)S(1)} %collective-permute-done.9.refs_6_.refs_2_, bf16[128,1024]{1,0:T(8,128)(2,1)S(1)} %collective-permute-done.11.refs_7_.refs_3_, ...), custom_call_target="tpu_custom_call" | custom-call | flops 4294967296 | bytes 9437184 | tf_op jit(solution)/shard_map/v_grad/pallas_call | solution.py:20
  196.4 7.1 %v_grad.3 = (bf16[8192,1024]{1,0:T(8,128)(2,1)}, bf16[256,16384]{1,0:T(8,128)(2,1)}) custom-call(s32[2]{0:T(128)S(1)} %pad_add_fusion.refs_0_, bf16[8192,512]{1,0:T(8,128)(2,1)S(1)} %bitcast.7, bf16[128,1024]{1,0:T(8,128)(2,1)S(1)} %collective-permute-done.9.refs_6_.refs_2_, ...), custom_call_target="tpu_custom_call", output_to_operand_aliasing={{0}: (6, {}), {1}: (9, {})} | custom-call | flops 4294967296 | bytes 38797312 | tf_op jit(solution)/shard_map/v_grad/pallas_call | solution.py:20
  (91 shorter events, 10.0 us)
Async XLA Ops:
  13.4 16.2 %copy-start.12 = (bf16[256,8192]{1,0:T(8,128)(2,1)}, bf16[256,8192]{1,0:T(8,128)(2,1)S(1)}, u32[]{:S(2)}) copy-start(bf16[256,8192]{1,0:T(8,128)(2,1)S(1)} %get-tuple-element.28.refs_1_) | copy-start | bytes 12582916
  13.4 2.1 %collective-permute-start.1 = (bf16[256,1024]{1,0:T(8,128)(2,1)S(1)}, bf16[256,1024]{1,0:T(8,128)(2,1)S(1)}, u32[]{:S(2)}, u32[]{:S(2)}) collective-permute-start(bf16[256,1024]{1,0:T(8,128)(2,1)S(1)} %get-tuple-element.29), channel_id=1, source_target_pairs={{0,1},{1,0},{2,3},{3,2},{4,5},{5,4},{6,7},{7,6},{8,9},{9,8},{10,11... | collective-permute-start | bytes 1572872 | tf_op jit(solution)/shard_map/ppermute | solution.py:527
  13.9 7.5 %collective-permute-start = (bf16[256,8192]{1,0:T(8,128)(2,1)S(1)}, bf16[256,8192]{1,0:T(8,128)(2,1)S(1)}, u32[]{:S(2)}, u32[]{:S(2)}) collective-permute-start(bf16[256,8192]{1,0:T(8,128)(2,1)S(1)} %cut_half.1.refs_4_), channel_id=1, source_target_pairs={{0,1},{1,0},{2,3},{3,2},{4,5},{5,4},{6,7},{7,6},{8,9},{9,8},{10,11... | collective-permute-start | bytes 12582920 | tf_op jit(solution)/shard_map/ppermute | solution.py:527
  16.0 13.6 %collective-permute-start.3 = (bf16[256,8192]{1,0:T(8,128)(2,1)S(1)}, bf16[256,8192]{1,0:T(8,128)(2,1)S(1)}, u32[]{:S(2)}, u32[]{:S(2)}) collective-permute-start(bf16[256,8192]{1,0:T(8,128)(2,1)S(1)} %hold.3), channel_id=1, source_target_pairs={{0,1},{1,0},{2,3},{3,2},{4,5},{5,4},{6,7},{7,6},{8,9},{9,8},{10,11... | collective-permute-start | bytes 12582920 | tf_op jit(solution)/shard_map/ppermute | solution.py:527
  21.4 8.1 %copy-start.4 = (bf16[256,8192]{1,0:T(8,128)(2,1)}, bf16[256,8192]{1,0:T(8,128)(2,1)S(1)}, u32[]{:S(2)}) copy-start(bf16[256,8192]{1,0:T(8,128)(2,1)S(1)} %collective-permute-done.refs_1_.refs_2_) | copy-start | bytes 12582916
  26.6 13.5 %collective-permute-start.2 = (bf16[128,1024]{1,0:T(8,128)(2,1)S(1)}, bf16[128,1024]{1,0:T(8,128)(2,1)S(1)}, u32[]{:S(2)}, u32[]{:S(2)}) collective-permute-start(bf16[128,1024]{1,0:T(8,128)(2,1)S(1)} %get-tuple-element.35), channel_id=1, source_target_pairs={{0,2},{2,0},{4,6},{6,4},{8,10},{10,8},{12,14},{14,12},{1,3},{3,1},... | collective-permute-start | bytes 786440 | tf_op jit(solution)/shard_map/ppermute | solution.py:530
  29.5 9.2 %copy-start.8 = (bf16[256,8192]{1,0:T(8,128)(2,1)}, bf16[256,8192]{1,0:T(8,128)(2,1)S(1)}, u32[]{:S(2)}) copy-start(bf16[256,8192]{1,0:T(8,128)(2,1)S(1)} %collective-permute-done.3.refs_4_.refs_5_.refs_2_) | copy-start | bytes 12582916
  38.8 1.4 copy-start.16
  41.4 22.2 %all-to-all-start = ((bf16[4,32,1024]{2,1,0:T(8,128)(2,1)}), bf16[4,32,1024]{2,1,0:T(8,128)(2,1)S(1)}, u32[]{:S(2)}, u32[]{:S(2)}) async-start(bf16[4,32,1024]{2,1,0:T(8,128)(2,1)} %pieces_of.2.refs_7_), calls=%async_computation | async-start | bytes 524288 | tf_op jit(solution)/shard_map/all_to_all | solution.py:534
  46.3 2.2 %copy-start.5 = (bf16[256,8192]{1,0:T(8,128)(2,1)S(1)}, bf16[256,8192]{1,0:T(8,128)(2,1)}, u32[]{:S(2)}) copy-start(bf16[256,8192]{1,0:T(8,128)(2,1)} %copy-done.4) | copy-start | bytes 12582916
  48.5 2.2 %copy-start.9 = (bf16[256,8192]{1,0:T(8,128)(2,1)S(1)}, bf16[256,8192]{1,0:T(8,128)(2,1)}, u32[]{:S(2)}) copy-start(bf16[256,8192]{1,0:T(8,128)(2,1)} %copy-done.8) | copy-start | bytes 12582916
  50.7 2.2 %copy-start.13 = (bf16[256,8192]{1,0:T(8,128)(2,1)S(1)}, bf16[256,8192]{1,0:T(8,128)(2,1)}, u32[]{:S(2)}) copy-start(bf16[256,8192]{1,0:T(8,128)(2,1)} %copy-done.12) | copy-start | bytes 12582916
  62.3 1.4 copy-start.18
  63.7 15.7 %copy-start.29 = (f32[256,1024]{1,0:T(8,128)}, f32[256,1024]{1,0:T(8,128)S(1)}, u32[]{:S(2)}) copy-start(f32[256,1024]{1,0:T(8,128)S(1)} %get-tuple-element.39.refs_1_) | copy-start | bytes 3145732
  63.7 15.7 %collective-permute-start.4 = (bf16[256,1024]{1,0:T(8,128)(2,1)}, bf16[256,1024]{1,0:T(8,128)(2,1)S(1)}, u32[]{:S(2)}, u32[]{:S(2)}) collective-permute-start(bf16[256,1024]{1,0:T(8,128)(2,1)} %get-tuple-element.38.refs_2_), channel_id=1, source_target_pairs={{0,1},{1,0},{2,3},{3,2},{4,5},{5,4},{6,7},{7,6},{8,9},{9,8},{10,11... | collective-permute-start | bytes 1572872 | tf_op jit(solution)/shard_map/ppermute | solution.py:527
  65.8 21.3 %all-to-all-start.1 = ((bf16[4,32,1024]{2,1,0:T(8,128)(2,1)}), bf16[4,32,1024]{2,1,0:T(8,128)(2,1)S(1)}, u32[]{:S(2)}, u32[]{:S(2)}) async-start(bf16[4,32,1024]{2,1,0:T(8,128)(2,1)} %add_pieces.2.refs_3_), calls=%async_computation.1 | async-start | bytes 524288 | tf_op jit(solution)/shard_map/all_to_all | solution.py:534
  70.9 2.2 %copy-start.6 = (bf16[256,8192]{1,0:T(8,128)(2,1)S(1)}, bf16[256,8192]{1,0:T(8,128)(2,1)}, u32[]{:S(2)}) copy-start(bf16[256,8192]{1,0:T(8,128)(2,1)} %copy-done.4) | copy-start | bytes 12582916
  73.1 2.2 %copy-start.14 = (bf16[256,8192]{1,0:T(8,128)(2,1)S(1)}, bf16[256,8192]{1,0:T(8,128)(2,1)}, u32[]{:S(2)}) copy-start(bf16[256,8192]{1,0:T(8,128)(2,1)} %copy-done.12) | copy-start | bytes 12582916
  82.4 14.5 %copy-start.35 = (bf16[16384]{0:T(1024)(128)(2,1)S(1)}, bf16[16384]{0:T(1024)(128)(2,1)}, u32[]{:S(2)}) copy-start(bf16[16384]{0:T(1024)(128)(2,1)} %param.9) | copy-start | bytes 98308
  82.4 14.6 %copy-start.17 = (bf16[256,4096]{1,0:T(8,128)(2,1)S(1)}, bf16[256,4096]{1,0:T(8,128)(2,1)}, u32[]{:S(2)}) copy-start(bf16[256,4096]{1,0:T(8,128)(2,1)} %copy-done.16) | copy-start | bytes 6291460
  83.7 3.4 %copy-start = (bf16[8192,512]{1,0:T(8,128)(2,1)}, bf16[8192,512]{1,0:T(8,128)(2,1)S(1)}, u32[]{:S(2)}) copy-start(bf16[8192,512]{1,0:T(8,128)(2,1)S(1)} %turn_x.1.refs_3_.refs_1_) | copy-start | bytes 25165828
  87.1 1.3 copy-start.31
  87.7 9.3 %collective-permute-start.7 = (bf16[128,1024]{1,0:T(8,128)(2,1)S(1)}, bf16[128,1024]{1,0:T(8,128)(2,1)S(1)}, u32[]{:S(2)}, u32[]{:S(2)}) collective-permute-start(bf16[128,1024]{1,0:T(8,128)(2,1)S(1)} %hold.4.refs_6_.refs_4_), channel_id=1, source_target_pairs={{0,2},{2,0},{4,6},{6,4},{8,10},{10,8},{12,14},{14,12},{1,3},{3,1},... | collective-permute-start | bytes 786440 | tf_op jit(solution)/shard_map/ppermute | solution.py:530
  88.5 20.4 %collective-permute-start.5 = (bf16[128,1024]{1,0:T(8,128)(2,1)}, bf16[128,1024]{1,0:T(8,128)(2,1)S(1)}, u32[]{:S(2)}, u32[]{:S(2)}) collective-permute-start(bf16[128,1024]{1,0:T(8,128)(2,1)} %get-tuple-element.41), channel_id=1, source_target_pairs={{0,2},{2,0},{4,6},{6,4},{8,10},{10,8},{12,14},{14,12},{1,3},{3,1},... | collective-permute-start | bytes 786440 | tf_op jit(solution)/shard_map/ppermute | solution.py:530
  89.8 29.0 %collective-permute-start.6 = (bf16[128,1024]{1,0:T(8,128)(2,1)S(1)}, bf16[128,1024]{1,0:T(8,128)(2,1)S(1)}, u32[]{:S(2)}, u32[]{:S(2)}) collective-permute-start(bf16[128,1024]{1,0:T(8,128)(2,1)S(1)} %hold.4.refs_6_.refs_4_), channel_id=1, source_target_pairs={{0,1},{1,0},{2,3},{3,2},{4,5},{5,4},{6,7},{7,6},{8,9},{9,8},{10,11... | collective-permute-start | bytes 786440 | tf_op jit(solution)/shard_map/ppermute | solution.py:527
  96.9 21.8 %collective-permute-start.8 = (bf16[128,1024]{1,0:T(8,128)(2,1)S(1)}, bf16[128,1024]{1,0:T(8,128)(2,1)S(1)}, u32[]{:S(2)}, u32[]{:S(2)}) collective-permute-start(bf16[128,1024]{1,0:T(8,128)(2,1)S(1)} %collective-permute-done.7.refs_5_), channel_id=1, source_target_pairs={{0,1},{1,0},{2,3},{3,2},{4,5},{5,4},{6,7},{7,6},{8,9},{9,8},{10,11... | collective-permute-start | bytes 786440 | tf_op jit(solution)/shard_map/ppermute | solution.py:527
  97.0 2.2 %copy-start.7 = (bf16[256,8192]{1,0:T(8,128)(2,1)S(1)}, bf16[256,8192]{1,0:T(8,128)(2,1)}, u32[]{:S(2)}) copy-start(bf16[256,8192]{1,0:T(8,128)(2,1)} %copy-done.4) | copy-start | bytes 12582916
  99.2 2.2 %copy-start.10 = (bf16[256,8192]{1,0:T(8,128)(2,1)S(1)}, bf16[256,8192]{1,0:T(8,128)(2,1)}, u32[]{:S(2)}) copy-start(bf16[256,8192]{1,0:T(8,128)(2,1)} %copy-done.8) | copy-start | bytes 12582916
  101.4 2.2 %copy-start.15 = (bf16[256,8192]{1,0:T(8,128)(2,1)S(1)}, bf16[256,8192]{1,0:T(8,128)(2,1)}, u32[]{:S(2)}) copy-start(bf16[256,8192]{1,0:T(8,128)(2,1)} %copy-done.12) | copy-start | bytes 12582916
  103.6 1.6 copy-start.19
  105.2 3.7 %copy-start.32 = (bf16[128,1024]{1,0:T(8,128)(2,1)S(1)}, bf16[128,1024]{1,0:T(8,128)(2,1)}, u32[]{:S(2)}) copy-start(bf16[128,1024]{1,0:T(8,128)(2,1)} %copy-done.31) | copy-start | bytes 786436
  109.5 3.4 %copy-start.1 = (bf16[8192,512]{1,0:T(8,128)(2,1)}, bf16[8192,512]{1,0:T(8,128)(2,1)S(1)}, u32[]{:S(2)}) copy-start(bf16[8192,512]{1,0:T(8,128)(2,1)S(1)} %turn_hidden.1.refs_3_.refs_1_) | copy-start | bytes 25165828
  113.6 17.7 %all-to-all-start.2 = ((bf16[4,32,1024]{2,1,0:T(8,128)(2,1)}), bf16[4,32,1024]{2,1,0:T(8,128)(2,1)}, u32[]{:S(2)}, u32[]{:S(2)}) async-start(bf16[4,32,1024]{2,1,0:T(8,128)(2,1)} %copy-done.27), calls=%async_computation.2 | async-start | bytes 524288 | tf_op jit(solution)/shard_map/all_to_all | solution.py:534
  118.7 32.1 %copy-start.21 = (bf16[128,1024]{1,0:T(8,128)(2,1)}, bf16[128,1024]{1,0:T(8,128)(2,1)S(1)}, u32[]{:S(2)}) copy-start(bf16[128,1024]{1,0:T(8,128)(2,1)S(1)} %collective-permute-done.6.refs_2_) | copy-start | bytes 786436
  118.8 3.5 %copy-start.2 = (bf16[8192,512]{1,0:T(8,128)(2,1)S(1)}, bf16[8192,512]{1,0:T(8,128)(2,1)}, u32[]{:S(2)}) copy-start(bf16[8192,512]{1,0:T(8,128)(2,1)} %copy-done.1) | copy-start | bytes 25165828
  123.2 27.6 %copy-start.23 = (bf16[128,1024]{1,0:T(8,128)(2,1)}, bf16[128,1024]{1,0:T(8,128)(2,1)S(1)}, u32[]{:S(2)}) copy-start(bf16[128,1024]{1,0:T(8,128)(2,1)S(1)} %collective-permute-done.8.refs_3_) | copy-start | bytes 786436
  133.0 16.5 %all-to-all-start.3 = ((bf16[4,32,1024]{2,1,0:T(8,128)(2,1)}), bf16[4,32,1024]{2,1,0:T(8,128)(2,1)S(1)}, u32[]{:S(2)}, u32[]{:S(2)}) async-start(bf16[4,32,1024]{2,1,0:T(8,128)(2,1)} %copy-done.25), calls=%async_computation.3 | async-start | bytes 524288 | tf_op jit(solution)/shard_map/all_to_all | solution.py:534
  138.1 3.4 %copy-start.3 = (bf16[8192,512]{1,0:T(8,128)(2,1)S(1)}, bf16[8192,512]{1,0:T(8,128)(2,1)}, u32[]{:S(2)}) copy-start(bf16[8192,512]{1,0:T(8,128)(2,1)} %copy-done.1) | copy-start | bytes 25165828
  150.0 8.1 %collective-permute-start.10 = (bf16[128,1024]{1,0:T(8,128)(2,1)S(1)}, bf16[128,1024]{1,0:T(8,128)(2,1)S(1)}, u32[]{:S(2)}, u32[]{:S(2)}) collective-permute-start(bf16[128,1024]{1,0:T(8,128)(2,1)S(1)} %hold.5.refs_6_.refs_8_.refs_4_), channel_id=1, source_target_pairs={{0,2},{2,0},{4,6},{6,4},{8,10},{10,8},{12,14},{14,12},{1,3},{3,1},... | collective-permute-start | bytes 786440 | tf_op jit(solution)/shard_map/ppermute | solution.py:530
  150.8 17.9 %collective-permute-start.9 = (bf16[128,1024]{1,0:T(8,128)(2,1)S(1)}, bf16[128,1024]{1,0:T(8,128)(2,1)S(1)}, u32[]{:S(2)}, u32[]{:S(2)}) collective-permute-start(bf16[128,1024]{1,0:T(8,128)(2,1)S(1)} %hold.5.refs_6_.refs_8_.refs_4_), channel_id=1, source_target_pairs={{0,1},{1,0},{2,3},{3,2},{4,5},{5,4},{6,7},{7,6},{8,9},{9,8},{10,11... | collective-permute-start | bytes 786440 | tf_op jit(solution)/shard_map/ppermute | solution.py:527
  158.1 10.6 %copy-start.11 = (bf16[256,8192]{1,0:T(8,128)(2,1)S(1)}, bf16[256,8192]{1,0:T(8,128)(2,1)}, u32[]{:S(2)}) copy-start(bf16[256,8192]{1,0:T(8,128)(2,1)} %copy-done.8) | copy-start | bytes 12582916
  158.2 10.5 %collective-permute-start.11 = (bf16[128,1024]{1,0:T(8,128)(2,1)S(1)}, bf16[128,1024]{1,0:T(8,128)(2,1)S(1)}, u32[]{:S(2)}, u32[]{:S(2)}) collective-permute-start(bf16[128,1024]{1,0:T(8,128)(2,1)S(1)} %collective-permute-done.10.refs_9_.refs_5_), channel_id=1, source_target_pairs={{0,1},{1,0},{2,3},{3,2},{4,5},{5,4},{6,7},{7,6},{8,9},{9,8},{10,11... | collective-permute-start | bytes 786440 | tf_op jit(solution)/shard_map/ppermute | solution.py:527
  158.7 1.2 copy-start.22
  168.7 8.8 %copy-start.20 = (bf16[256,4096]{1,0:T(8,128)(2,1)S(1)}, bf16[256,4096]{1,0:T(8,128)(2,1)}, u32[]{:S(2)}) copy-start(bf16[256,4096]{1,0:T(8,128)(2,1)} %copy-done.18) | copy-start | bytes 6291460
  177.4 12.0 %slice-start = ((s8[8388608]{0:T(1024)(128)(4,1)}), s8[4194304]{0:T(1024)(128)(4,1)S(1)}, s32[]{:S(2)}) async-start(s8[8388608]{0:T(1024)(128)(4,1)} %bitcast.6), calls=%async_computation.4 | async-start | bytes 8388608
  177.4 11.9 %slice-start.1 = ((s8[8388608]{0:T(1024)(128)(4,1)}), s8[4194304]{0:T(1024)(128)(4,1)S(1)}, s32[]{:S(2)}) async-start(s8[8388608]{0:T(1024)(128)(4,1)} %bitcast.6), calls=%async_computation.5 | async-start | bytes 8388608
  188.2 8.3 %collective-permute-start.13 = (bf16[256,4096]{1,0:T(8,128)(2,1)S(1)}, bf16[256,4096]{1,0:T(8,128)(2,1)S(1)}, u32[]{:S(2)}, u32[]{:S(2)}) collective-permute-start(bf16[256,4096]{1,0:T(8,128)(2,1)S(1)} %get-tuple-element.45.refs_6_), channel_id=1, source_target_pairs={{0,1},{1,0},{2,3},{3,2},{4,5},{5,4},{6,7},{7,6},{8,9},{9,8},{10,11... | collective-permute-start | bytes 6291464 | tf_op jit(solution)/shard_map/ppermute | solution.py:527
  188.3 8.2 %collective-permute-start.12 = (bf16[256,4096]{1,0:T(8,128)(2,1)S(1)}, bf16[256,4096]{1,0:T(8,128)(2,1)S(1)}, u32[]{:S(2)}, u32[]{:S(2)}) collective-permute-start(bf16[256,4096]{1,0:T(8,128)(2,1)S(1)} %get-tuple-element.46), channel_id=1, source_target_pairs={{0,1},{1,0},{2,3},{3,2},{4,5},{5,4},{6,7},{7,6},{8,9},{9,8},{10,11... | collective-permute-start | bytes 6291464 | tf_op jit(solution)/shard_map/ppermute | solution.py:527
  (8 other events, 7.4 us)

commit v5 on v4

--- a/solution.py
+++ b/solution.py
@@ -10,22 +10,25 @@
 NT = (((1,), (1,)), ((), ()))
 
 
-def call(body, name, at, ins, outs, scratch=(), flops=0, aliases=None, mib=4, after=()):
+def call(body, name, at, ins, outs, scratch=(), flops=0, aliases=None, mib=4, after=(), us=0.6, carry=()):
     specs = {"v": pl.BlockSpec(memory_space=pltpu.VMEM), "h": pl.BlockSpec(memory_space=pl.ANY)}
     spaces = {"v": pltpu.VMEM, "h": pltpu.HBM}
-    nbytes = sum(a.size * a.dtype.itemsize for a, _ in ins)
-    skip = 1 + len(ins)
-    ins = list(ins) + [a if isinstance(a, tuple) else (a, "v") for a in after]
+    skip, n_outs = 1 + len(ins), len(outs)
+    ins = list(ins) + [(a, "v") for a in carry] + [a if isinstance(a, tuple) else (a, "v") for a in after]
+    outs = list(outs) + [(a.shape, a.dtype, "v") for a in carry]
+    aliases = dict(aliases or {})
+    aliases.update({skip + i: n_outs + i for i in range(len(carry))})
     args = [pltpu.with_memory_space_constraint(a, spaces[w]) for a, w in ins]
+    first = skip + len(carry) + len(after)
     return pl.pallas_call(
-        lambda *refs: body(*refs[:skip], *refs[skip + len(after) :]),
+        lambda *refs: body(*refs[:skip], *refs[first : first + n_outs], *refs[first + len(outs) :]),
         out_shape=tuple(spaces[w](dims, dtype) for dims, dtype, w in outs),
         in_specs=[pl.BlockSpec(memory_space=pltpu.SMEM)] + [specs[w] for _, w in ins],
         out_specs=tuple(specs[w] for _, _, w in outs),
         scratch_shapes=list(scratch),
-        input_output_aliases=aliases or {},
+        input_output_aliases=aliases,
         compiler_params=pltpu.CompilerParams(vmem_limit_bytes=mib * MIB),
-        cost_estimate=pl.CostEstimate(flops=int(flops), bytes_accessed=int(nbytes), transcendentals=0),
+        cost_estimate=pl.CostEstimate(flops=int(1.7 * flops + us * 1.15e9), bytes_accessed=0, transcendentals=0),
         name=name,
     )(at, *args)
 
@@ -153,12 +156,12 @@
     return (c.astype(F32) * x.astype(F32)).astype(BF)
 
 
-def back_project(at, s, x, x_o, c, c_o, u, so_far, after=(), tk=1024):
+def back_project(at, s, x, x_o, c, c_o, u, so_far, after=(), tk=512):
     rows, (half, rank) = x.shape[0], u.shape
     part = half // 2
     tk = min(tk, part)
     n = part // tk
-    slots = min(2, n)
+    slots = min(4, n)
     first = so_far is None
 
     def body(at_ref, x_ref, xo_ref, c_ref, co_ref, u_ref, *rest):
@@ -224,49 +227,48 @@
         + ([] if first else [whole])
         + [dma(n), dma(slots)],
         flops=2 * rows * half * rank,
-        mib=16,
+        mib=12,
         after=after,
     )
 
 
-def turn_x(at, x, x_o, after=()):
+def turn_x(at, x, after=()):
     rows, half = x.shape
     tw = min(512, half)
 
-    def body(at_ref, x_ref, xo_ref, o_ref):
+    def body(at_ref, x_ref, o_ref):
         @pl.loop(0, half // tw)
         def _(k):
             here = at_block(k, tw)
-            o_ref[here, :rows] = x_ref[:, here].T
-            o_ref[here, rows:] = xo_ref[:, here].T
-
-    return call(body, "turn_x", at, [(x, "v"), (x_o, "v")], [((half, 2 * rows), BF, "v")], mib=6, after=after)[0]
-
-
-def turn_hidden(at, x, x_o, cs, c_o, after=()):
+            o_ref[here, :] = x_ref[:, here].T
+
+    return call(body, "turn_x", at, [(x, "v")], [((half, rows), BF, "v")], after=after, us=1.8)[0]
+
+
+def turn_hidden(at, s, x, x_o, c, c_o, after=(), carry=()):
     rows, half = x.shape
     part = half // 2
     tw = min(512, part)
 
-    def body(at_ref, x_ref, xo_ref, c0_ref, c1_ref, co_ref, o_ref):
-        for s, c_ref in enumerate((c0_ref, c1_ref)):
-
-            @pl.loop(0, part // tw)
-            def _(k):
-                here = at_block(k, tw)
-                there = pl.ds(pl.multiple_of(s * part + k * tw, tw), tw)
-                o_ref[there, :rows] = hidden(c_ref[:, here], x_ref[:, there]).T
-                o_ref[there, rows:] = hidden(co_ref[:, there], xo_ref[:, there]).T
+    def body(at_ref, x_ref, xo_ref, c_ref, co_ref, o_ref):
+        @pl.loop(0, part // tw)
+        def _(k):
+            here = at_block(k, tw)
+            there = pl.ds(pl.multiple_of(s * part + k * tw, tw), tw)
+            o_ref[here, :rows] = hidden(c_ref[:, here], x_ref[:, there]).T
+            o_ref[here, rows:] = hidden(co_ref[:, there], xo_ref[:, there]).T
 
     return call(
         body,
         "turn_hidden",
         at,
-        [(a, "v") for a in (x, x_o, *cs, c_o)],
-        [((half, 2 * rows), BF, "v")],
+        [(a, "v") for a in (x, x_o, c, c_o)],
+        [((part, 2 * rows), BF, "v")],
         mib=6,
         after=after,
-    )[0]
+        us=1.8,
+        carry=carry,
+    )
 
 
 def fill(at_ref, both, refs):
@@ -282,16 +284,17 @@
         both[at_block(2 * i + 1 - bit, each), :] = other[...]
 
 
-def factor_grad(at, name, s, turned, p, so_far, placed=None, after=(), tw=1024):
-    half, rows2 = turned.shape
-    rank = p[0].shape[1]
+def factor_grad(at, name, s, half, turned, p, so_far, placed=None, after=(), tw=1024):
+    rows2, rank = sum(a.shape[0] for a in p), p[0].shape[1]
     part = half // 2
+    shift = s * part if turned[0].shape[0] == half else 0
+    nt = len(turned)
     tw = min(tw, part)
     n = part // tw
     np_ = len(p)
     recv, full = placed or ((), None)
     nr = len(recv)
-    ins = [(turned, "v")] + [(a, "v") for a in p]
+    ins = [(a, "v") for a in (*turned, *p)]
     aliases = {}
     if so_far is not None:
         aliases[1 + len(ins)] = 0
@@ -301,7 +304,8 @@
         aliases[1 + len(ins)] = 1
         ins.append((full, "h"))
 
-    def body(at_ref, t_ref, *refs):
+    def body(at_ref, *refs):
+        t_refs, refs = refs[:nt], refs[nt:]
         p_refs, refs = refs[:np_], refs[np_ + (so_far is not None) :]
         r_refs, refs = refs[:nr], refs[nr + (nr > 0) :]
         o_ref, refs = refs[0], refs[1:]
@@ -330,8 +334,12 @@
             def _():
                 out(k, slot).wait()
 
-            left = t_ref[pl.ds(pl.multiple_of(s * part + k * tw, tw), tw), :]
-            stage[slot] = jnp.dot(left, both[...], preferred_element_type=F32).astype(BF)
+            here = pl.ds(pl.multiple_of(shift + k * tw, tw), tw)
+            each = rows2 // nt
+            parts = [
+                jnp.dot(t_refs[i][here, :], both[i * each : (i + 1) * each, :], preferred_element_type=F32) for i in range(nt)
+            ]
+            stage[slot] = sum(parts[1:], parts[0]).astype(BF)
             out(k, slot).start()
 
         for k in range(max(0, n - 2), n):
@@ -349,7 +357,7 @@
         [pltpu.VMEM((2, tw, rank), BF), pltpu.VMEM((rows2, rank), BF), dma(2), dma(max(1, nr))],
         flops=rows2 * half * rank,
         aliases=aliases,
-        mib=16,
+        mib=12,
         after=after,
     )
 
@@ -467,7 +475,7 @@
         ],
         flops=2 * rows * half * rank,
         aliases=aliases,
-        mib=16,
+        mib=12,
         after=after,
     )
 
@@ -485,30 +493,37 @@
     return call(body, "pair_halves", at, [(a, "v"), (b, "v")], halves_of(rows, rank, direct), after=after)
 
 
-def pieces_of(at, a, b, m, after=()):
+def pieces_of(at, a, b, m, after=(), carry=()):
     rows, rank = a.shape
     each = rows // m
 
-    def body(at_ref, a_ref, b_ref, o_ref):
-        for j in range(m):
-            here = slice(j * each, (j + 1) * each)
-            o_ref[j] = plus(a_ref[here, :], b_ref[here, :]).astype(BF)
-
-    return call(body, "pieces_of", at, [(a, "v"), (b, "v")], [((m, each, rank), BF, "v")], after=after)[0]
-
-
-def add_pieces(at, parts, after=()):
-    m = parts.shape[0]
-
-    def body(at_ref, a_ref, o_ref):
-        total = a_ref[0].astype(F32)
-        for j in range(1, m):
-            total += a_ref[j].astype(F32)
-        total = total.astype(BF)
-        for j in range(m):
-            o_ref[j] = total
-
-    return call(body, "add_pieces", at, [(parts, "v")], [(parts.shape, BF, "v")], after=after)[0]
+    def body(at_ref, a_ref, b_ref, *outs):
+        for d in range(m):
+            here = at_block((at_ref[1] >> 1) ^ d, each)
+            outs[d][...] = plus(a_ref[here, :], b_ref[here, :]).astype(BF)
+
+    return call(body, "pieces_of", at, [(a, "v"), (b, "v")], [((each, rank), BF, "v")] * m, after=after, carry=carry)
+
+
+def add_pieces(at, parts, after=(), carry=()):
+    def body(at_ref, *refs):
+        total = refs[0][...].astype(F32)
+        for r in refs[1:-1]:
+            total += r[...].astype(F32)
+        refs[-1][...] = total.astype(BF)
+
+    return call(body, "add_pieces", at, [(a, "v") for a in parts], [(parts[0].shape, BF, "v")], after=after, carry=carry)
+
+
+def join_pieces(at, parts, after=()):
+    m = len(parts)
+    each, rank = parts[0].shape
+
+    def body(at_ref, *refs):
+        for d in range(m):
+            refs[-1][at_block((at_ref[1] >> 1) ^ d, each), :] = refs[d][...]
+
+    return call(body, "join_pieces", at, [(a, "v") for a in parts], [((m * each, rank), BF, "v")], after=after)[0]
 
 
 def hold(at, a, after):
@@ -530,15 +545,7 @@
         return lax.ppermute(a, "col", [(i, i ^ d) for i in range(n)])
 
     def spread(parts):
-        groups = [[bit + 2 * j for j in range(m)] for bit in range(2)]
-        return lax.all_to_all(parts, "col", split_axis=0, concat_axis=0, axis_index_groups=groups, tiled=True)
-
-    def whole(parts):
-        return parts.reshape(-1, parts.shape[-1])
-
-    def ends(half):
-        other = to(half, 1)
-        return [trade(half), trade(other), half, other]
+        return [parts[0]] + [to(parts[d], 2 * d) for d in range(1, m)]
 
     def local(x, c, u, v, bias):
         half, width = u.shape[0], x.shape[1]
@@ -554,42 +561,45 @@
         x_o = trade(x_s)
         own, x_own, c_s, *v_in = project_own(at, x, v, c, [x_s])
         theirs = trade(own)
-        c_o = trade(hold(at, c_s, [theirs]))
+        x_t = turn_x(at, x_own)
+        c_o = trade(hold(at, c_s, [theirs, x_t]))
         sums = project_other(at, x_o, v_in, theirs, direct)
-        acc, b0, c0 = back_project(at, 0, x_own, x_o, c, c_o, u, None, [sums[0]])
+        x_t = [x_t, turn_x(at, x_o, [sums[0]])]
+        acc, b0, c0 = back_project(at, 0, x_own, x_o, c, c_o, u, None, x_t)
         if direct:
             parts = pieces_of(at, sums[0], to(sums[1], 1), m, [acc])
-            own_g, mine_g, b1, c1 = back_project(at, 1, x_own, x_o, c, c_o, u, acc, [parts])
-            theirs_g = trade(own_g)
-            total = add_pieces(at, spread(parts), [own_g])
-            x_t = turn_x(at, x_own, x_o, [total])
-            sums_g = pair_halves(at, mine_g, theirs_g, direct, [x_t])
-            half_p = hold(at, whole(spread(total)), [sums_g[0]])
-            p = ends(half_p)
-            h_t = turn_hidden(at, x_own, x_o, (c0, c1), c_o, [half_p])
-            parts_g = pieces_of(at, sums_g[0], to(sums_g[1], 1), m, [h_t])
-            (grad_u,) = factor_grad(at, "u_grad", 0, h_t, p, None, after=[parts_g], tw=512)
-            total_g = add_pieces(at, spread(parts_g), [(grad_u, "h")])
-            (grad_u,) = factor_grad(at, "u_grad", 1, h_t, p, grad_u, after=[total_g])
-            half_g = hold(at, whole(spread(total_g)), [(grad_u, "h")])
-            g = ends(half_g)
+            own_g, mine_g, b1, c1 = back_project(at, 1, x_own, x_o, c, c_o, u, acc, [parts[0]])
+            total, own_g = add_pieces(at, spread(parts), carry=[own_g])
+            (h_t0,) = turn_hidden(at, 0, x_own, x_o, c0, c_o, [total])
+            sums_g = pair_halves(at, mine_g, trade(own_g), direct, [h_t0])
+            half_p = join_pieces(at, spread([total] * m), [sums_g[0]])
+            other_p = to(half_p, 1)
+            *parts_g, other_p = pieces_of(at, sums_g[0], to(sums_g[1], 1), m, [half_p], carry=[other_p])
+            (h_t1,) = turn_hidden(at, 1, x_own, x_o, c1, c_o, [parts_g[0]])
+            p = [trade(half_p), trade(other_p), half_p, other_p]
+            (grad_u,) = factor_grad(at, "u_grad", 0, half, [h_t0], p, None, after=[h_t1])
+            (total_g,) = add_pieces(at, spread(parts_g), [(grad_u, "h")])
+            (grad_u,) = factor_grad(at, "u_grad", 1, half, [h_t1], p, grad_u, after=[total_g])
+            half_g = join_pieces(at, spread([total_g] * m), [(grad_u, "h")])
+            other_g = to(half_g, 1)
             ex0 = expand(at, 0, u, p, [half_g])
-            ex1 = expand(at, 1, u, p, [ex0], tw=512)
+            g = [trade(half_g), trade(other_g), half_g, other_g]
+            ex1 = expand(at, 1, u, p, [ex0])
         else:
             own_g, mine_g, b1, c1 = back_project(at, 1, x_own, x_o, c, c_o, u, acc)
             (sums_g,) = pair_halves(at, mine_g, trade(own_g), direct)
             p, g = plain(sums[0]), plain(sums_g)
-            x_t = turn_x(at, x_own, x_o)
-            h_t = turn_hidden(at, x_own, x_o, (c0, c1), c_o)
-            (grad_u,) = factor_grad(at, "u_grad", 0, h_t, p, None)
-            (grad_u,) = factor_grad(at, "u_grad", 1, h_t, p, grad_u)
+            (h_t0,) = turn_hidden(at, 0, x_own, x_o, c0, c_o)
+            (h_t1,) = turn_hidden(at, 1, x_own, x_o, c1, c_o)
+            (grad_u,) = factor_grad(at, "u_grad", 0, half, [h_t0], p, None)
+            (grad_u,) = factor_grad(at, "u_grad", 1, half, [h_t1], p, grad_u)
             ex0, ex1 = expand(at, 0, u, p), expand(at, 1, u, p)
         bias = bias[None, :]
         out, oth0 = input_grad(at, 0, c0, c_o, ex0, v, bias, g, None, width, [ex1])
-        out, oth1 = input_grad(at, 1, c1, c_o, ex1, v, bias, g, out, width, tw=512)
+        out, oth1 = input_grad(at, 1, c1, c_o, ex1, v, bias, g, out, width)
         back = [trade(oth0), trade(oth1)]
-        (grad_v,) = factor_grad(at, "v_grad", 0, x_t, g, None, after=[oth1])
-        grad_v, out = factor_grad(at, "v_grad", 1, x_t, g, grad_v, (back, out))
+        (grad_v,) = factor_grad(at, "v_grad", 0, half, x_t, g, None, after=[oth1])
+        grad_v, out = factor_grad(at, "v_grad", 1, half, x_t, g, grad_v, (back, out))
         return out, grad_u, grad_v, jnp.concatenate([b0[0], b1[0]])
 
     return jax.shard_map(

time: 205 us -> 151 us (0.74)
  local copies, waits for them, and re-layouts: 44.1 us -> 0.04 us
  Pallas kernels: 116 us -> 110 us
  starting transfers between devices: 28.2 us -> 25.5 us
    unnamed x76 -> x2, local copies, waits for them, and re-layouts: 44.1 us -> 0.01 us
    all_to_all x4 -> x0, starting transfers between devices: 20.2 us -> none  [spread(): lax.all_to_all(parts, 'col', split_axis=0, concat_axis=0, axis_index_grou...]
    ppermute x4 -> x16, starting transfers between devices: 5.8 us -> 23.1 us  [to(): return lax.ppermute(a, 'col', [(i, i ^ d) for i in range(n)])]
    ppermute x10, waiting for transfers between devices: 6.49 us -> 0.03 us  [trade(): return lax.ppermute(a, 'batch', swap)]
    ppermute x4 -> x16, waiting for transfers between devices: 7.17 us -> 13.6 us  [to(): return lax.ppermute(a, 'col', [(i, i ^ d) for i in range(n)])]
    pallas_call x23 -> x25, Pallas kernels: 116 us -> 110 us  [call(): pl.pallas_call(lambda *refs: body(*refs[:skip], *refs[first:first + n_out...]
  transfers between devices with their start and end apart: 18 -> 26, of which waited for: 3 -> 4; matrix products, arithmetic and copies ran while one was open for 0% -> 0% of each run, Pallas kernels for 36% -> 53%
where the time goes in v5:
time: 151 us
  Pallas kernels  110 us (73%)
  starting transfers between devices  25.5 us (17%)
  waiting for transfers between devices  13.6 us (9%)
    pallas_call x25, Pallas kernels, call(): pl.pallas_call(lambda *refs: body(*refs[:skip], *refs[first:first + n_out...  110 us
    ppermute x16, starting transfers between devices, to(): return lax.ppermute(a, 'col', [(i, i ^ d) for i in range(n)])  23.1 us
    ppermute x16, waiting for transfers between devices, to(): return lax.ppermute(a, 'col', [(i, i ^ d) for i in range(n)])  13.6 us
  transfers between devices with their start and end apart: 26, of which 4 were waited for; matrix products, arithmetic and copies ran while one was open for 0% of the time, Pallas kernels for 53%

profile of v5, /device:TPU:0, one launch (start us, length us, event | category | flops | bytes accessed | tf_op | source)
XLA Modules:
  0.0 150.6 jit_solution(16892350148403637982)
XLA Ops:
  0.7 2.8 %cut_half.1.refs_4_ = bf16[256,8192]{1,0:T(8,128)(2,1)S(1)} custom-call(s32[2]{0:T(128)S(1)} %pad_add_fusion.refs_0_, bf16[256,16384]{1,0:T(8,128)(2,1)} %refs_1_.5), custom_call_target="tpu_custom_call" | custom-call | flops 690000000 | tf_op jit(solution)/shard_map/cut_half/pallas_call | solution.py:23
  3.5 0.5 collective-permute-start
  4.0 9.9 %project_own.1 = (bf16[256,1024]{1,0:T(8,128)(2,1)S(1)}, bf16[256,8192]{1,0:T(8,128)(2,1)S(1)}, bf16[256,8192]{1,0:T(8,128)(2,1)S(1)}, bf16[2048,1024]{1,0:T(8,1...) custom-call(s32[2]{0:T(128)S(1)} %pad_add_fusion.refs_0_, ...), custom_call_target="tpu_custom_call" | custom-call | flops 7991444480 | tf_op jit(solution)/shard_map/project_own/pallas_call | solution.py:23
  14.0 2.7 %turn_x.2.refs_3_.refs_6_.refs_1_ = bf16[8192,256]{1,0:T(8,128)(2,1)S(1)} custom-call(s32[2]{0:T(128)S(1)} %pad_add_fusion.refs_0_, bf16[256,8192]{1,0:T(8,128)(2,1)S(1)} %get-tuple-element.39.refs_1_), custom_call_target="tpu_custom_call" | custom-call | flops 2070000000 | tf_op jit(solution)/shard_map/turn_x/pallas_call | solution.py:23
  16.7 0.5 hold.1
  17.3 0.5 collective-permute-start.2
  17.8 5.2 %project_other.1 = (bf16[128,1024]{1,0:T(8,128)(2,1)S(1)}, bf16[128,1024]{1,0:T(8,128)(2,1)S(1)}) custom-call(s32[2]{0:T(128)S(1)} %pad_add_fusion.refs_0_, bf16[256,8192]{1,0:T(8,128)(2,1)S(1)} %collective-permute-done.refs_1_.refs_2_, bf16[256,1024]{1,0:T(8,128)(2,1)S(1)} %collective-permute-done.1.refs_2_, ...), custom_call_target="tpu_custom_call" | custom-call | flops 7991444480 | tf_op jit(solution)/shard_map/project_other/pallas_call | solution.py:23
  23.0 2.6 %collective-permute-start.3 = (bf16[128,1024]{1,0:T(8,128)(2,1)S(1)}, bf16[128,1024]{1,0:T(8,128)(2,1)S(1)}, u32[]{:S(2)}, u32[]{:S(2)}) collective-permute-start(bf16[128,1024]{1,0:T(8,128)(2,1)S(1)} %get-tuple-element.48), channel_id=1, source_target_pairs={{0,2},{2,0},{4,6},{6,4},{8,10},{10,8},{12,14},{14,12},{1,3},{3,1},... | collective-permute-start | bytes 786440 | tf_op jit(solution)/shard_map/ppermute | solution.py:545
  25.6 2.5 %turn_x.3.refs_7_.refs_2_ = bf16[8192,256]{1,0:T(8,128)(2,1)S(1)} custom-call(s32[2]{0:T(128)S(1)} %pad_add_fusion.refs_0_, bf16[256,8192]{1,0:T(8,128)(2,1)S(1)} %collective-permute-done.refs_1_.refs_2_, bf16[128,1024]{1,0:T(8,128)(2,1)S(1)} %get-tuple-element.45.refs_2_.refs_1_), custom_call_target="tpu_custom_call" | custom-call | flops 2070000000 | tf_op jit(solution)/shard_map/turn_x/pallas_call | solution.py:23
  28.1 8.8 %back_project.2 = (f32[512,1024]{1,0:T(8,128)S(1)}, f32[1,4096]{1,0:T(1,128)S(1)}, bf16[256,4096]{1,0:T(8,128)(2,1)S(1)}) custom-call(s32[2]{0:T(128)S(1)} %pad_add_fusion.refs_0_, bf16[256,8192]{1,0:T(8,128)(2,1)S(1)} %get-tuple-element.39.refs_1_, bf16[256,8192]{1,0:T(8,128)(2,1)S(1)} %collective-permute-done.refs_1_.refs_2_, bf16[256,16384]{1,0:T(8,128)(2,1)} %refs_3_.5, ...), custom_call_target="tpu_custom_call" | custom-call | flops 7991444480 | tf_op jit(solution)/shard_map/back_project/pallas_call | solution.py:23
  36.9 0.6 pieces_of.2
  37.5 1.6 %collective-permute-start.4 = (bf16[32,1024]{1,0:T(8,128)(2,1)S(1)}, bf16[32,1024]{1,0:T(8,128)(2,1)S(1)}, u32[]{:S(2)}, u32[]{:S(2)}) collective-permute-start(bf16[32,1024]{1,0:T(8,128)(2,1)S(1)} %get-tuple-element.51), channel_id=1, source_target_pairs={{0,4},{2,6},{4,0},{6,2},{8,12},{10,14},{12,8},{14,10},{1,5},{3,7},... | collective-permute-start | bytes 196616 | tf_op jit(solution)/shard_map/ppermute | solution.py:545
  39.2 2.6 %collective-permute-start.5 = (bf16[32,1024]{1,0:T(8,128)(2,1)S(1)}, bf16[32,1024]{1,0:T(8,128)(2,1)S(1)}, u32[]{:S(2)}, u32[]{:S(2)}) collective-permute-start(bf16[32,1024]{1,0:T(8,128)(2,1)S(1)} %get-tuple-element.52), channel_id=1, source_target_pairs={{0,8},{2,10},{4,12},{6,14},{8,0},{10,2},{12,4},{14,6},{1,9},{3,11}... | collective-permute-start | bytes 196616 | tf_op jit(solution)/shard_map/ppermute | solution.py:545
  41.8 0.2 collective-permute-start.6
  42.0 8.4 %back_project.3 = (bf16[256,1024]{1,0:T(8,128)(2,1)S(1)}, f32[256,1024]{1,0:T(8,128)S(1)}, f32[1,4096]{1,0:T(1,128)S(1)}, bf16[256,4096]{1,0:T(8,128)(2,1)S(1)}) custom-call(s32[2]{0:T(128)S(1)} %pad_add_fusion.refs_0_, bf16[256,8192]{1,0:T(8,128)(2,1)S(1)} %get-tuple-element.39.refs_1_, bf16[256,8192]{1,0:T(8,128)(2,1)S(1)} %collective-permute-done.refs_1_.refs_2_, ...), custom_call_target="tpu_custom_call" | custom-call | flops 7991444480 | tf_op jit(solution)/shard_map/back_project/pallas_call | solution.py:23
  50.4 0.6 add_pieces.2
  51.1 3.7 %collective-permute-start.11 = (bf16[32,1024]{1,0:T(8,128)(2,1)S(1)}, bf16[32,1024]{1,0:T(8,128)(2,1)S(1)}, u32[]{:S(2)}, u32[]{:S(2)}) collective-permute-start(bf16[32,1024]{1,0:T(8,128)(2,1)S(1)} %get-tuple-element.57.refs_5_.refs_1_), channel_id=1, source_target_pairs={{0,12},{2,14},{4,8},{6,10},{8,4},{10,6},{12,0},{14,2},{1,13},{3,15... | collective-permute-start | bytes 196616 | tf_op jit(solution)/shard_map/ppermute | solution.py:545
  54.7 0.8 collective-permute-start.9
  55.5 2.1 %turn_hidden.2.refs_3_.refs_1_ = bf16[4096,512]{1,0:T(8,128)(2,1)S(1)} custom-call(s32[2]{0:T(128)S(1)} %pad_add_fusion.refs_0_, bf16[256,8192]{1,0:T(8,128)(2,1)S(1)} %get-tuple-element.39.refs_1_, bf16[256,8192]{1,0:T(8,128)(2,1)S(1)} %collective-permute-done.refs_1_.refs_2_, bf16[256,4096]{1,0:T(8,128)(2,1)S(1)} %get-tuple-element.56.refs_3_.refs_1_, ...), custom_call_target="tpu_custom_call" | custom-call | flops 2070000000 | tf_op jit(solution)/shard_map/turn_hidden/pallas_call | solution.py:23
  57.7 0.6 pair_halves.1
  58.3 2.0 %collective-permute-done.10.refs_3_ = bf16[32,1024]{1,0:T(8,128)(2,1)S(1)} collective-permute-done((bf16[32,1024]{1,0:T(8,128)(2,1)S(1)}, bf16[32,1024]{1,0:T(8,128)(2,1)S(1)}, u32[]{:S(2)}, u32[]{:S(2)}) %collective-permute-start.10) | collective-permute-done | bytes 65568 | tf_op jit(solution)/shard_map/ppermute | solution.py:545
  60.3 0.1 collective-permute-done.9.refs_2_
  60.5 0.6 join_pieces.2.refs_4_
  61.0 0.5 collective-permute-start.12
  61.6 1.6 %collective-permute-start.8 = (bf16[128,1024]{1,0:T(8,128)(2,1)S(1)}, bf16[128,1024]{1,0:T(8,128)(2,1)S(1)}, u32[]{:S(2)}, u32[]{:S(2)}) collective-permute-start(bf16[128,1024]{1,0:T(8,128)(2,1)S(1)} %get-tuple-element.59), channel_id=1, source_target_pairs={{0,2},{2,0},{4,6},{6,4},{8,10},{10,8},{12,14},{14,12},{1,3},{3,1},... | collective-permute-start | bytes 786440 | tf_op jit(solution)/shard_map/ppermute | solution.py:545
  63.1 7.2 %collective-permute-done.12.refs_3_ = bf16[128,1024]{1,0:T(8,128)(2,1)S(1)} collective-permute-done((bf16[128,1024]{1,0:T(8,128)(2,1)S(1)}, bf16[128,1024]{1,0:T(8,128)(2,1)S(1)}, u32[]{:S(2)}, u32[]{:S(2)}) %collective-permute-start.12) | collective-permute-done | bytes 262176 | tf_op jit(solution)/shard_map/ppermute | solution.py:545
  70.3 4.2 %collective-permute-done.8.refs_2_ = bf16[128,1024]{1,0:T(8,128)(2,1)S(1)} collective-permute-done((bf16[128,1024]{1,0:T(8,128)(2,1)S(1)}, bf16[128,1024]{1,0:T(8,128)(2,1)S(1)}, u32[]{:S(2)}, u32[]{:S(2)}) %collective-permute-start.8) | collective-permute-done | bytes 262176 | tf_op jit(solution)/shard_map/ppermute | solution.py:545
  74.5 0.6 pieces_of.3
  75.3 1.7 %collective-permute-start.13 = (bf16[32,1024]{1,0:T(8,128)(2,1)S(1)}, bf16[32,1024]{1,0:T(8,128)(2,1)S(1)}, u32[]{:S(2)}, u32[]{:S(2)}) collective-permute-start(bf16[32,1024]{1,0:T(8,128)(2,1)S(1)} %get-tuple-element.61), channel_id=1, source_target_pairs={{0,4},{2,6},{4,0},{6,2},{8,12},{10,14},{12,8},{14,10},{1,5},{3,7},... | collective-permute-start | bytes 196616 | tf_op jit(solution)/shard_map/ppermute | solution.py:545
  77.0 1.7 %collective-permute-start.14 = (bf16[32,1024]{1,0:T(8,128)(2,1)S(1)}, bf16[32,1024]{1,0:T(8,128)(2,1)S(1)}, u32[]{:S(2)}, u32[]{:S(2)}) collective-permute-start(bf16[32,1024]{1,0:T(8,128)(2,1)S(1)} %get-tuple-element.62), channel_id=1, source_target_pairs={{0,8},{2,10},{4,12},{6,14},{8,0},{10,2},{12,4},{14,6},{1,9},{3,11}... | collective-permute-start | bytes 196616 | tf_op jit(solution)/shard_map/ppermute | solution.py:545
  78.7 1.0 collective-permute-start.15
  79.7 2.1 %turn_hidden.3.refs_6_.refs_1_ = bf16[4096,512]{1,0:T(8,128)(2,1)S(1)} custom-call(s32[2]{0:T(128)S(1)} %pad_add_fusion.refs_0_, bf16[256,8192]{1,0:T(8,128)(2,1)S(1)} %get-tuple-element.39.refs_1_, bf16[256,8192]{1,0:T(8,128)(2,1)S(1)} %collective-permute-done.refs_1_.refs_2_, bf16[256,4096]{1,0:T(8,128)(2,1)S(1)} %get-tuple-element.65.refs_3_.refs_1_, ...), custom_call_target="tpu_custom_call" | custom-call | flops 2070000000 | tf_op jit(solution)/shard_map/turn_hidden/pallas_call | solution.py:23
  81.9 7.1 %u_grad.2.refs_5_.refs_6_ = bf16[8192,1024]{1,0:T(8,128)(2,1)} custom-call(s32[2]{0:T(128)S(1)} %pad_add_fusion.refs_0_, bf16[4096,512]{1,0:T(8,128)(2,1)S(1)} %turn_hidden.2.refs_3_.refs_1_, bf16[128,1024]{1,0:T(8,128)(2,1)S(1)} %collective-permute-done.16.refs_2_, bf16[128,1024]{1,0:T(8,128)(2,1)S(1)} %collective-permute-done.17.refs_3_, ...), custom_call_target="tpu_custom_call" | custom-call | flops 7991444480 | tf_op jit(solution)/shard_map/u_grad/pallas_call | solution.py:23
  89.0 0.6 add_pieces.3.refs_7_.refs_1_
  89.5 2.9 %collective-permute-start.20 = (bf16[32,1024]{1,0:T(8,128)(2,1)S(1)}, bf16[32,1024]{1,0:T(8,128)(2,1)S(1)}, u32[]{:S(2)}, u32[]{:S(2)}) collective-permute-start(bf16[32,1024]{1,0:T(8,128)(2,1)S(1)} %add_pieces.3.refs_7_.refs_1_), channel_id=1, source_target_pairs={{0,12},{2,14},{4,8},{6,10},{8,4},{10,6},{12,0},{14,2},{1,13},{3,15... | collective-permute-start | bytes 196616 | tf_op jit(solution)/shard_map/ppermute | solution.py:545
  92.4 1.6 %collective-permute-start.18 = (bf16[32,1024]{1,0:T(8,128)(2,1)S(1)}, bf16[32,1024]{1,0:T(8,128)(2,1)S(1)}, u32[]{:S(2)}, u32[]{:S(2)}) collective-permute-start(bf16[32,1024]{1,0:T(8,128)(2,1)S(1)} %add_pieces.3.refs_7_.refs_1_), channel_id=1, source_target_pairs={{0,4},{2,6},{4,0},{6,2},{8,12},{10,14},{12,8},{14,10},{1,5},{3,7},... | collective-permute-start | bytes 196616 | tf_op jit(solution)/shard_map/ppermute | solution.py:545
  94.0 7.1 %u_grad.3.refs_5_ = bf16[8192,1024]{1,0:T(8,128)(2,1)} custom-call(s32[2]{0:T(128)S(1)} %pad_add_fusion.refs_0_, bf16[4096,512]{1,0:T(8,128)(2,1)S(1)} %turn_hidden.3.refs_6_.refs_1_, bf16[128,1024]{1,0:T(8,128)(2,1)S(1)} %collective-permute-done.16.refs_2_, bf16[128,1024]{1,0:T(8,128)(2,1)S(1)} %collective-permute-done.17.refs_3_, ...), custom_call_target="tpu_custom_call", output_to_operand_aliasing={{}: (6, {})} | custom-call | flops 7991444480 | tf_op jit(solution)/shard_map/u_grad/pallas_call | solution.py:23
  101.1 0.6 join_pieces.3.refs_6_.refs_8_.refs_5_
  101.7 0.6 collective-permute-start.22
  102.3 7.3 %expand.2.refs_6_.refs_3_ = f32[512,4096]{1,0:T(8,128)S(1)} custom-call(s32[2]{0:T(128)S(1)} %pad_add_fusion.refs_0_, bf16[8192,1024]{1,0:T(8,128)(2,1)} %refs_1_.7, bf16[128,1024]{1,0:T(8,128)(2,1)S(1)} %collective-permute-done.16.refs_2_, bf16[128,1024]{1,0:T(8,128)(2,1)S(1)} %collective-permute-done.17.refs_3_, bf16[128,1024]{1,0:T(8,128)(2,1)S(1)} %join_pieces.2.refs_4_, ...), custom_call_target="tpu_custom_call" | custom-call | flops 7991444480 | tf_op jit(solution)/shard_map/expand/pallas_call | solution.py:23
  109.6 0.6 collective-permute-start.23
  110.2 7.3 %expand.3.refs_10_.refs_3_ = f32[512,4096]{1,0:T(8,128)S(1)} custom-call(s32[2]{0:T(128)S(1)} %pad_add_fusion.refs_0_, bf16[8192,1024]{1,0:T(8,128)(2,1)} %refs_1_.7, bf16[128,1024]{1,0:T(8,128)(2,1)S(1)} %collective-permute-done.16.refs_2_, bf16[128,1024]{1,0:T(8,128)(2,1)S(1)} %collective-permute-done.17.refs_3_, ...), custom_call_target="tpu_custom_call" | custom-call | flops 7991444480 | tf_op jit(solution)/shard_map/expand/pallas_call | solution.py:23
  117.5 8.7 %input_grad.2 = (bf16[256,16384]{1,0:T(8,128)(2,1)}, bf16[256,4096]{1,0:T(8,128)(2,1)S(1)}) custom-call(s32[2]{0:T(128)S(1)} %pad_add_fusion.refs_0_, bf16[256,4096]{1,0:T(8,128)(2,1)S(1)} %get-tuple-element.56.refs_3_.refs_1_, bf16[256,8192]{1,0:T(8,128)(2,1)S(1)} %collective-permute-done.2.refs_4_.refs_2_, f32[512,4096]{1,0:T(8,128)S(1)} %expand.2.refs_6_.refs_3_, ...), custom_call_target="tpu_custom_call" | custom-call | flops 7991444480 | tf_op jit(solution)/shard_map/input_grad/pallas_call | solution.py:23
  126.3 8.8 %input_grad.3 = (bf16[256,16384]{1,0:T(8,128)(2,1)}, bf16[256,4096]{1,0:T(8,128)(2,1)S(1)}) custom-call(s32[2]{0:T(128)S(1)} %pad_add_fusion.refs_0_, bf16[256,4096]{1,0:T(8,128)(2,1)S(1)} %get-tuple-element.65.refs_3_.refs_1_, bf16[256,8192]{1,0:T(8,128)(2,1)S(1)} %collective-permute-done.2.refs_4_.refs_2_, ...), custom_call_target="tpu_custom_call", output_to_operand_aliasing={{0}: (10, {})} | custom-call | flops 7991444480 | tf_op jit(solution)/shard_map/input_grad/pallas_call | solution.py:23
  135.1 0.5 collective-permute-start.24
  135.6 0.6 pad_maximum_fusion
  136.2 7.1 %v_grad.2.refs_7_ = bf16[8192,1024]{1,0:T(8,128)(2,1)} custom-call(s32[2]{0:T(128)S(1)} %pad_add_fusion.refs_0_, bf16[8192,256]{1,0:T(8,128)(2,1)S(1)} %turn_x.2.refs_3_.refs_6_.refs_1_, bf16[8192,256]{1,0:T(8,128)(2,1)S(1)} %turn_x.3.refs_7_.refs_2_, bf16[128,1024]{1,0:T(8,128)(2,1)S(1)} %collective-permute-done.21.refs_6_.refs_3_, ...), custom_call_target="tpu_custom_call" | custom-call | flops 7991444480 | tf_op jit(solution)/shard_map/v_grad/pallas_call | solution.py:23
  143.3 7.1 %v_grad.3 = (bf16[8192,1024]{1,0:T(8,128)(2,1)}, bf16[256,16384]{1,0:T(8,128)(2,1)}) custom-call(s32[2]{0:T(128)S(1)} %pad_add_fusion.refs_0_, bf16[8192,256]{1,0:T(8,128)(2,1)S(1)} %turn_x.2.refs_3_.refs_6_.refs_1_, bf16[8192,256]{1,0:T(8,128)(2,1)S(1)} %turn_x.3.refs_7_.refs_2_, ...), custom_call_target="tpu_custom_call", output_to_operand_aliasing={{0}: (7, {}), {1}: (10, {})} | custom-call | flops 7991444480 | tf_op jit(solution)/shard_map/v_grad/pallas_call | solution.py:23
  (34 shorter events, 0.5 us)
Async XLA Ops:
  3.5 14.3 %collective-permute-start = (bf16[256,8192]{1,0:T(8,128)(2,1)S(1)}, bf16[256,8192]{1,0:T(8,128)(2,1)S(1)}, u32[]{:S(2)}, u32[]{:S(2)}) collective-permute-start(bf16[256,8192]{1,0:T(8,128)(2,1)S(1)} %cut_half.1.refs_4_), channel_id=1, source_target_pairs={{0,1},{1,0},{2,3},{3,2},{4,5},{5,4},{6,7},{7,6},{8,9},{9,8},{10,11... | collective-permute-start | bytes 12582920 | tf_op jit(solution)/shard_map/ppermute | solution.py:542
  13.9 2.8 %collective-permute-start.1 = (bf16[256,1024]{1,0:T(8,128)(2,1)S(1)}, bf16[256,1024]{1,0:T(8,128)(2,1)S(1)}, u32[]{:S(2)}, u32[]{:S(2)}) collective-permute-start(bf16[256,1024]{1,0:T(8,128)(2,1)S(1)} %get-tuple-element.40), channel_id=1, source_target_pairs={{0,1},{1,0},{2,3},{3,2},{4,5},{5,4},{6,7},{7,6},{8,9},{9,8},{10,11... | collective-permute-start | bytes 1572872 | tf_op jit(solution)/shard_map/ppermute | solution.py:542
  17.3 10.8 %collective-permute-start.2 = (bf16[256,8192]{1,0:T(8,128)(2,1)S(1)}, bf16[256,8192]{1,0:T(8,128)(2,1)S(1)}, u32[]{:S(2)}, u32[]{:S(2)}) collective-permute-start(bf16[256,8192]{1,0:T(8,128)(2,1)S(1)} %hold.1), channel_id=1, source_target_pairs={{0,1},{1,0},{2,3},{3,2},{4,5},{5,4},{6,7},{7,6},{8,9},{9,8},{10,11... | collective-permute-start | bytes 12582920 | tf_op jit(solution)/shard_map/ppermute | solution.py:542
  23.0 13.9 %collective-permute-start.3 = (bf16[128,1024]{1,0:T(8,128)(2,1)S(1)}, bf16[128,1024]{1,0:T(8,128)(2,1)S(1)}, u32[]{:S(2)}, u32[]{:S(2)}) collective-permute-start(bf16[128,1024]{1,0:T(8,128)(2,1)S(1)} %get-tuple-element.48), channel_id=1, source_target_pairs={{0,2},{2,0},{4,6},{6,4},{8,10},{10,8},{12,14},{14,12},{1,3},{3,1},... | collective-permute-start | bytes 786440 | tf_op jit(solution)/shard_map/ppermute | solution.py:545
  37.5 12.9 %collective-permute-start.4 = (bf16[32,1024]{1,0:T(8,128)(2,1)S(1)}, bf16[32,1024]{1,0:T(8,128)(2,1)S(1)}, u32[]{:S(2)}, u32[]{:S(2)}) collective-permute-start(bf16[32,1024]{1,0:T(8,128)(2,1)S(1)} %get-tuple-element.51), channel_id=1, source_target_pairs={{0,4},{2,6},{4,0},{6,2},{8,12},{10,14},{12,8},{14,10},{1,5},{3,7},... | collective-permute-start | bytes 196616 | tf_op jit(solution)/shard_map/ppermute | solution.py:545
  39.2 11.2 %collective-permute-start.5 = (bf16[32,1024]{1,0:T(8,128)(2,1)S(1)}, bf16[32,1024]{1,0:T(8,128)(2,1)S(1)}, u32[]{:S(2)}, u32[]{:S(2)}) collective-permute-start(bf16[32,1024]{1,0:T(8,128)(2,1)S(1)} %get-tuple-element.52), channel_id=1, source_target_pairs={{0,8},{2,10},{4,12},{6,14},{8,0},{10,2},{12,4},{14,6},{1,9},{3,11}... | collective-permute-start | bytes 196616 | tf_op jit(solution)/shard_map/ppermute | solution.py:545
  41.8 8.6 %collective-permute-start.6 = (bf16[32,1024]{1,0:T(8,128)(2,1)S(1)}, bf16[32,1024]{1,0:T(8,128)(2,1)S(1)}, u32[]{:S(2)}, u32[]{:S(2)}) collective-permute-start(bf16[32,1024]{1,0:T(8,128)(2,1)S(1)} %get-tuple-element.53), channel_id=1, source_target_pairs={{0,12},{2,14},{4,8},{6,10},{8,4},{10,6},{12,0},{14,2},{1,13},{3,15... | collective-permute-start | bytes 196616 | tf_op jit(solution)/shard_map/ppermute | solution.py:545
  51.0 6.7 %collective-permute-start.7 = (bf16[256,1024]{1,0:T(8,128)(2,1)S(1)}, bf16[256,1024]{1,0:T(8,128)(2,1)S(1)}, u32[]{:S(2)}, u32[]{:S(2)}) collective-permute-start(bf16[256,1024]{1,0:T(8,128)(2,1)S(1)} %get-tuple-element.55), channel_id=1, source_target_pairs={{0,1},{1,0},{2,3},{3,2},{4,5},{5,4},{6,7},{7,6},{8,9},{9,8},{10,11... | collective-permute-start | bytes 1572872 | tf_op jit(solution)/shard_map/ppermute | solution.py:542
  51.1 7.2 %collective-permute-start.11 = (bf16[32,1024]{1,0:T(8,128)(2,1)S(1)}, bf16[32,1024]{1,0:T(8,128)(2,1)S(1)}, u32[]{:S(2)}, u32[]{:S(2)}) collective-permute-start(bf16[32,1024]{1,0:T(8,128)(2,1)S(1)} %get-tuple-element.57.refs_5_.refs_1_), channel_id=1, source_target_pairs={{0,12},{2,14},{4,8},{6,10},{8,4},{10,6},{12,0},{14,2},{1,13},{3,15... | collective-permute-start | bytes 196616 | tf_op jit(solution)/shard_map/ppermute | solution.py:545
  54.7 5.6 %collective-permute-start.10 = (bf16[32,1024]{1,0:T(8,128)(2,1)S(1)}, bf16[32,1024]{1,0:T(8,128)(2,1)S(1)}, u32[]{:S(2)}, u32[]{:S(2)}) collective-permute-start(bf16[32,1024]{1,0:T(8,128)(2,1)S(1)} %get-tuple-element.57.refs_5_.refs_1_), channel_id=1, source_target_pairs={{0,8},{2,10},{4,12},{6,14},{8,0},{10,2},{12,4},{14,6},{1,9},{3,11}... | collective-permute-start | bytes 196616 | tf_op jit(solution)/shard_map/ppermute | solution.py:545
  54.7 5.7 %collective-permute-start.9 = (bf16[32,1024]{1,0:T(8,128)(2,1)S(1)}, bf16[32,1024]{1,0:T(8,128)(2,1)S(1)}, u32[]{:S(2)}, u32[]{:S(2)}) collective-permute-start(bf16[32,1024]{1,0:T(8,128)(2,1)S(1)} %get-tuple-element.57.refs_5_.refs_1_), channel_id=1, source_target_pairs={{0,4},{2,6},{4,0},{6,2},{8,12},{10,14},{12,8},{14,10},{1,5},{3,7},... | collective-permute-start | bytes 196616 | tf_op jit(solution)/shard_map/ppermute | solution.py:545
  57.6 17.6 %copy-start = (bf16[16384]{0:T(1024)(128)(2,1)S(1)}, bf16[16384]{0:T(1024)(128)(2,1)}, u32[]{:S(2)}) copy-start(bf16[16384]{0:T(1024)(128)(2,1)} %param.9) | copy-start | bytes 98308
  61.0 9.3 %collective-permute-start.12 = (bf16[128,1024]{1,0:T(8,128)(2,1)S(1)}, bf16[128,1024]{1,0:T(8,128)(2,1)S(1)}, u32[]{:S(2)}, u32[]{:S(2)}) collective-permute-start(bf16[128,1024]{1,0:T(8,128)(2,1)S(1)} %join_pieces.2.refs_4_), channel_id=1, source_target_pairs={{0,2},{2,0},{4,6},{6,4},{8,10},{10,8},{12,14},{14,12},{1,3},{3,1},... | collective-permute-start | bytes 786440 | tf_op jit(solution)/shard_map/ppermute | solution.py:545
  61.6 12.9 %collective-permute-start.8 = (bf16[128,1024]{1,0:T(8,128)(2,1)S(1)}, bf16[128,1024]{1,0:T(8,128)(2,1)S(1)}, u32[]{:S(2)}, u32[]{:S(2)}) collective-permute-start(bf16[128,1024]{1,0:T(8,128)(2,1)S(1)} %get-tuple-element.59), channel_id=1, source_target_pairs={{0,2},{2,0},{4,6},{6,4},{8,10},{10,8},{12,14},{14,12},{1,3},{3,1},... | collective-permute-start | bytes 786440 | tf_op jit(solution)/shard_map/ppermute | solution.py:545
  63.1 18.7 %collective-permute-start.16 = (bf16[128,1024]{1,0:T(8,128)(2,1)S(1)}, bf16[128,1024]{1,0:T(8,128)(2,1)S(1)}, u32[]{:S(2)}, u32[]{:S(2)}) collective-permute-start(bf16[128,1024]{1,0:T(8,128)(2,1)S(1)} %join_pieces.2.refs_4_), channel_id=1, source_target_pairs={{0,1},{1,0},{2,3},{3,2},{4,5},{5,4},{6,7},{7,6},{8,9},{9,8},{10,11... | collective-permute-start | bytes 786440 | tf_op jit(solution)/shard_map/ppermute | solution.py:542
  75.1 6.7 %collective-permute-start.17 = (bf16[128,1024]{1,0:T(8,128)(2,1)S(1)}, bf16[128,1024]{1,0:T(8,128)(2,1)S(1)}, u32[]{:S(2)}, u32[]{:S(2)}) collective-permute-start(bf16[128,1024]{1,0:T(8,128)(2,1)S(1)} %get-tuple-element.64.refs_5_), channel_id=1, source_target_pairs={{0,1},{1,0},{2,3},{3,2},{4,5},{5,4},{6,7},{7,6},{8,9},{9,8},{10,11... | collective-permute-start | bytes 786440 | tf_op jit(solution)/shard_map/ppermute | solution.py:542
  75.3 13.7 %collective-permute-start.13 = (bf16[32,1024]{1,0:T(8,128)(2,1)S(1)}, bf16[32,1024]{1,0:T(8,128)(2,1)S(1)}, u32[]{:S(2)}, u32[]{:S(2)}) collective-permute-start(bf16[32,1024]{1,0:T(8,128)(2,1)S(1)} %get-tuple-element.61), channel_id=1, source_target_pairs={{0,4},{2,6},{4,0},{6,2},{8,12},{10,14},{12,8},{14,10},{1,5},{3,7},... | collective-permute-start | bytes 196616 | tf_op jit(solution)/shard_map/ppermute | solution.py:545
  77.0 12.0 %collective-permute-start.14 = (bf16[32,1024]{1,0:T(8,128)(2,1)S(1)}, bf16[32,1024]{1,0:T(8,128)(2,1)S(1)}, u32[]{:S(2)}, u32[]{:S(2)}) collective-permute-start(bf16[32,1024]{1,0:T(8,128)(2,1)S(1)} %get-tuple-element.62), channel_id=1, source_target_pairs={{0,8},{2,10},{4,12},{6,14},{8,0},{10,2},{12,4},{14,6},{1,9},{3,11}... | collective-permute-start | bytes 196616 | tf_op jit(solution)/shard_map/ppermute | solution.py:545
  78.7 10.3 %collective-permute-start.15 = (bf16[32,1024]{1,0:T(8,128)(2,1)S(1)}, bf16[32,1024]{1,0:T(8,128)(2,1)S(1)}, u32[]{:S(2)}, u32[]{:S(2)}) collective-permute-start(bf16[32,1024]{1,0:T(8,128)(2,1)S(1)} %get-tuple-element.63), channel_id=1, source_target_pairs={{0,12},{2,14},{4,8},{6,10},{8,4},{10,6},{12,0},{14,2},{1,13},{3,15... | collective-permute-start | bytes 196616 | tf_op jit(solution)/shard_map/ppermute | solution.py:545
  89.5 11.5 %collective-permute-start.20 = (bf16[32,1024]{1,0:T(8,128)(2,1)S(1)}, bf16[32,1024]{1,0:T(8,128)(2,1)S(1)}, u32[]{:S(2)}, u32[]{:S(2)}) collective-permute-start(bf16[32,1024]{1,0:T(8,128)(2,1)S(1)} %add_pieces.3.refs_7_.refs_1_), channel_id=1, source_target_pairs={{0,12},{2,14},{4,8},{6,10},{8,4},{10,6},{12,0},{14,2},{1,13},{3,15... | collective-permute-start | bytes 196616 | tf_op jit(solution)/shard_map/ppermute | solution.py:545
  92.4 8.7 %collective-permute-start.19 = (bf16[32,1024]{1,0:T(8,128)(2,1)S(1)}, bf16[32,1024]{1,0:T(8,128)(2,1)S(1)}, u32[]{:S(2)}, u32[]{:S(2)}) collective-permute-start(bf16[32,1024]{1,0:T(8,128)(2,1)S(1)} %add_pieces.3.refs_7_.refs_1_), channel_id=1, source_target_pairs={{0,8},{2,10},{4,12},{6,14},{8,0},{10,2},{12,4},{14,6},{1,9},{3,11}... | collective-permute-start | bytes 196616 | tf_op jit(solution)/shard_map/ppermute | solution.py:545
  92.4 8.7 %collective-permute-start.18 = (bf16[32,1024]{1,0:T(8,128)(2,1)S(1)}, bf16[32,1024]{1,0:T(8,128)(2,1)S(1)}, u32[]{:S(2)}, u32[]{:S(2)}) collective-permute-start(bf16[32,1024]{1,0:T(8,128)(2,1)S(1)} %add_pieces.3.refs_7_.refs_1_), channel_id=1, source_target_pairs={{0,4},{2,6},{4,0},{6,2},{8,12},{10,14},{12,8},{14,10},{1,5},{3,7},... | collective-permute-start | bytes 196616 | tf_op jit(solution)/shard_map/ppermute | solution.py:545
  101.7 7.9 %collective-permute-start.22 = (bf16[128,1024]{1,0:T(8,128)(2,1)S(1)}, bf16[128,1024]{1,0:T(8,128)(2,1)S(1)}, u32[]{:S(2)}, u32[]{:S(2)}) collective-permute-start(bf16[128,1024]{1,0:T(8,128)(2,1)S(1)} %join_pieces.3.refs_6_.refs_8_.refs_5_), channel_id=1, source_target_pairs={{0,2},{2,0},{4,6},{6,4},{8,10},{10,8},{12,14},{14,12},{1,3},{3,1},... | collective-permute-start | bytes 786440 | tf_op jit(solution)/shard_map/ppermute | solution.py:545
  102.3 15.2 %collective-permute-start.21 = (bf16[128,1024]{1,0:T(8,128)(2,1)S(1)}, bf16[128,1024]{1,0:T(8,128)(2,1)S(1)}, u32[]{:S(2)}, u32[]{:S(2)}) collective-permute-start(bf16[128,1024]{1,0:T(8,128)(2,1)S(1)} %join_pieces.3.refs_6_.refs_8_.refs_5_), channel_id=1, source_target_pairs={{0,1},{1,0},{2,3},{3,2},{4,5},{5,4},{6,7},{7,6},{8,9},{9,8},{10,11... | collective-permute-start | bytes 786440 | tf_op jit(solution)/shard_map/ppermute | solution.py:542
  109.6 7.9 %collective-permute-start.23 = (bf16[128,1024]{1,0:T(8,128)(2,1)S(1)}, bf16[128,1024]{1,0:T(8,128)(2,1)S(1)}, u32[]{:S(2)}, u32[]{:S(2)}) collective-permute-start(bf16[128,1024]{1,0:T(8,128)(2,1)S(1)} %collective-permute-done.22.refs_9_.refs_6_), channel_id=1, source_target_pairs={{0,1},{1,0},{2,3},{3,2},{4,5},{5,4},{6,7},{7,6},{8,9},{9,8},{10,11... | collective-permute-start | bytes 786440 | tf_op jit(solution)/shard_map/ppermute | solution.py:542
  135.0 8.3 %collective-permute-start.25 = (bf16[256,4096]{1,0:T(8,128)(2,1)S(1)}, bf16[256,4096]{1,0:T(8,128)(2,1)S(1)}, u32[]{:S(2)}, u32[]{:S(2)}) collective-permute-start(bf16[256,4096]{1,0:T(8,128)(2,1)S(1)} %get-tuple-element.67.refs_7_), channel_id=1, source_target_pairs={{0,1},{1,0},{2,3},{3,2},{4,5},{5,4},{6,7},{7,6},{8,9},{9,8},{10,11... | collective-permute-start | bytes 6291464 | tf_op jit(solution)/shard_map/ppermute | solution.py:542
  135.1 8.2 %collective-permute-start.24 = (bf16[256,4096]{1,0:T(8,128)(2,1)S(1)}, bf16[256,4096]{1,0:T(8,128)(2,1)S(1)}, u32[]{:S(2)}, u32[]{:S(2)}) collective-permute-start(bf16[256,4096]{1,0:T(8,128)(2,1)S(1)} %get-tuple-element.68), channel_id=1, source_target_pairs={{0,1},{1,0},{2,3},{3,2},{4,5},{5,4},{6,7},{7,6},{8,9},{9,8},{10,11... | collective-permute-start | bytes 6291464 | tf_op jit(solution)/shard_map/ppermute | solution.py:542
